TPU v7x, 512 devices: a whole 4x8x8 slice. The times are simulated.
512 devices in a mesh: dp: 32 (over y, z_lo), tensor: 16 (over x, z_hi, core).
Axes of the slice: x: 4, y: 8, z: 8 (z_hi: 2, z_lo: 4; z = z_hi * 4 + z_lo), core: 2. Of those that a mesh axis runs over, the one named last changes fastest.
Arguments:
- tokens: bfloat16 [4096, 16384], P('dp', 'tensor'), may hold values from -6 to 6
- query_key_value_weight: bfloat16 [16384, 12288], P('tensor', 'dp'), may hold values from -0.046875 to 0.046875
- adapter_down_weight: bfloat16 [32, 16, 16384], P(None, None, 'tensor'), may hold values from -0.046875 to 0.046875
- adapter_up_weight: bfloat16 [32, 16, 12288], P(None, None, 'dp'), may hold values from -1.5 to 1.5
- adapter_per_block: int32 [32], replicated, may hold values from 0 to 31
Outputs:
- projected: bfloat16 [4096, 12288], P('tensor', 'dp')
All inputs are finite; a program needn't handle non-finite values.
Results may differ from a plain program's by a relative error of at most 0.02.
Values may be sent and summed in bfloat16 or wider, within the bound.
No kernel may reach another device: no remote copies, remote signals or barrier semaphores. Data moves between devices by JAX's collectives and lax.ppermute only.
A program may use at most 64 MiB of HBM per device.

v0:
```python
import jax
import jax.numpy as jnp
from jax import lax
from jax.sharding import PartitionSpec as P

BLOCK = 128


def local(
    tokens, query_key_value_weight, adapter_down_weight, adapter_up_weight, adapter_per_block
):
    gathered = lax.all_gather(tokens, "dp", axis=0, tiled=True)
    total_rows = gathered.shape[0]
    features = gathered.shape[1]
    block_len = BLOCK
    blocks = total_rows // block_len
    partial_value = jnp.dot(gathered, query_key_value_weight, preferred_element_type=jnp.float32)
    down_weights = adapter_down_weight[adapter_per_block]
    tok_blocks = gathered.reshape(blocks, block_len, features)
    shrink_part = jnp.einsum(
        "btd,brd->btr", tok_blocks, down_weights, preferred_element_type=jnp.float32
    )
    shrink_part = shrink_part.reshape(total_rows, shrink_part.shape[2])
    width = lax.axis_size("tensor")
    my_rows = total_rows // width
    position = lax.axis_index("tensor")
    shrink_all = lax.psum(shrink_part.astype(jnp.bfloat16), "tensor").astype(jnp.float32)
    base = lax.psum_scatter(
        partial_value.astype(jnp.bfloat16), "tensor", scatter_dimension=0, tiled=True
    ).astype(jnp.float32)
    shrink_mine = lax.dynamic_slice_in_dim(shrink_all, position * my_rows, my_rows, 0)
    my_blocks = my_rows // block_len
    local_adapter_index = lax.dynamic_slice_in_dim(
        adapter_per_block, position * my_blocks, my_blocks, 0
    )
    up_weights = adapter_up_weight[local_adapter_index]
    shrink_low = shrink_mine.astype(jnp.bfloat16).reshape(
        my_blocks, block_len, shrink_mine.shape[1]
    )
    expand = jnp.einsum("btr,brf->btf", shrink_low, up_weights, preferred_element_type=jnp.float32)
    expand = expand.reshape(my_rows, up_weights.shape[2])
    return (base + 0.5 * expand).astype(jnp.bfloat16)


def solution(mesh):
    return jax.shard_map(
        local,
        mesh=mesh,
        in_specs=(
            P("dp", "tensor"),
            P("tensor", "dp"),
            P(None, None, "tensor"),
            P(None, None, "dp"),
            P(),
        ),
        out_specs=P("tensor", "dp"),
        check_vma=False,
    )
```

profile of v0, /device:TPU:1, one launch (start us, length us, event | category | flops | bytes accessed | tf_op | source)
XLA Modules:
  0.0 513.1 jit_solution(1341105289887228927)
XLA Ops:
  6.5 0.0 copy-start
  6.5 0.0 copy-start.1
  6.5 0.0 all-gather.2.cloned.1.call-start
  6.5 0.7 all-gather.2.cloned.1.call-update
  7.3 0.0 all-reduce.2.cloned.1.call-start
  7.3 0.7 compare_select_fusion.1
  8.0 0.0 copy-done
  8.0 0.6 gather_fusion
  8.6 198.6 %all-gather.2.cloned.1.call-done = bf16[4096,1024]{1,0:T(8,128)(2,1)} async-done(((bf16[128,1024]{1,0:T(8,128)(2,1)}), bf16[4096,1024]{1,0:T(8,128)(2,1)}) %all-gather.2.cloned.1.call-update) | async-done | bytes 8388624 | tf_op jit(solution)/shard_map/all_gather | solution.py:12
  207.2 5.7 %fusion = bf16[32,2,8,128]{3,2,1,0:T(8,128)(2,1)S(1)} fusion(bf16[32,16,1024]{2,1,0:T(8,128)(2,1)S(1)} %gather_fusion, bf16[32,128,1024]{2,1,0:T(8,128)(2,1)} %bitcast.23), kind=kOutput, calls=%fused_computation.5 | convolution fusion | flops 134283264 | bytes 9568256 | tf_op jit(solution)/shard_map/btd,brd->btr/dot_general | solution.py:20
  212.9 0.7 copy.15
  213.6 0.0 all-reduce.2.cloned.1.call-update
  213.6 0.0 copy-start.2
  213.6 0.0 reduce-scatter.2.cloned.1.call-start
  213.7 0.0 copy-done.1
  213.7 9.2 %convolution_convert_fusion = bf16[4096,384]{1,0:T(8,128)(2,1)} fusion(bf16[4096,1024]{1,0:T(8,128)(2,1)} %all-gather.2.cloned.1.call-done, bf16[1024,384]{1,0:T(8,128)(2,1)S(1)} %copy-done.1), kind=kOutput, calls=%fused_computation.2 | convolution fusion | flops 3222798336 | bytes 12320768 | tf_op jit(solution)/shard_map/dot_general | solution.py:17
  222.9 0.0 reduce-scatter.2.cloned.1.call-update
  222.9 0.0 copy-done.2
  222.9 0.1 compare_select_fusion
  223.0 1.6 gather_fusion.1
  224.6 170.9 %all-reduce.2.cloned.1.call-done = bf16[4096,16]{0,1:T(8,128)(2,1)} async-done(((bf16[4096,16]{0,1:T(8,128)(2,1)}), bf16[4096,16]{0,1:T(8,128)(2,1)}) %all-reduce.2.cloned.1.call-update) | async-done | bytes 131088 | tf_op jit(solution)/shard_map/psum | solution.py:27
  395.5 0.9 convolution_multiply_fusion
  396.4 108.5 %reduce-scatter.2.cloned.1.call-done = bf16[256,384]{1,0:T(8,128)(2,1)} async-done(((bf16[4096,384]{1,0:T(8,128)(2,1)}), bf16[256,384]{1,0:T(8,128)(2,1)}) %reduce-scatter.2.cloned.1.call-update) | async-done | bytes 196624 | tf_op jit(solution)/shard_map/reduce_scatter | solution.py:28
  504.9 1.7 fusion.1
  (2 shorter events, 0.0 us)
Async XLA Ops:
  6.5 1.4 copy-start
  6.5 207.1 %copy-start.1 = (bf16[1024,384]{1,0:T(8,128)(2,1)S(1)}, bf16[1024,384]{1,0:T(8,128)(2,1)}, u32[]{:S(2)}) copy-start(bf16[1024,384]{1,0:T(8,128)(2,1)} %param.6) | copy-start | bytes 2359300
  6.5 200.7 %all-gather.2.cloned.1.call-start = ((), (), s32[]{:S(2)}) async-start(), calls=%async_computation.1 | async-start | bytes 8650752 | tf_op jit(solution)/shard_map/all_gather | solution.py:12
  7.3 388.2 %all-reduce.2.cloned.1.call-start = ((), (), s32[]{:S(2)}) async-start(), calls=%async_computation.3 | async-start | bytes 262144 | tf_op jit(solution)/shard_map/psum | solution.py:27
  213.6 9.3 %copy-start.2 = (s32[32]{0:T(128)S(1)}, s32[32]{0:T(128)}, u32[]{:S(2)}) copy-start(s32[32]{0:T(128)} %param.9) | copy-start | bytes 388
  213.6 291.3 %reduce-scatter.2.cloned.1.call-start = ((), (), s32[]{:S(2)}) async-start(), calls=%async_computation.2 | async-start | bytes 3342336 | tf_op jit(solution)/shard_map/reduce_scatter | solution.py:28
Sparse Core Ops, SparseCore 0:
  9.4 197.7 all-gather.1
  213.7 181.6 all-reduce.1
  401.1 103.7 reduce-scatter.1
where the time goes:
time: 514 us; the launch traced here: 513 us
  waiting for transfers between devices  479 us (93%)
  matrix products  15.8 us (3%)
  between operations  13.2 us (3%)
    all_gather x1, waiting for transfers between devices, local(): gathered = lax.all_gather(tokens, 'dp', axis=0, tiled=True)  199 us
    psum x1, waiting for transfers between devices, local(): lax.psum(shrink_part.astype(jnp.bfloat16), 'tensor').astype(jnp.float32)  171 us
    reduce_scatter x1, waiting for transfers between devices, local(): lax.psum_scatter(partial_value.astype(jnp.bfloat16), 'tensor', scatter_di...  109 us
  transfers between devices with their start and end apart: 3, of which 3 were waited for; matrix products, arithmetic and copies ran while one was open for 3% of the time, Pallas kernels for 0%

commit v1 on v0

v1 whole, which is shorter than its diff:
```python
import jax
import jax.numpy as jnp
from jax import lax
from jax.experimental import pallas as pl
from jax.experimental.pallas import tpu as pltpu
from jax.sharding import Mesh, PartitionSpec as P

BLOCK = 128
Y, ZP, ZQ, X, ZH, C = 8, 2, 2, 4, 2, 2
AXES = ("y", "p", "q", "x", "zh", "c")
DP, TENSOR = ("y", "p", "q"), ("x", "zh", "c")


def ring(axis, size, step):
    return [(i, (i + step) % size) for i in range(size)]


def project(order, tokens, down, keep_w, send_w, keep, send):
    rows, features = tokens.shape
    rank = down.shape[0] // 2
    tile = pl.program_id(0)
    tok = tokens[...]
    shrink = lax.dot_general(
        tok, down[...], (((1,), (1,)), ((), ())), preferred_element_type=jnp.float32
    )
    row = lax.broadcasted_iota(jnp.int32, shrink.shape, 0) // BLOCK
    col = lax.broadcasted_iota(jnp.int32, shrink.shape, 1) // rank
    low = jnp.where(row == col, 0.5 * shrink, 0.0).astype(jnp.bfloat16)
    ups = pl.ds(pl.multiple_of(features + tile * 2 * rank, 2 * rank), 2 * rank)
    for w, out in ((keep_w, keep), (send_w, send)):
        total = jnp.dot(tok, w[:features, :], preferred_element_type=jnp.float32)
        total += jnp.dot(low, w[ups, :], preferred_element_type=jnp.float32)
        out[...] = total.astype(out.dtype)


def partials(x, gathered, down, keep_w, send_w):
    tiles, rows, features = gathered.shape
    columns = keep_w.shape[1]

    def place(t, order):
        return ((t // 2 - order[0] + X) % X * 2 + t % 2, 0, 0)

    whole = pl.BlockSpec(keep_w.shape, lambda t, order: (0, 0))
    out = jax.ShapeDtypeStruct((tiles, rows, columns), jnp.bfloat16)
    return pl.pallas_call(
        project,
        out_shape=(out, out),
        grid_spec=pltpu.PrefetchScalarGridSpec(
            num_scalar_prefetch=1,
            grid=(tiles,),
            in_specs=[
                pl.BlockSpec((None, rows, features), lambda t, order: (t, 0, 0)),
                pl.BlockSpec((None,) + down.shape[1:], lambda t, order: (t, 0, 0)),
                whole,
                whole,
            ],
            out_specs=[pl.BlockSpec((None, rows, columns), place)] * 2,
        ),
        compiler_params=pltpu.CompilerParams(vmem_limit_bytes=32 * 1024 * 1024),
        cost_estimate=pl.CostEstimate(
            flops=4 * tiles * rows * features * columns,
            bytes_accessed=2 * (gathered.size + 2 * tiles * rows * columns),
            transcendentals=0,
        ),
    )(x.reshape(1), gathered, down, keep_w, send_w)


def local(
    tokens, query_key_value_weight, adapter_down_weight, adapter_up_weight, adapter_per_block
):
    p, q, x, zh, c = (lax.axis_index(a) for a in AXES[1:])
    own_rows, features = tokens.shape
    columns = query_key_value_weight.shape[1]
    rank = adapter_down_weight.shape[1]

    other = lax.ppermute(tokens, "q", ring("q", ZQ, 1))
    gathered = lax.all_gather(jnp.concatenate([tokens, other], 0), "y", axis=0, tiled=False)

    per = adapter_per_block.reshape(Y, ZP, ZQ)
    per = jnp.where(q == 0, per, per[:, :, ::-1])
    mine = jnp.where(p == 0, per[:, 0], per[:, 1])
    theirs = jnp.where(p == 0, per[:, 1], per[:, 0])
    down = adapter_down_weight[mine.reshape(-1)].reshape(Y, ZQ * rank, features)
    up_mine = adapter_up_weight[mine.reshape(-1)].reshape(-1, columns)
    up_theirs = adapter_up_weight[theirs.reshape(-1)].reshape(-1, columns)

    own_w = jnp.concatenate([query_key_value_weight, up_mine], 0)
    their_w = lax.ppermute(
        jnp.concatenate([query_key_value_weight, up_theirs], 0), "p", ring("p", ZP, 1)
    )
    keep_w = jnp.where(c == p, own_w, their_w)
    send_w = jnp.where(c == p, their_w, own_w)

    keep, send = partials(x, gathered, down, keep_w, send_w)
    received = lax.ppermute(send, "c", ring("c", C, 1))

    def added(d):
        a, b = keep[2 * d : 2 * d + 2], received[2 * d : 2 * d + 2]
        return a.astype(jnp.float32) + b.astype(jnp.float32)

    total = added(0)
    for d in (2, 1, 3):
        total += lax.ppermute(added(d).astype(jnp.bfloat16), "x", ring("x", X, d)).astype(
            jnp.float32
        )
    total = total.astype(jnp.bfloat16)

    here = jnp.where(zh == 0, total[0], total[1])
    there = jnp.where(zh == 0, total[1], total[0])
    swap = [(i * 4 + h * 2 + j, j * 4 + h * 2 + i) for i in range(ZP) for h in range(ZH) for j in range(C)]
    cross = [(i * 4 + h * 2 + j, j * 4 + (1 - h) * 2 + i) for i in range(ZP) for h in range(ZH) for j in range(C)]
    far = lax.ppermute(there, ("p", "zh", "c"), cross)
    near = lax.ppermute(here, ("p", "zh", "c"), swap)
    out = near.astype(jnp.float32) + far.astype(jnp.float32)
    out = out.reshape(ZQ, own_rows, columns)
    out = jnp.where(q == 0, out, out[::-1])
    return out.reshape(ZQ * own_rows, columns).astype(jnp.bfloat16)


def solution(mesh):
    physical = Mesh(mesh.devices.reshape(Y, ZP, ZQ, X, ZH, C), AXES)
    return jax.shard_map(
        local,
        mesh=physical,
        in_specs=(
            P(DP, TENSOR),
            P(TENSOR, DP),
            P(None, None, TENSOR),
            P(None, None, DP),
            P(),
        ),
        out_specs=P(TENSOR, DP),
        check_vma=False,
    )
```

time: 514 us -> 155 us (0.30)
  waiting for transfers between devices: 479 us -> 76 us
  starting transfers between devices: 0.08 us -> 35.7 us
  matrix products: 15.8 us -> 0 us
  Pallas kernels: 0 us -> 10 us
  other arithmetic: 2.41 us -> 10.5 us
  local copies, waits for them, and re-layouts: 2.86 us -> 8.37 us
    all_gather x1, waiting for transfers between devices: 199 us -> 6.78 us  [local(): lax.all_gather(jnp.concatenate([tokens, other], 0), 'y', axis=0, tiled=Fa...]
    psum x1 -> x0, waiting for transfers between devices: 171 us -> none  [local(): lax.psum(shrink_part.astype(jnp.bfloat16), 'tensor').astype(jnp.float32)]
    reduce_scatter x1 -> x0, waiting for transfers between devices: 109 us -> none  [local(): lax.psum_scatter(partial_value.astype(jnp.bfloat16), 'tensor', scatter_di...]
    ppermute x0 -> x8, waiting for transfers between devices: none -> 69.2 us  [the longest x1 41.3 us: local(): lax.ppermute(jnp.concatenate([query_key_value_weight, up_theirs], 0), 'p'...]
    ppermute x0 -> x8, starting transfers between devices: none -> 35.7 us  [the longest x3 9.88 us: local(): lax.ppermute(added(d).astype(jnp.bfloat16), 'x', ring('x', X, d))]
    dot_general x3 -> x0, matrix products: 15.8 us -> none  [the longest x1 9.22 us: local(): jnp.dot(gathered, query_key_value_weight, preferred_element_type=jnp.floa...]
    pallas_call x0 -> x1, Pallas kernels: none -> 10 us  [partials(): pl.pallas_call(project, out_shape=(out, out), grid_spec=pltpu.PrefetchSca...]
  transfers between devices with their start and end apart: 3 -> 9, of which waited for: 3 -> 9; matrix products, arithmetic and copies ran while one was open for 3% -> 5% of each run, Pallas kernels for 0% -> 0%
where the time goes in v1:
time: 155 us; the launch traced here: 154 us
  waiting for transfers between devices  76 us (49%)
  starting transfers between devices  35.7 us (23%)
  between operations  13.6 us (9%)
  other arithmetic  10.5 us (7%)
  Pallas kernels  10 us (6%)
  local copies, waits for them, and re-layouts  8.37 us (5%)
    ppermute x1, waiting for transfers between devices, local(): lax.ppermute(jnp.concatenate([query_key_value_weight, up_theirs], 0), 'p'...  41.3 us
    ppermute x3, waiting for transfers between devices, local(): lax.ppermute(added(d).astype(jnp.bfloat16), 'x', ring('x', X, d))  13 us
    pallas_call x1, Pallas kernels, partials(): pl.pallas_call(project, out_shape=(out, out), grid_spec=pltpu.PrefetchSca...  10 us
    ppermute x3, starting transfers between devices, local(): lax.ppermute(added(d).astype(jnp.bfloat16), 'x', ring('x', X, d))  9.88 us
    ppermute x1, starting transfers between devices, local(): lax.ppermute(jnp.concatenate([query_key_value_weight, up_theirs], 0), 'p'...  8.07 us
    all_gather x1, waiting for transfers between devices, local(): lax.all_gather(jnp.concatenate([tokens, other], 0), 'y', axis=0, tiled=Fa...  6.78 us
    ppermute x1, starting transfers between devices, local(): far = lax.ppermute(there, ('p', 'zh', 'c'), cross)  5.16 us
    ppermute x1, starting transfers between devices, local(): near = lax.ppermute(here, ('p', 'zh', 'c'), swap)  5.04 us
  transfers between devices with their start and end apart: 9, of which 9 were waited for; matrix products, arithmetic and copies ran while one was open for 5% of the time, Pallas kernels for 0%

profile of v1, /device:TPU:1, one launch (start us, length us, event | category | flops | bytes accessed | tf_op | source)
XLA Modules:
  0.0 154.2 jit_solution(4493701839138523135)
XLA Ops:
  6.5 5.0 %collective-permute-start = (bf16[128,1024]{1,0:T(8,128)(2,1)}, bf16[128,1024]{1,0:T(8,128)(2,1)S(1)}, u32[]{:S(2)}, u32[]{:S(2)}) collective-permute-start(bf16[128,1024]{1,0:T(8,128)(2,1)} %param.5), channel_id=1, source_target_pairs={{0,16},{16,0},{1,17},{17,1},{2,18},{18,2},{3,19},{19,3},{4,20},{20... | collective-permute-start | bytes 786440 | tf_op jit(solution)/shard_map/ppermute | solution.py:76
  11.5 4.0 %collective-permute-done = bf16[128,1024]{1,0:T(8,128)(2,1)S(1)} collective-permute-done((bf16[128,1024]{1,0:T(8,128)(2,1)}, bf16[128,1024]{1,0:T(8,128)(2,1)S(1)}, u32[]{:S(2)}, u32[]{:S(2)}) %collective-permute-start) | collective-permute-done | bytes 262176 | tf_op jit(solution)/shard_map/ppermute | solution.py:76
  15.5 1.8 %pad_maximum_fusion.2 = bf16[256,1024]{1,0:T(8,128)(2,1)} fusion(bf16[128,1024]{1,0:T(8,128)(2,1)S(1)} %collective-permute-done, bf16[128,1024]{1,0:T(8,128)(2,1)} %param.5), kind=kLoop, calls=%fused_computation.12 | loop fusion | flops 1048576 | bytes 1048576 | tf_op jit(solution)/shard_map/concatenate | solution.py:77
  17.3 0.7 reshape.88
  18.0 0.1 rev.6
  18.3 1.6 %gather_fusion.2 = bf16[16,16,384]{2,1,0:T(8,128)(2,1)S(1)} fusion(bf16[32,16,384]{2,1,0:T(8,128)(2,1)} %param.8, s32[1024]{0:T(1024)S(1)} %pad_clamp_fusion), kind=kCustom, calls=%fused_computation.2 | custom fusion | bytes 393280 | tf_op jit(solution)/shard_map/gather | solution.py:85
  19.9 1.1 pad_maximum_fusion.1
  21.0 8.1 %collective-permute-start.1 = (bf16[1280,384]{1,0:T(8,128)(2,1)}, bf16[1280,384]{1,0:T(8,128)(2,1)}, u32[]{:S(2)}, u32[]{:S(2)}) collective-permute-start(bf16[1280,384]{1,0:T(8,128)(2,1)} %pad_maximum_fusion.1), channel_id=1, source_target_pairs={{0,32},{32,0},{1,33},{33,1},{2,34},{34,2},{3,35},{35,3},{4,36},{36... | collective-permute-start | bytes 2949128 | tf_op jit(solution)/shard_map/ppermute | solution.py:88
  29.1 0.6 gather_fusion.1
  29.8 0.6 gather_fusion
  30.3 41.3 %collective-permute-done.1 = bf16[1280,384]{1,0:T(8,128)(2,1)} collective-permute-done((bf16[1280,384]{1,0:T(8,128)(2,1)}, bf16[1280,384]{1,0:T(8,128)(2,1)}, u32[]{:S(2)}, u32[]{:S(2)}) %collective-permute-start.1) | collective-permute-done | bytes 983072 | tf_op jit(solution)/shard_map/ppermute | solution.py:88
  71.7 2.9 %broadcast_select_fusion = (bf16[1280,384]{1,0:T(8,128)(2,1)}, bf16[1280,384]{1,0:T(8,128)(2,1)}) fusion(bf16[1280,384]{1,0:T(8,128)(2,1)} %collective-permute-done.1, pred[]{:T(512)S(6)} %eq.19, bf16[256,384]{1,0:T(8,128)(2,1)S(1)} %bitcast.20, bf16[1024,384]{1,0:T(8,128)(2,1)S(1)} %copy-done.4), kind=kLoop, calls=%fused_computation.5 | loop fusion | flops 2949120 | bytes 3932161 | tf_op jit(solution)/shard_map/jit(_where)/select_n | solution.py:92
  74.6 6.8 %all-gather.3.cloned.1.call-done = bf16[2048,1024]{1,0:T(8,128)(2,1)} async-done(((bf16[256,1024]{1,0:T(8,128)(2,1)}), bf16[2048,1024]{1,0:T(8,128)(2,1)}) %all-gather.3.cloned.1.call-update) | async-done | bytes 4194320 | tf_op jit(solution)/shard_map/all_gather | solution.py:77
  81.4 1.2 copy-done.1
  82.6 1.2 copy-done.2
  83.8 2.2 %copy-done.3 = bf16[2048,1024]{1,0:T(8,128)(2,1)S(1)} copy-done((bf16[2048,1024]{1,0:T(8,128)(2,1)S(1)}, bf16[2048,1024]{1,0:T(8,128)(2,1)}, u32[]{:S(2)}) %copy-start.3) | copy-done | bytes 4194328
  86.0 10.0 %shard_map.55 = (bf16[8,256,384]{2,1,0:T(8,128)(2,1)S(1)}, bf16[8,256,384]{2,1,0:T(8,128)(2,1)S(1)}) custom-call(s32[1]{0:T(128)} %bitcast.order, bf16[8,256,1024]{2,1,0:T(8,128)(2,1)S(1)} %bitcast.19, bf16[8,32,1024]{2,1,0:T(8,128)(2,1)S(1)} %bitcast.18, bf16[1280,384]{1,0:T(8,128)(2,1)S(1)} %copy-done.2, bf16[1280,384]{1,0:T(8,128)(2,1)S(1)} %copy-done.1), custom_call_target="tpu_custom_call" | custom-call | flops 3221225472 | bytes 7340032 | tf_op jit(solution)/shard_map/pallas_call | solution.py:45
  96.0 2.6 %collective-permute-start.2 = (bf16[8,256,384]{2,1,0:T(8,128)(2,1)S(1)}, bf16[8,256,384]{2,1,0:T(8,128)(2,1)}, u32[]{:S(2)}, u32[]{:S(2)}) collective-permute-start(bf16[8,256,384]{2,1,0:T(8,128)(2,1)S(1)} %get-tuple-element.8), channel_id=1, source_target_pairs={{0,1},{1,0},{2,3},{3,2},{4,5},{5,4},{6,7},{7,6},{8,9},{9,8},{10,11... | collective-permute-start | bytes 4718600 | tf_op jit(solution)/shard_map/ppermute | solution.py:95
  98.6 3.1 %collective-permute-done.2 = bf16[8,256,384]{2,1,0:T(8,128)(2,1)} collective-permute-done((bf16[8,256,384]{2,1,0:T(8,128)(2,1)S(1)}, bf16[8,256,384]{2,1,0:T(8,128)(2,1)}, u32[]{:S(2)}, u32[]{:S(2)}) %collective-permute-start.2) | collective-permute-done | bytes 1572896 | tf_op jit(solution)/shard_map/ppermute | solution.py:95
  101.7 2.4 %add_convert_fusion.3 = (bf16[2,256,384]{2,1,0:T(8,128)(2,1)}, bf16[2,256,384]{2,1,0:T(8,128)(2,1)}, bf16[2,256,384]{2,1,0:T(8,128)(2,1)S(1)}) fusion(bf16[8,256,384]{2,1,0:T(8,128)(2,1)} %collective-permute-done.2, bf16[8,256,384]{2,1,0:T(8,128)(2,1)S(1)} %get-tuple-element.7), kind=kLoop, calls=%fused_computation.10 | loop fusion | flops 2359296 | bytes 3538944 | tf_op jit(solution)/shard_map/convert_element_type | solution.py:103
  104.2 4.6 %collective-permute-start.3 = (bf16[2,256,384]{2,1,0:T(8,128)(2,1)}, bf16[2,256,384]{2,1,0:T(8,128)(2,1)S(1)}, u32[]{:S(2)}, u32[]{:S(2)}) collective-permute-start(bf16[2,256,384]{2,1,0:T(8,128)(2,1)} %get-tuple-element.11), channel_id=1, source_target_pairs={{0,8},{4,12},{8,0},{12,4},{1,9},{5,13},{9,1},{13,5},{2,10},{6,14},... | collective-permute-start | bytes 1179656 | tf_op jit(solution)/shard_map/ppermute | solution.py:103
  108.8 2.8 %collective-permute-start.5 = (bf16[2,256,384]{2,1,0:T(8,128)(2,1)}, bf16[2,256,384]{2,1,0:T(8,128)(2,1)}, u32[]{:S(2)}, u32[]{:S(2)}) collective-permute-start(bf16[2,256,384]{2,1,0:T(8,128)(2,1)} %get-tuple-element.12), channel_id=1, source_target_pairs={{0,12},{4,0},{8,4},{12,8},{1,13},{5,1},{9,5},{13,9},{2,14},{6,2},{... | collective-permute-start | bytes 1179656 | tf_op jit(solution)/shard_map/ppermute | solution.py:103
  111.6 2.5 %collective-permute-start.4 = (bf16[2,256,384]{2,1,0:T(8,128)(2,1)S(1)}, bf16[2,256,384]{2,1,0:T(8,128)(2,1)}, u32[]{:S(2)}, u32[]{:S(2)}) collective-permute-start(bf16[2,256,384]{2,1,0:T(8,128)(2,1)S(1)} %get-tuple-element.13), channel_id=1, source_target_pairs={{0,4},{4,8},{8,12},{12,0},{1,5},{5,9},{9,13},{13,1},{2,6},{6,10},{... | collective-permute-start | bytes 1179656 | tf_op jit(solution)/shard_map/ppermute | solution.py:103
  114.1 4.0 %collective-permute-done.3 = bf16[2,256,384]{2,1,0:T(8,128)(2,1)S(1)} collective-permute-done((bf16[2,256,384]{2,1,0:T(8,128)(2,1)}, bf16[2,256,384]{2,1,0:T(8,128)(2,1)S(1)}, u32[]{:S(2)}, u32[]{:S(2)}) %collective-permute-start.3) | collective-permute-done | bytes 393248 | tf_op jit(solution)/shard_map/ppermute | solution.py:103
  118.1 8.6 %collective-permute-done.5 = bf16[2,256,384]{2,1,0:T(8,128)(2,1)} collective-permute-done((bf16[2,256,384]{2,1,0:T(8,128)(2,1)}, bf16[2,256,384]{2,1,0:T(8,128)(2,1)}, u32[]{:S(2)}, u32[]{:S(2)}) %collective-permute-start.5) | collective-permute-done | bytes 393248 | tf_op jit(solution)/shard_map/ppermute | solution.py:103
  126.7 0.4 collective-permute-done.4
  127.1 1.5 add_convert_fusion
  128.6 5.0 %collective-permute-start.6 = (bf16[256,384]{1,0:T(8,128)(2,1)S(1)}, bf16[256,384]{1,0:T(8,128)(2,1)S(1)}, u32[]{:S(2)}, u32[]{:S(2)}) collective-permute-start(bf16[256,384]{1,0:T(8,128)(2,1)S(1)} %get-tuple-element.16), channel_id=1, source_target_pairs={{0,0},{1,32},{2,2},{3,34},{32,1},{33,33},{34,3},{35,35},{4,4},{5,3... | collective-permute-start | bytes 589832 | tf_op jit(solution)/shard_map/ppermute | solution.py:113
  133.7 5.2 %collective-permute-start.7 = (bf16[256,384]{1,0:T(8,128)(2,1)S(1)}, bf16[256,384]{1,0:T(8,128)(2,1)S(1)}, u32[]{:S(2)}, u32[]{:S(2)}) collective-permute-start(bf16[256,384]{1,0:T(8,128)(2,1)S(1)} %get-tuple-element.17), channel_id=1, source_target_pairs={{0,2},{1,34},{2,0},{3,32},{32,3},{33,35},{34,1},{35,33},{4,6},{5,3... | collective-permute-start | bytes 589832 | tf_op jit(solution)/shard_map/ppermute | solution.py:112
  138.8 3.7 %collective-permute-done.6 = bf16[256,384]{1,0:T(8,128)(2,1)S(1)} collective-permute-done((bf16[256,384]{1,0:T(8,128)(2,1)S(1)}, bf16[256,384]{1,0:T(8,128)(2,1)S(1)}, u32[]{:S(2)}, u32[]{:S(2)}) %collective-permute-start.6) | collective-permute-done | bytes 196640 | tf_op jit(solution)/shard_map/ppermute | solution.py:113
  142.6 4.0 %collective-permute-done.7 = bf16[256,384]{1,0:T(8,128)(2,1)S(1)} collective-permute-done((bf16[256,384]{1,0:T(8,128)(2,1)S(1)}, bf16[256,384]{1,0:T(8,128)(2,1)S(1)}, u32[]{:S(2)}, u32[]{:S(2)}) %collective-permute-start.7) | collective-permute-done | bytes 196640 | tf_op jit(solution)/shard_map/ppermute | solution.py:112
  146.7 0.7 fusion
  (21 shorter events, 0.4 us)
Async XLA Ops:
  6.5 23.2 %copy-start = (bf16[32,16,1024]{2,1,0:T(8,128)(2,1)S(1)}, bf16[32,16,1024]{2,1,0:T(8,128)(2,1)}, u32[]{:S(2)}) copy-start(bf16[32,16,1024]{2,1,0:T(8,128)(2,1)} %param.7) | copy-start | bytes 3145732
  6.5 22.6 %copy-start.5 = (bf16[32,16,384]{2,1,0:T(8,128)(2,1)S(1)}, bf16[32,16,384]{2,1,0:T(8,128)(2,1)}, u32[]{:S(2)}) copy-start(bf16[32,16,384]{2,1,0:T(8,128)(2,1)} %param.8) | copy-start | bytes 1179652
  6.5 13.3 %copy-start.4 = (bf16[1024,384]{1,0:T(8,128)(2,1)S(1)}, bf16[1024,384]{1,0:T(8,128)(2,1)}, u32[]{:S(2)}) copy-start(bf16[1024,384]{1,0:T(8,128)(2,1)} %param.6) | copy-start | bytes 2359300
  6.5 74.9 %all-gather.3.cloned.1.call-start = ((), (), s32[]{:S(2)}) async-start(), calls=%async_computation | async-start | bytes 4718592 | tf_op jit(solution)/shard_map/all_gather | solution.py:77
  6.5 8.9 %collective-permute-start = (bf16[128,1024]{1,0:T(8,128)(2,1)}, bf16[128,1024]{1,0:T(8,128)(2,1)S(1)}, u32[]{:S(2)}, u32[]{:S(2)}) collective-permute-start(bf16[128,1024]{1,0:T(8,128)(2,1)} %param.5), channel_id=1, source_target_pairs={{0,16},{16,0},{1,17},{17,1},{2,18},{18,2},{3,19},{19,3},{4,20},{20... | collective-permute-start | bytes 786440 | tf_op jit(solution)/shard_map/ppermute | solution.py:76
  21.0 50.7 %collective-permute-start.1 = (bf16[1280,384]{1,0:T(8,128)(2,1)}, bf16[1280,384]{1,0:T(8,128)(2,1)}, u32[]{:S(2)}, u32[]{:S(2)}) collective-permute-start(bf16[1280,384]{1,0:T(8,128)(2,1)} %pad_maximum_fusion.1), channel_id=1, source_target_pairs={{0,32},{32,0},{1,33},{33,1},{2,34},{34,2},{3,35},{35,3},{4,36},{36... | collective-permute-start | bytes 2949128 | tf_op jit(solution)/shard_map/ppermute | solution.py:88
  81.4 1.2 copy-start.1
  82.6 1.2 copy-start.2
  83.8 2.2 %copy-start.3 = (bf16[2048,1024]{1,0:T(8,128)(2,1)S(1)}, bf16[2048,1024]{1,0:T(8,128)(2,1)}, u32[]{:S(2)}) copy-start(bf16[2048,1024]{1,0:T(8,128)(2,1)} %all-gather.3.cloned.1.call-done) | copy-start | bytes 12582916
  96.0 5.7 %collective-permute-start.2 = (bf16[8,256,384]{2,1,0:T(8,128)(2,1)S(1)}, bf16[8,256,384]{2,1,0:T(8,128)(2,1)}, u32[]{:S(2)}, u32[]{:S(2)}) collective-permute-start(bf16[8,256,384]{2,1,0:T(8,128)(2,1)S(1)} %get-tuple-element.8), channel_id=1, source_target_pairs={{0,1},{1,0},{2,3},{3,2},{4,5},{5,4},{6,7},{7,6},{8,9},{9,8},{10,11... | collective-permute-start | bytes 4718600 | tf_op jit(solution)/shard_map/ppermute | solution.py:95
  104.2 13.9 %collective-permute-start.3 = (bf16[2,256,384]{2,1,0:T(8,128)(2,1)}, bf16[2,256,384]{2,1,0:T(8,128)(2,1)S(1)}, u32[]{:S(2)}, u32[]{:S(2)}) collective-permute-start(bf16[2,256,384]{2,1,0:T(8,128)(2,1)} %get-tuple-element.11), channel_id=1, source_target_pairs={{0,8},{4,12},{8,0},{12,4},{1,9},{5,13},{9,1},{13,5},{2,10},{6,14},... | collective-permute-start | bytes 1179656 | tf_op jit(solution)/shard_map/ppermute | solution.py:103
  108.8 17.9 %collective-permute-start.5 = (bf16[2,256,384]{2,1,0:T(8,128)(2,1)}, bf16[2,256,384]{2,1,0:T(8,128)(2,1)}, u32[]{:S(2)}, u32[]{:S(2)}) collective-permute-start(bf16[2,256,384]{2,1,0:T(8,128)(2,1)} %get-tuple-element.12), channel_id=1, source_target_pairs={{0,12},{4,0},{8,4},{12,8},{1,13},{5,1},{9,5},{13,9},{2,14},{6,2},{... | collective-permute-start | bytes 1179656 | tf_op jit(solution)/shard_map/ppermute | solution.py:103
  111.6 15.5 %collective-permute-start.4 = (bf16[2,256,384]{2,1,0:T(8,128)(2,1)S(1)}, bf16[2,256,384]{2,1,0:T(8,128)(2,1)}, u32[]{:S(2)}, u32[]{:S(2)}) collective-permute-start(bf16[2,256,384]{2,1,0:T(8,128)(2,1)S(1)} %get-tuple-element.13), channel_id=1, source_target_pairs={{0,4},{4,8},{8,12},{12,0},{1,5},{5,9},{9,13},{13,1},{2,6},{6,10},{... | collective-permute-start | bytes 1179656 | tf_op jit(solution)/shard_map/ppermute | solution.py:103
  128.6 13.9 %collective-permute-start.6 = (bf16[256,384]{1,0:T(8,128)(2,1)S(1)}, bf16[256,384]{1,0:T(8,128)(2,1)S(1)}, u32[]{:S(2)}, u32[]{:S(2)}) collective-permute-start(bf16[256,384]{1,0:T(8,128)(2,1)S(1)} %get-tuple-element.16), channel_id=1, source_target_pairs={{0,0},{1,32},{2,2},{3,34},{32,1},{33,33},{34,3},{35,35},{4,4},{5,3... | collective-permute-start | bytes 589832 | tf_op jit(solution)/shard_map/ppermute | solution.py:113
  133.7 12.9 %collective-permute-start.7 = (bf16[256,384]{1,0:T(8,128)(2,1)S(1)}, bf16[256,384]{1,0:T(8,128)(2,1)S(1)}, u32[]{:S(2)}, u32[]{:S(2)}) collective-permute-start(bf16[256,384]{1,0:T(8,128)(2,1)S(1)} %get-tuple-element.17), channel_id=1, source_target_pairs={{0,2},{1,34},{2,0},{3,32},{32,3},{33,35},{34,1},{35,33},{4,6},{5,3... | collective-permute-start | bytes 589832 | tf_op jit(solution)/shard_map/ppermute | solution.py:112
Sparse Core Ops, SparseCore 0:
  17.4 63.9 all-gather.2

commit v2 on v1

v2 whole, which is shorter than its diff:
```python
import jax
import jax.numpy as jnp
from jax import lax
from jax.experimental import pallas as pl
from jax.experimental.pallas import tpu as pltpu
from jax.sharding import Mesh, PartitionSpec as P

BLOCK = 128
HALF = BLOCK // 2
Y, ZP, ZQ, X, ZH, C = 8, 2, 2, 4, 2, 2
AXES = ("y", "p", "q", "x", "zh", "c")
DP, TENSOR = ("y", "p", "q"), ("x", "zh", "c")
VMEM_BYTES = 56 * 1024 * 1024


def flip(size):
    return [(i, i ^ 1) for i in range(size)]


def stack_rows(half, tokens, along_q, along_x, along_qx, out):
    out[:HALF] = tokens[pl.ds(pl.multiple_of(half[0] * HALF, HALF), HALF), :]
    out[HALF : 2 * HALF] = along_q[...]
    out[2 * HALF : 3 * HALF] = along_x[...]
    out[3 * HALF :] = along_qx[...]


def stacked(half, tokens, *received):
    whole = pl.BlockSpec(memory_space=pltpu.VMEM)
    return pl.pallas_call(
        stack_rows,
        out_shape=jax.ShapeDtypeStruct((4 * HALF, tokens.shape[1]), tokens.dtype),
        in_specs=[pl.BlockSpec(memory_space=pltpu.SMEM)] + [whole] * 4,
        out_specs=whole,
    )(half.reshape(1), tokens, *received)


def project(order, tokens, down, weight, up, keep, send):
    tiles, rows, features = tokens.shape
    columns = keep.shape[1]
    rank = down.shape[1] // (tiles * ZQ)
    mine = tokens[:, : rows // 2, :].reshape(-1, features)
    pair = tokens[:, rows // 2 :, :].reshape(-1, features)
    across = (((1,), (1,)), ((), ()))
    shrink = lax.dot_general(mine, down[0], across, preferred_element_type=jnp.float32)
    shrink += lax.dot_general(pair, down[1], across, preferred_element_type=jnp.float32)
    row = lax.broadcasted_iota(jnp.int32, shrink.shape, 0) // HALF
    col = lax.broadcasted_iota(jnp.int32, shrink.shape, 1) // rank
    low = jnp.where(row == col, 0.5 * shrink, 0.0).astype(jnp.bfloat16)
    total = jnp.dot(mine, weight[0], preferred_element_type=jnp.float32)
    total += jnp.dot(pair, weight[1], preferred_element_type=jnp.float32)
    total += jnp.dot(low, up[...], preferred_element_type=jnp.float32)
    total = total.astype(keep.dtype)
    keep[...] = total[:, :columns]
    send[...] = total[:, columns:]


def partials(x, gathered, down, weight, up):
    rows, features = gathered.shape[1:]
    columns = weight.shape[2] // 2

    def place(t, order):
        return (t + order[0]) % X

    out = jax.ShapeDtypeStruct((X, rows, columns), jnp.bfloat16)
    return pl.pallas_call(
        project,
        out_shape=(out, out),
        grid_spec=pltpu.PrefetchScalarGridSpec(
            num_scalar_prefetch=1,
            grid=(X,),
            in_specs=[
                pl.BlockSpec((2, rows, features), lambda t, order: (place(t, order), 0, 0)),
                pl.BlockSpec(
                    (2, None) + down.shape[2:], lambda t, order: (0, place(t, order), 0, 0)
                ),
                pl.BlockSpec(weight.shape, lambda t, order: (0, 0, 0)),
                pl.BlockSpec((None,) + up.shape[1:], lambda t, order: (place(t, order), 0, 0)),
            ],
            out_specs=[pl.BlockSpec((None, rows, columns), lambda t, order: (t, 0, 0))] * 2,
        ),
        compiler_params=pltpu.CompilerParams(vmem_limit_bytes=VMEM_BYTES),
        cost_estimate=pl.CostEstimate(
            flops=4 * gathered.size * columns,
            bytes_accessed=2 * (gathered.size + weight.size + 2 * X * rows * columns),
            transcendentals=0,
        ),
    )(x.reshape(1), gathered, down, weight, up)


def local(
    tokens, query_key_value_weight, adapter_down_weight, adapter_up_weight, adapter_per_block
):
    p, q, x, zh, c = (lax.axis_index(a) for a in AXES[1:])
    features = tokens.shape[1]
    columns = query_key_value_weight.shape[1]
    rank = adapter_down_weight.shape[1]
    half = x % 2

    same = lax.dynamic_slice_in_dim(tokens, half * HALF, HALF, 0)
    rest = lax.dynamic_slice_in_dim(tokens, (1 - half) * HALF, HALF, 0)
    along_q = lax.ppermute(same, "q", flip(ZQ))
    along_x = lax.ppermute(rest, "x", flip(X))
    along_qx = lax.ppermute(
        rest, ("q", "x"), [(i * X + j, (1 - i) * X + (j ^ 1)) for i in range(ZQ) for j in range(X)]
    )
    rows = stacked(half, tokens, along_q, along_x, along_qx)
    gathered = lax.all_gather(rows, "y", axis=0, tiled=False)

    first = query_key_value_weight
    second = lax.ppermute(first, "p", flip(ZP))
    first_pair = lax.ppermute(first, "x", flip(X))
    second_pair = lax.ppermute(second, "x", flip(X))
    mine_kept = c == p
    weight = jnp.stack(
        [
            jnp.where(mine_kept, jnp.concatenate(v, 1), jnp.concatenate(v[::-1], 1))
            for v in ((first, second), (first_pair, second_pair))
        ]
    )

    per = adapter_per_block.reshape(Y, ZP, ZQ)
    per = jnp.where(q == 0, per, per[:, :, ::-1])
    mine = jnp.where(p == 0, per[:, 0], per[:, 1]).reshape(-1)
    theirs = jnp.where(p == 0, per[:, 1], per[:, 0]).reshape(-1)
    down = adapter_down_weight[mine].reshape(X, 2 * ZQ * rank, features)
    down = jnp.stack([down, lax.ppermute(down, "x", flip(X))])
    up_first = adapter_up_weight[mine].reshape(X, 2 * ZQ * rank, columns)
    up_second = lax.ppermute(
        adapter_up_weight[theirs].reshape(X, 2 * ZQ * rank, columns), "p", flip(ZP)
    )
    up = jnp.where(
        mine_kept,
        jnp.concatenate([up_first, up_second], 2),
        jnp.concatenate([up_second, up_first], 2),
    )

    keep, send = partials(x, gathered, down, weight, up)
    received = lax.ppermute(send, "c", flip(C))

    def added(d):
        return keep[d].astype(jnp.float32) + received[d].astype(jnp.float32)

    def moved(d):
        shift = [(i, (i + d) % X) for i in range(X)]
        return lax.ppermute(added(d).astype(jnp.bfloat16), "x", shift).astype(jnp.float32)

    across = moved(2)
    beside = moved(1) + moved(3)
    total = jnp.stack([added(0) + across, beside]).astype(jnp.bfloat16)
    total = total.reshape(2, ZH, ZQ * HALF, columns)

    here = jnp.where(zh == 0, total[:, 0], total[:, 1])
    there = jnp.where(zh == 0, total[:, 1], total[:, 0])
    places = [(i, h, j) for i in range(ZP) for h in range(ZH) for j in range(C)]
    swap = [(i * 4 + h * 2 + j, j * 4 + h * 2 + i) for i, h, j in places]
    cross = [(i * 4 + h * 2 + j, j * 4 + (1 - h) * 2 + i) for i, h, j in places]
    far = lax.ppermute(there, ("p", "zh", "c"), cross)
    near = lax.ppermute(here, ("p", "zh", "c"), swap)
    out = near.astype(jnp.float32) + far.astype(jnp.float32)
    out = out.reshape(2, ZQ, HALF, columns)
    out = jnp.where(half == 0, out, out[::-1])
    out = jnp.where(q == 0, out, out[:, ::-1])
    return out.transpose(1, 0, 2, 3).reshape(ZQ * BLOCK, columns).astype(jnp.bfloat16)


def solution(mesh):
    physical = Mesh(mesh.devices.reshape(Y, ZP, ZQ, X, ZH, C), AXES)
    return jax.shard_map(
        local,
        mesh=physical,
        in_specs=(
            P(DP, TENSOR),
            P(TENSOR, DP),
            P(None, None, TENSOR),
            P(None, None, DP),
            P(),
        ),
        out_specs=P(TENSOR, DP),
        check_vma=False,
    )
```

time: 155 us -> 148 us (0.955)
  waiting for transfers between devices: 76 us -> 56.4 us
  starting transfers between devices: 35.7 us -> 48.6 us
  local copies, waits for them, and re-layouts: 8.37 us -> 5.61 us
    ppermute x6 -> x12, starting transfers between devices: 25.5 us -> 37.7 us  [the longest x3 9.64 us: moved(): lax.ppermute(added(d).astype(jnp.bfloat16), 'x', shift).astype(jnp.float32)]
    ppermute x6 -> x12, waiting for transfers between devices: 61.5 us -> 49.9 us  [the longest x1 28.3 us: local(): second = lax.ppermute(first, 'p', flip(ZP))]
    all_gather x1, waiting for transfers between devices: 6.78 us -> 0.01 us  [local(): gathered = lax.all_gather(rows, 'y', axis=0, tiled=False)]
    another operation x0 -> x4, other arithmetic: none -> 5.21 us  [the longest x1 2.2 us: local(): down = jnp.stack([down, lax.ppermute(down, 'x', flip(X))])]
    ppermute x1, waiting for transfers between devices: 4.04 us -> 0.01 us  [local(): far = lax.ppermute(there, ('p', 'zh', 'c'), cross)]
    unnamed x12 -> x14, local copies, waits for them, and re-layouts: 4.6 us -> 0.67 us
    concatenate x2 -> x0, other arithmetic: 2.84 us -> none  [the longest x1 1.76 us: local(): jnp.concatenate([tokens, other], 0)]
    ppermute x1, waiting for transfers between devices: 3.72 us -> 6.53 us  [local(): near = lax.ppermute(here, ('p', 'zh', 'c'), swap)]
  transfers between devices with their start and end apart: 9 -> 15, of which waited for: 9 -> 9; matrix products, arithmetic and copies ran while one was open for 5% -> 9% of each run, Pallas kernels for 0% -> 0%
where the time goes in v2:
time: 148 us; the launch traced here: 146 us
  waiting for transfers between devices  56.4 us (38%)
  starting transfers between devices  48.6 us (33%)
  between operations  13.8 us (9%)
  other arithmetic  10.9 us (7%)
  Pallas kernels  10.6 us (7%)
  local copies, waits for them, and re-layouts  5.61 us (4%)
    ppermute x1, waiting for transfers between devices, local(): second = lax.ppermute(first, 'p', flip(ZP))  28.3 us
    ppermute x3, starting transfers between devices, moved(): lax.ppermute(added(d).astype(jnp.bfloat16), 'x', shift).astype(jnp.float32)  9.64 us
    ppermute x1, waiting for transfers between devices, local(): lax.ppermute(adapter_up_weight[theirs].reshape(X, 2 * ZQ * rank, columns)...  9.4 us
    pallas_call x1, Pallas kernels, partials(): pl.pallas_call(project, out_shape=(out, out), grid_spec=pltpu.PrefetchSca...  8.65 us
    ppermute x1, starting transfers between devices, local(): far = lax.ppermute(there, ('p', 'zh', 'c'), cross)  7.24 us
    ppermute x1, waiting for transfers between devices, local(): near = lax.ppermute(here, ('p', 'zh', 'c'), swap)  6.53 us
    ppermute x1, starting transfers between devices, local(): second = lax.ppermute(first, 'p', flip(ZP))  5.7 us
    ppermute x1, starting transfers between devices, local(): along_q = lax.ppermute(same, 'q', flip(ZQ))  4.83 us
  transfers between devices with their start and end apart: 15, of which 9 were waited for; matrix products, arithmetic and copies ran while one was open for 9% of the time, Pallas kernels for 0%

profile of v2, /device:TPU:1, one launch (start us, length us, event | category | flops | bytes accessed | tf_op | source)
XLA Modules:
  0.0 146.0 jit_solution(5892150744877660785)
XLA Ops:
  6.6 1.1 constant_dynamic-slice_fusion
  7.7 4.8 %collective-permute-start = (bf16[64,1024]{1,0:T(8,128)(2,1)S(1)}, bf16[64,1024]{1,0:T(8,128)(2,1)S(1)}, u32[]{:S(2)}, u32[]{:S(2)}) collective-permute-start(bf16[64,1024]{1,0:T(8,128)(2,1)S(1)} %get-tuple-element.15), channel_id=1, source_target_pairs={{0,16},{16,0},{1,17},{17,1},{2,18},{18,2},{3,19},{19,3},{4,20},{20... | collective-permute-start | bytes 393224 | tf_op jit(solution)/shard_map/ppermute | solution.py:101
  12.6 3.1 %collective-permute-start.1 = (bf16[64,1024]{1,0:T(8,128)(2,1)S(1)}, bf16[64,1024]{1,0:T(8,128)(2,1)S(1)}, u32[]{:S(2)}, u32[]{:S(2)}) collective-permute-start(bf16[64,1024]{1,0:T(8,128)(2,1)S(1)} %get-tuple-element.14), channel_id=1, source_target_pairs={{0,4},{4,0},{8,12},{12,8},{1,5},{5,1},{9,13},{13,9},{2,6},{6,2},{1... | collective-permute-start | bytes 393224 | tf_op jit(solution)/shard_map/ppermute | solution.py:102
  15.7 1.9 %collective-permute-start.2 = (bf16[64,1024]{1,0:T(8,128)(2,1)S(1)}, bf16[64,1024]{1,0:T(8,128)(2,1)S(1)}, u32[]{:S(2)}, u32[]{:S(2)}) collective-permute-start(bf16[64,1024]{1,0:T(8,128)(2,1)S(1)} %get-tuple-element.14), channel_id=1, source_target_pairs={{0,20},{4,16},{8,28},{12,24},{16,4},{20,0},{24,12},{28,8},{1,21},{... | collective-permute-start | bytes 393224 | tf_op jit(solution)/shard_map/ppermute | solution.py:103
  18.3 4.1 %collective-permute-done.2.along_qx = bf16[64,1024]{1,0:T(8,128)(2,1)S(1)} collective-permute-done((bf16[64,1024]{1,0:T(8,128)(2,1)S(1)}, bf16[64,1024]{1,0:T(8,128)(2,1)S(1)}, u32[]{:S(2)}, u32[]{:S(2)}) %collective-permute-start.2) | collective-permute-done | bytes 131104 | tf_op jit(solution)/shard_map/ppermute | solution.py:103
  23.1 2.0 %shard_map.55 = bf16[256,1024]{1,0:T(8,128)(2,1)} custom-call(s32[1]{0:T(128)} %bitcast.1.half, bf16[128,1024]{1,0:T(8,128)(2,1)} %tokens.1, bf16[64,1024]{1,0:T(8,128)(2,1)} %copy-done.3, bf16[64,1024]{1,0:T(8,128)(2,1)} %copy-done.4, bf16[64,1024]{1,0:T(8,128)(2,1)} %copy-done.5), custom_call_target="tpu_custom_call" | custom-call | tf_op jit(solution)/shard_map/pallas_call | solution.py:29
  25.1 5.7 %collective-permute-start.4 = (bf16[1024,384]{1,0:T(8,128)(2,1)S(1)}, bf16[1024,384]{1,0:T(8,128)(2,1)S(1)}, u32[]{:S(2)}, u32[]{:S(2)}) collective-permute-start(bf16[1024,384]{1,0:T(8,128)(2,1)S(1)} %copy-done.1), channel_id=1, source_target_pairs={{0,32},{32,0},{1,33},{33,1},{2,34},{34,2},{3,35},{35,3},{4,36},{36... | collective-permute-start | bytes 2359304 | tf_op jit(solution)/shard_map/ppermute | solution.py:110
  31.9 2.2 %collective-permute-start.3 = (bf16[4,64,1024]{2,1,0:T(8,128)(2,1)S(1)}, bf16[4,64,1024]{2,1,0:T(8,128)(2,1)}, u32[]{:S(2)}, u32[]{:S(2)}) collective-permute-start(bf16[4,64,1024]{2,1,0:T(8,128)(2,1)S(1)} %bitcast.51), channel_id=1, source_target_pairs={{0,4},{4,0},{8,12},{12,8},{1,5},{5,1},{9,13},{13,9},{2,6},{6,2},{1... | collective-permute-start | bytes 1572872 | tf_op jit(solution)/shard_map/ppermute | solution.py:126
  34.0 3.1 %collective-permute-start.5 = (bf16[1024,384]{1,0:T(8,128)(2,1)S(1)}, bf16[1024,384]{1,0:T(8,128)(2,1)}, u32[]{:S(2)}, u32[]{:S(2)}) collective-permute-start(bf16[1024,384]{1,0:T(8,128)(2,1)S(1)} %copy-done.1), channel_id=1, source_target_pairs={{0,4},{4,0},{8,12},{12,8},{1,5},{5,1},{9,13},{13,9},{2,6},{6,2},{1... | collective-permute-start | bytes 2359304 | tf_op jit(solution)/shard_map/ppermute | solution.py:111
  37.2 28.3 %collective-permute-done.4 = bf16[1024,384]{1,0:T(8,128)(2,1)S(1)} collective-permute-done((bf16[1024,384]{1,0:T(8,128)(2,1)S(1)}, bf16[1024,384]{1,0:T(8,128)(2,1)S(1)}, u32[]{:S(2)}, u32[]{:S(2)}) %collective-permute-start.4) | collective-permute-done | bytes 786464 | tf_op jit(solution)/shard_map/ppermute | solution.py:110
  65.5 2.2 %collective-permute-start.6 = (bf16[1024,384]{1,0:T(8,128)(2,1)S(1)}, bf16[1024,384]{1,0:T(8,128)(2,1)}, u32[]{:S(2)}, u32[]{:S(2)}) collective-permute-start(bf16[1024,384]{1,0:T(8,128)(2,1)S(1)} %collective-permute-done.4), channel_id=1, source_target_pairs={{0,4},{4,0},{8,12},{12,8},{1,5},{5,1},{9,13},{13,9},{2,6},{6,2},{1... | collective-permute-start | bytes 2359304 | tf_op jit(solution)/shard_map/ppermute | solution.py:112
  67.7 1.3 gather_fusion.2
  68.9 1.9 %collective-permute-start.7 = (bf16[4,64,384]{2,1,0:T(8,128)(2,1)}, bf16[4,64,384]{2,1,0:T(8,128)(2,1)S(1)}, u32[]{:S(2)}, u32[]{:S(2)}) collective-permute-start(bf16[4,64,384]{2,1,0:T(8,128)(2,1)} %bitcast.61), channel_id=1, source_target_pairs={{0,32},{32,0},{1,33},{33,1},{2,34},{34,2},{3,35},{35,3},{4,36},{36... | collective-permute-start | bytes 589832 | tf_op jit(solution)/shard_map/ppermute | solution.py:128
  70.9 1.6 %gather_fusion.1 = bf16[16,16,384]{2,1,0:T(8,128)(2,1)S(1)} fusion(bf16[32,16,384]{2,1,0:T(8,128)(2,1)} %param.8, s32[1024]{0:T(1024)S(1)} %pad_clamp_fusion.1), kind=kCustom, calls=%fused_computation.1 | custom fusion | bytes 393280 | tf_op jit(solution)/shard_map/gather | solution.py:127
  72.5 9.4 %collective-permute-done.7 = bf16[4,64,384]{2,1,0:T(8,128)(2,1)S(1)} collective-permute-done((bf16[4,64,384]{2,1,0:T(8,128)(2,1)}, bf16[4,64,384]{2,1,0:T(8,128)(2,1)S(1)}, u32[]{:S(2)}, u32[]{:S(2)}) %collective-permute-start.7) | collective-permute-done | bytes 196640 | tf_op jit(solution)/shard_map/ppermute | solution.py:128
  82.7 2.2 %pad_maximum_fusion.1.down = bf16[2,4,64,1024]{3,2,1,0:T(8,128)(2,1)} fusion(bf16[1,4,64,1024]{3,2,1,0:T(8,128)(2,1)} %bitcast.6, bf16[1,4,64,1024]{3,2,1,0:T(8,128)(2,1)S(1)} %bitcast.52), kind=kLoop, calls=%fused_computation.6 | loop fusion | flops 524288 | bytes 2097152 | tf_op jit(solution)/shard_map/stack | solution.py:126
  85.3 0.9 collective-permute-done.6
  86.2 2.3 %maximum_select_fusion.1 = bf16[1,1024,768]{2,1,0:T(8,128)(2,1)S(1)} fusion(bf16[1,1024,384]{2,1,0:T(8,128)(2,1)} %bitcast.10, bf16[1,1024,384]{2,1,0:T(8,128)(2,1)} %bitcast.9, pred[]{:T(512)S(6)} %eq.24), kind=kLoop, calls=%fused_computation.5 | loop fusion | flops 7077888 | bytes 3145729 | tf_op jit(solution)/shard_map/jit(_where)/select_n | solution.py:116
  88.5 2.0 %pad_maximum_fusion.weight = bf16[2,1024,768]{2,1,0:T(8,128)(2,1)} fusion(bf16[1,1024,768]{2,1,0:T(8,128)(2,1)S(1)} %maximum_select_fusion.1, bf16[1,1024,768]{2,1,0:T(8,128)(2,1)S(1)} %maximum_select_fusion), kind=kLoop, calls=%fused_computation.3 | loop fusion | flops 1572864 | bytes 6291456 | tf_op jit(solution)/shard_map/stack | solution.py:114
  90.4 8.6 %shard_map.56 = (bf16[4,256,384]{2,1,0:T(8,128)(2,1)}, bf16[4,256,384]{2,1,0:T(8,128)(2,1)}) custom-call(s32[1]{0:T(128)} %bitcast.order, bf16[8,256,1024]{2,1,0:T(8,128)(2,1)} %bitcast.65, bf16[2,4,64,1024]{3,2,1,0:T(8,128)(2,1)} %pad_maximum_fusion.1.down, bf16[2,1024,768]{2,1,0:T(8,128)(2,1)} %pad_maximum_fusion.weight, ...), custom_call_target="tpu_custom_call" | custom-call | flops 3221225472 | bytes 8912896 | tf_op jit(solution)/shard_map/pallas_call | solution.py:65
  99.1 3.1 %collective-permute-start.8 = (bf16[4,256,384]{2,1,0:T(8,128)(2,1)}, bf16[4,256,384]{2,1,0:T(8,128)(2,1)S(1)}, u32[]{:S(2)}, u32[]{:S(2)}) collective-permute-start(bf16[4,256,384]{2,1,0:T(8,128)(2,1)} %get-tuple-element.8), channel_id=1, source_target_pairs={{0,1},{1,0},{2,3},{3,2},{4,5},{5,4},{6,7},{7,6},{8,9},{9,8},{10,11... | collective-permute-start | bytes 2359304 | tf_op jit(solution)/shard_map/ppermute | solution.py:138
  102.2 2.1 %collective-permute-done.8 = bf16[4,256,384]{2,1,0:T(8,128)(2,1)S(1)} collective-permute-done((bf16[4,256,384]{2,1,0:T(8,128)(2,1)}, bf16[4,256,384]{2,1,0:T(8,128)(2,1)S(1)}, u32[]{:S(2)}, u32[]{:S(2)}) %collective-permute-start.8) | collective-permute-done | bytes 786464 | tf_op jit(solution)/shard_map/ppermute | solution.py:138
  104.3 1.3 fusion.3
  105.6 4.4 %collective-permute-start.9 = (bf16[256,384]{1,0:T(8,128)(2,1)S(1)}, bf16[256,384]{1,0:T(8,128)(2,1)S(1)}, u32[]{:S(2)}, u32[]{:S(2)}) collective-permute-start(bf16[256,384]{1,0:T(8,128)(2,1)S(1)} %get-tuple-element.11), channel_id=1, source_target_pairs={{0,8},{4,12},{8,0},{12,4},{1,9},{5,13},{9,1},{13,5},{2,10},{6,14},... | collective-permute-start | bytes 589832 | tf_op jit(solution)/shard_map/ppermute | solution.py:145
  109.9 2.1 %collective-permute-start.11 = (bf16[256,384]{1,0:T(8,128)(2,1)S(1)}, bf16[256,384]{1,0:T(8,128)(2,1)S(1)}, u32[]{:S(2)}, u32[]{:S(2)}) collective-permute-start(bf16[256,384]{1,0:T(8,128)(2,1)S(1)} %get-tuple-element.12), channel_id=1, source_target_pairs={{0,12},{4,0},{8,4},{12,8},{1,13},{5,1},{9,5},{13,9},{2,14},{6,2},{... | collective-permute-start | bytes 589832 | tf_op jit(solution)/shard_map/ppermute | solution.py:145
  112.1 3.2 %collective-permute-start.10 = (bf16[256,384]{1,0:T(8,128)(2,1)S(1)}, bf16[256,384]{1,0:T(8,128)(2,1)S(1)}, u32[]{:S(2)}, u32[]{:S(2)}) collective-permute-start(bf16[256,384]{1,0:T(8,128)(2,1)S(1)} %get-tuple-element.13), channel_id=1, source_target_pairs={{0,4},{4,8},{8,12},{12,0},{1,5},{5,9},{9,13},{13,1},{2,6},{6,10},{... | collective-permute-start | bytes 589832 | tf_op jit(solution)/shard_map/ppermute | solution.py:145
  115.2 1.0 fusion.1
  116.3 2.6 %collective-permute-done.11 = bf16[256,384]{1,0:T(8,128)(2,1)S(1)} collective-permute-done((bf16[256,384]{1,0:T(8,128)(2,1)S(1)}, bf16[256,384]{1,0:T(8,128)(2,1)S(1)}, u32[]{:S(2)}, u32[]{:S(2)}) %collective-permute-start.11) | collective-permute-done | bytes 196640 | tf_op jit(solution)/shard_map/ppermute | solution.py:145
  118.8 1.8 %collective-permute-done.10 = bf16[256,384]{1,0:T(8,128)(2,1)S(1)} collective-permute-done((bf16[256,384]{1,0:T(8,128)(2,1)S(1)}, bf16[256,384]{1,0:T(8,128)(2,1)S(1)}, u32[]{:S(2)}, u32[]{:S(2)}) %collective-permute-start.10) | collective-permute-done | bytes 196640 | tf_op jit(solution)/shard_map/ppermute | solution.py:145
  120.8 7.2 %collective-permute-start.13 = (bf16[2,128,384]{2,1,0:T(8,128)(2,1)S(1)}, bf16[2,128,384]{2,1,0:T(8,128)(2,1)S(1)}, u32[]{:S(2)}, u32[]{:S(2)}) collective-permute-start(bf16[2,128,384]{2,1,0:T(8,128)(2,1)S(1)} %fusion.2), channel_id=1, source_target_pairs={{0,2},{1,34},{2,0},{3,32},{32,3},{33,35},{34,1},{35,33},{4,6},{5,3... | collective-permute-start | bytes 589832 | tf_op jit(solution)/shard_map/ppermute | solution.py:157
  128.0 3.7 %collective-permute-start.12 = (bf16[2,128,384]{2,1,0:T(8,128)(2,1)S(1)}, bf16[2,128,384]{2,1,0:T(8,128)(2,1)S(1)}, u32[]{:S(2)}, u32[]{:S(2)}) collective-permute-start(bf16[2,128,384]{2,1,0:T(8,128)(2,1)S(1)} %fusion.7), channel_id=1, source_target_pairs={{0,0},{1,32},{2,2},{3,34},{32,1},{33,33},{34,3},{35,35},{4,4},{5,3... | collective-permute-start | bytes 589832 | tf_op jit(solution)/shard_map/ppermute | solution.py:158
  131.7 6.5 %collective-permute-done.12 = bf16[2,128,384]{2,1,0:T(8,128)(2,1)S(1)} collective-permute-done((bf16[2,128,384]{2,1,0:T(8,128)(2,1)S(1)}, bf16[2,128,384]{2,1,0:T(8,128)(2,1)S(1)}, u32[]{:S(2)}, u32[]{:S(2)}) %collective-permute-start.12) | collective-permute-done | bytes 196640 | tf_op jit(solution)/shard_map/ppermute | solution.py:158
  (42 shorter events, 4.5 us)
Async XLA Ops:
  6.5 24.7 %copy-start = (bf16[32,16,1024]{2,1,0:T(8,128)(2,1)S(1)}, bf16[32,16,1024]{2,1,0:T(8,128)(2,1)}, u32[]{:S(2)}) copy-start(bf16[32,16,1024]{2,1,0:T(8,128)(2,1)} %param.7) | copy-start | bytes 3145732
  6.5 18.5 %copy-start.1 = (bf16[1024,384]{1,0:T(8,128)(2,1)S(1)}, bf16[1024,384]{1,0:T(8,128)(2,1)}, u32[]{:S(2)}) copy-start(bf16[1024,384]{1,0:T(8,128)(2,1)} %param.6) | copy-start | bytes 2359300
  6.5 24.3 %copy-start.6 = (s32[32]{0:T(128)S(1)}, s32[32]{0:T(128)}, u32[]{:S(2)}) copy-start(s32[32]{0:T(128)} %param.9) | copy-start | bytes 388
  6.5 83.9 %all-gather.3.cloned.1.call-start = ((), (), s32[]{:S(2)}) async-start(), calls=%async_computation | async-start | bytes 4718592 | tf_op jit(solution)/shard_map/all_gather | solution.py:107
  6.6 61.1 %copy-start.2 = (bf16[32,16,384]{2,1,0:T(8,128)(2,1)S(1)}, bf16[32,16,384]{2,1,0:T(8,128)(2,1)}, u32[]{:S(2)}) copy-start(bf16[32,16,384]{2,1,0:T(8,128)(2,1)} %param.8) | copy-start | bytes 1179652
  7.7 9.9 %collective-permute-start = (bf16[64,1024]{1,0:T(8,128)(2,1)S(1)}, bf16[64,1024]{1,0:T(8,128)(2,1)S(1)}, u32[]{:S(2)}, u32[]{:S(2)}) collective-permute-start(bf16[64,1024]{1,0:T(8,128)(2,1)S(1)} %get-tuple-element.15), channel_id=1, source_target_pairs={{0,16},{16,0},{1,17},{17,1},{2,18},{18,2},{3,19},{19,3},{4,20},{20... | collective-permute-start | bytes 393224 | tf_op jit(solution)/shard_map/ppermute | solution.py:101
  12.6 5.7 %collective-permute-start.1 = (bf16[64,1024]{1,0:T(8,128)(2,1)S(1)}, bf16[64,1024]{1,0:T(8,128)(2,1)S(1)}, u32[]{:S(2)}, u32[]{:S(2)}) collective-permute-start(bf16[64,1024]{1,0:T(8,128)(2,1)S(1)} %get-tuple-element.14), channel_id=1, source_target_pairs={{0,4},{4,0},{8,12},{12,8},{1,5},{5,1},{9,13},{13,9},{2,6},{6,2},{1... | collective-permute-start | bytes 393224 | tf_op jit(solution)/shard_map/ppermute | solution.py:102
  15.7 6.7 %collective-permute-start.2 = (bf16[64,1024]{1,0:T(8,128)(2,1)S(1)}, bf16[64,1024]{1,0:T(8,128)(2,1)S(1)}, u32[]{:S(2)}, u32[]{:S(2)}) collective-permute-start(bf16[64,1024]{1,0:T(8,128)(2,1)S(1)} %get-tuple-element.14), channel_id=1, source_target_pairs={{0,20},{4,16},{8,28},{12,24},{16,4},{20,0},{24,12},{28,8},{1,21},{... | collective-permute-start | bytes 393224 | tf_op jit(solution)/shard_map/ppermute | solution.py:103
  17.6 4.8 %copy-start.3 = (bf16[64,1024]{1,0:T(8,128)(2,1)}, bf16[64,1024]{1,0:T(8,128)(2,1)S(1)}, u32[]{:S(2)}) copy-start(bf16[64,1024]{1,0:T(8,128)(2,1)S(1)} %collective-permute-done.along_q) | copy-start | bytes 393220
  18.3 4.1 %copy-start.4 = (bf16[64,1024]{1,0:T(8,128)(2,1)}, bf16[64,1024]{1,0:T(8,128)(2,1)S(1)}, u32[]{:S(2)}) copy-start(bf16[64,1024]{1,0:T(8,128)(2,1)S(1)} %collective-permute-done.1.along_x) | copy-start | bytes 393220
  22.4 0.7 copy-start.5
  25.1 40.4 %collective-permute-start.4 = (bf16[1024,384]{1,0:T(8,128)(2,1)S(1)}, bf16[1024,384]{1,0:T(8,128)(2,1)S(1)}, u32[]{:S(2)}, u32[]{:S(2)}) collective-permute-start(bf16[1024,384]{1,0:T(8,128)(2,1)S(1)} %copy-done.1), channel_id=1, source_target_pairs={{0,32},{32,0},{1,33},{33,1},{2,34},{34,2},{3,35},{35,3},{4,36},{36... | collective-permute-start | bytes 2359304 | tf_op jit(solution)/shard_map/ppermute | solution.py:110
  31.9 50.9 %collective-permute-start.3 = (bf16[4,64,1024]{2,1,0:T(8,128)(2,1)S(1)}, bf16[4,64,1024]{2,1,0:T(8,128)(2,1)}, u32[]{:S(2)}, u32[]{:S(2)}) collective-permute-start(bf16[4,64,1024]{2,1,0:T(8,128)(2,1)S(1)} %bitcast.51), channel_id=1, source_target_pairs={{0,4},{4,0},{8,12},{12,8},{1,5},{5,1},{9,13},{13,9},{2,6},{6,2},{1... | collective-permute-start | bytes 1572872 | tf_op jit(solution)/shard_map/ppermute | solution.py:126
  34.0 51.3 %collective-permute-start.5 = (bf16[1024,384]{1,0:T(8,128)(2,1)S(1)}, bf16[1024,384]{1,0:T(8,128)(2,1)}, u32[]{:S(2)}, u32[]{:S(2)}) collective-permute-start(bf16[1024,384]{1,0:T(8,128)(2,1)S(1)} %copy-done.1), channel_id=1, source_target_pairs={{0,4},{4,0},{8,12},{12,8},{1,5},{5,1},{9,13},{13,9},{2,6},{6,2},{1... | collective-permute-start | bytes 2359304 | tf_op jit(solution)/shard_map/ppermute | solution.py:111
  65.5 20.7 %collective-permute-start.6 = (bf16[1024,384]{1,0:T(8,128)(2,1)S(1)}, bf16[1024,384]{1,0:T(8,128)(2,1)}, u32[]{:S(2)}, u32[]{:S(2)}) collective-permute-start(bf16[1024,384]{1,0:T(8,128)(2,1)S(1)} %collective-permute-done.4), channel_id=1, source_target_pairs={{0,4},{4,0},{8,12},{12,8},{1,5},{5,1},{9,13},{13,9},{2,6},{6,2},{1... | collective-permute-start | bytes 2359304 | tf_op jit(solution)/shard_map/ppermute | solution.py:112
  68.9 12.9 %collective-permute-start.7 = (bf16[4,64,384]{2,1,0:T(8,128)(2,1)}, bf16[4,64,384]{2,1,0:T(8,128)(2,1)S(1)}, u32[]{:S(2)}, u32[]{:S(2)}) collective-permute-start(bf16[4,64,384]{2,1,0:T(8,128)(2,1)} %bitcast.61), channel_id=1, source_target_pairs={{0,32},{32,0},{1,33},{33,1},{2,34},{34,2},{3,35},{35,3},{4,36},{36... | collective-permute-start | bytes 589832 | tf_op jit(solution)/shard_map/ppermute | solution.py:128
  99.1 5.2 %collective-permute-start.8 = (bf16[4,256,384]{2,1,0:T(8,128)(2,1)}, bf16[4,256,384]{2,1,0:T(8,128)(2,1)S(1)}, u32[]{:S(2)}, u32[]{:S(2)}) collective-permute-start(bf16[4,256,384]{2,1,0:T(8,128)(2,1)} %get-tuple-element.8), channel_id=1, source_target_pairs={{0,1},{1,0},{2,3},{3,2},{4,5},{5,4},{6,7},{7,6},{8,9},{9,8},{10,11... | collective-permute-start | bytes 2359304 | tf_op jit(solution)/shard_map/ppermute | solution.py:138
  105.6 9.7 %collective-permute-start.9 = (bf16[256,384]{1,0:T(8,128)(2,1)S(1)}, bf16[256,384]{1,0:T(8,128)(2,1)S(1)}, u32[]{:S(2)}, u32[]{:S(2)}) collective-permute-start(bf16[256,384]{1,0:T(8,128)(2,1)S(1)} %get-tuple-element.11), channel_id=1, source_target_pairs={{0,8},{4,12},{8,0},{12,4},{1,9},{5,13},{9,1},{13,5},{2,10},{6,14},... | collective-permute-start | bytes 589832 | tf_op jit(solution)/shard_map/ppermute | solution.py:145
  109.9 8.9 %collective-permute-start.11 = (bf16[256,384]{1,0:T(8,128)(2,1)S(1)}, bf16[256,384]{1,0:T(8,128)(2,1)S(1)}, u32[]{:S(2)}, u32[]{:S(2)}) collective-permute-start(bf16[256,384]{1,0:T(8,128)(2,1)S(1)} %get-tuple-element.12), channel_id=1, source_target_pairs={{0,12},{4,0},{8,4},{12,8},{1,13},{5,1},{9,5},{13,9},{2,14},{6,2},{... | collective-permute-start | bytes 589832 | tf_op jit(solution)/shard_map/ppermute | solution.py:145
  112.1 8.6 %collective-permute-start.10 = (bf16[256,384]{1,0:T(8,128)(2,1)S(1)}, bf16[256,384]{1,0:T(8,128)(2,1)S(1)}, u32[]{:S(2)}, u32[]{:S(2)}) collective-permute-start(bf16[256,384]{1,0:T(8,128)(2,1)S(1)} %get-tuple-element.13), channel_id=1, source_target_pairs={{0,4},{4,8},{8,12},{12,0},{1,5},{5,9},{9,13},{13,1},{2,6},{6,10},{... | collective-permute-start | bytes 589832 | tf_op jit(solution)/shard_map/ppermute | solution.py:145
  120.8 10.9 %collective-permute-start.13 = (bf16[2,128,384]{2,1,0:T(8,128)(2,1)S(1)}, bf16[2,128,384]{2,1,0:T(8,128)(2,1)S(1)}, u32[]{:S(2)}, u32[]{:S(2)}) collective-permute-start(bf16[2,128,384]{2,1,0:T(8,128)(2,1)S(1)} %fusion.2), channel_id=1, source_target_pairs={{0,2},{1,34},{2,0},{3,32},{32,3},{33,35},{34,1},{35,33},{4,6},{5,3... | collective-permute-start | bytes 589832 | tf_op jit(solution)/shard_map/ppermute | solution.py:157
  128.0 10.2 %collective-permute-start.12 = (bf16[2,128,384]{2,1,0:T(8,128)(2,1)S(1)}, bf16[2,128,384]{2,1,0:T(8,128)(2,1)S(1)}, u32[]{:S(2)}, u32[]{:S(2)}) collective-permute-start(bf16[2,128,384]{2,1,0:T(8,128)(2,1)S(1)} %fusion.7), channel_id=1, source_target_pairs={{0,0},{1,32},{2,2},{3,34},{32,1},{33,33},{34,3},{35,35},{4,4},{5,3... | collective-permute-start | bytes 589832 | tf_op jit(solution)/shard_map/ppermute | solution.py:158
Sparse Core Ops, SparseCore 0:
  25.2 62.1 all-gather.2

commit v3 on v0

v3 whole, which is shorter than its diff:
```python
import jax
import jax.numpy as jnp
from jax import lax
from jax.experimental import pallas as pl
from jax.experimental.pallas import tpu as pltpu
from jax.sharding import Mesh, PartitionSpec as P

Y, ZP, ZQ, X, ZH, C = 8, 2, 2, 4, 2, 2
AXES = ("y", "p", "q", "x", "zh", "c")
DP, TENSOR = ("y", "p", "q"), ("x", "zh", "c")
VMEM_BYTES = 48_000_000
SMALL_VMEM_BYTES = 16_000_000
DOWN_COLUMNS = 512


def flip(size):
    return [(i, i ^ 1) for i in range(size)]


def copied(moves):
    for move in moves:
        move.start()
    for move in moves:
        move.wait()


def join_features(first, second, out, sems):
    width = first.shape[1]
    copied(
        [
            pltpu.make_async_copy(v, out.at[:, pl.ds(i * width, width)], sems.at[i])
            for i, v in enumerate((first, second))
        ]
    )


def joined(first, second):
    rows, width = first.shape
    return pl.pallas_call(
        join_features,
        out_shape=jax.ShapeDtypeStruct((rows, 2 * width), first.dtype),
        in_specs=[pl.BlockSpec(memory_space=pltpu.VMEM)] * 2,
        out_specs=pl.BlockSpec(memory_space=pl.ANY),
        scratch_shapes=[pltpu.SemaphoreType.DMA((2,))],
        compiler_params=pltpu.CompilerParams(vmem_limit_bytes=SMALL_VMEM_BYTES),
    )(first, second)


def place_weights(slots, *refs):
    ins, (table, sems) = refs[:-2], refs[-2:]
    first, *halves = ins[:3]
    pair, *pair_halves = ins[3:6]
    up, up_swapped, down_own, down_pair = ins[6:]
    features, columns = first.shape
    moves = []

    def move(source, row, col):
        at = tuple(
            pl.ds(pl.multiple_of(i, 128), n) for i, n in zip((row, col), source.shape)
        )
        moves.append(pltpu.make_async_copy(source, table.at[at], sems.at[len(moves)]))

    own, other = slots[1] * columns, (1 - slots[1]) * columns
    for k, whole, split in ((slots[0], first, halves), (1 - slots[0], pair, pair_halves)):
        move(whole, k * features, own)
        for i, v in enumerate(split):
            move(v, k * features + i * v.shape[0], other)
    move(up, 2 * features, own)
    move(up_swapped, 2 * features, other)
    ranks = down_own.shape[0]
    for k, v in ((slots[0], down_own), (1 - slots[0], down_pair)):
        for i in range(features // DOWN_COLUMNS):
            row = 2 * features + ranks * (1 + k * (features // DOWN_COLUMNS) + i)
            move(v.at[:, pl.ds(i * DOWN_COLUMNS, DOWN_COLUMNS)], row, 0)
    copied(moves)


def placed(slots, parts):
    features, columns = parts[0].shape
    ranks = parts[-1].shape[0]
    down_rows = 2 * features // DOWN_COLUMNS * ranks
    return pl.pallas_call(
        place_weights,
        out_shape=pltpu.VMEM((2 * features + ranks + down_rows, 2 * columns), parts[0].dtype),
        in_specs=[pl.BlockSpec(memory_space=pltpu.SMEM)]
        + [pl.BlockSpec(memory_space=pl.ANY)] * len(parts),
        out_specs=pl.BlockSpec(memory_space=pltpu.VMEM),
        scratch_shapes=[pltpu.SemaphoreType.DMA((16,))],
        compiler_params=pltpu.CompilerParams(vmem_limit_bytes=SMALL_VMEM_BYTES),
    )(slots, *parts)


def project(order, tokens, table, keep, send, held, sems):
    step = pl.program_id(0)
    rows, features = tokens.shape[1:]
    ranks = held.shape[3] - features
    rank = ranks // Y
    tiles, tile_rows, columns = keep.shape
    groups = tile_rows // rows

    def fetch(t):
        at = pl.ds((t + order[0]) % X * groups, groups)
        return pltpu.make_async_copy(
            tokens.at[at], held.at[t, :, :, pl.ds(0, features)], sems.at[t]
        )

    @pl.when(step == 0)
    def _():
        for t in range(X):
            fetch(t).start()

    here = [step * tiles + i for i in range(tiles)]
    for t in here:
        fetch(t).wait()
    for t in here:
        shrink = 0.0
        for i in range(features // DOWN_COLUMNS):
            at = slice(i * DOWN_COLUMNS, (i + 1) * DOWN_COLUMNS)
            start = features + (1 + i) * ranks
            shrink += lax.dot_general(
                held[t, :, :, at].reshape(tile_rows, DOWN_COLUMNS),
                table[start : start + ranks, :DOWN_COLUMNS],
                (((1,), (1,)), ((), ())),
                preferred_element_type=jnp.float32,
            )
        block = lax.broadcasted_iota(jnp.int32, shrink.shape, 0) // rows
        block += (t + order[0]) % X * groups
        adapter = lax.broadcasted_iota(jnp.int32, shrink.shape, 1) // rank
        low = jnp.where(block == adapter, 0.5 * shrink, 0.0).astype(held.dtype)
        held[t, :, :, features:] = low.reshape(groups, rows, ranks)
    for i, t in enumerate(here):
        tok = held[t].reshape(tile_rows, features + ranks)
        total = jnp.dot(tok, table[: features + ranks], preferred_element_type=jnp.float32)
        total = total.astype(keep.dtype)
        keep[i] = total[:, :columns]
        send[i] = total[:, columns:]


def partials(x, gathered, table, ranks):
    rows, features = gathered.shape[1:]
    columns = table.shape[1] // 2
    groups = Y // X
    tiles = 2
    out = jax.ShapeDtypeStruct((X, groups * rows, columns), jnp.bfloat16)
    return pl.pallas_call(
        project,
        out_shape=(out, out),
        grid_spec=pltpu.PrefetchScalarGridSpec(
            num_scalar_prefetch=1,
            grid=(X // tiles,),
            in_specs=[
                pl.BlockSpec(memory_space=pltpu.HBM),
                pl.BlockSpec(memory_space=pltpu.VMEM),
            ],
            out_specs=[
                pl.BlockSpec((tiles,) + out.shape[1:], lambda t, order: (t, 0, 0))
            ]
            * 2,
            scratch_shapes=[
                pltpu.VMEM((X, groups, rows, features + ranks), jnp.bfloat16),
                pltpu.SemaphoreType.DMA((X,)),
            ],
        ),
        compiler_params=pltpu.CompilerParams(vmem_limit_bytes=VMEM_BYTES),
        cost_estimate=pl.CostEstimate(
            flops=4 * gathered.size * columns,
            bytes_accessed=2 * (gathered.size + table.size + 2 * out.size),
            transcendentals=0,
        ),
    )(x.reshape(1), gathered, table)


def local(
    tokens, query_key_value_weight, adapter_down_weight, adapter_up_weight, adapter_per_block
):
    p, q, x, zh, c = (lax.axis_index(a) for a in AXES[1:])
    rows, features = tokens.shape
    columns = query_key_value_weight.shape[1]
    half = x % 2
    order = jnp.where(q == half, 0, 1)

    grid = [(i, j) for i in range(ZQ) for j in range(X)]

    def over(target):
        return [(i * X + j, target(i, j)) for i, j in grid]

    first = lax.ppermute(
        tokens, ("q", "x"), over(lambda i, j: i * X + j if i == j % 2 else (1 - i) * X + (j ^ 1))
    )
    second = lax.ppermute(
        tokens, ("q", "x"), over(lambda i, j: (1 - i) * X + j if i == j % 2 else i * X + (j ^ 1))
    )
    gathered = lax.all_gather(joined(first, second), "y", axis=0, tiled=False)

    per = adapter_per_block.reshape(Y, ZP, ZQ)

    def adapters(i, j):
        return lax.dynamic_slice(per, (0, i, j), (Y, 1, 1)).reshape(Y)

    def taken(table, i, j):
        return table[adapters(i, j)].reshape(-1, table.shape[2])

    down = taken(adapter_down_weight, p, half)
    down_pair = lax.ppermute(taken(adapter_down_weight, p, 1 - half), "x", flip(X))
    up = taken(adapter_up_weight, p, half)
    up_swapped = lax.ppermute(taken(adapter_up_weight, 1 - p, half), "p", flip(ZP))

    own = query_key_value_weight
    pair = lax.ppermute(own, "x", flip(X))
    swapped = [lax.ppermute(v, "p", flip(ZP)) for v in jnp.split(own, 2)]
    swapped_pair = [lax.ppermute(v, "x", flip(X)) for v in swapped]
    slots = jnp.stack([order, jnp.where(c == p, 0, 1)]).astype(jnp.int32)
    table = placed(
        slots, [own, *swapped, pair, *swapped_pair, up, up_swapped, down, down_pair]
    )

    keep, send = partials(x, gathered, table, down.shape[0])
    received = lax.ppermute(send, "c", flip(C))

    def added(d):
        return keep[d].astype(jnp.float32) + received[d].astype(jnp.float32)

    def moved(d):
        shift = [(i, (i + d) % X) for i in range(X)]
        return lax.ppermute(added(d).astype(jnp.bfloat16), "x", shift).astype(jnp.float32)

    across = moved(2)
    beside = moved(3) + moved(1)
    total = jnp.stack([added(0) + across, beside]).astype(jnp.bfloat16)
    total = total.reshape(2, ZH, rows, columns)

    here = jnp.where(zh == 0, total[:, 0], total[:, 1])
    there = jnp.where(zh == 0, total[:, 1], total[:, 0])
    places = [(i, h, j) for i in range(ZP) for h in range(ZH) for j in range(C)]
    swap = [(i * 4 + h * 2 + j, j * 4 + h * 2 + i) for i, h, j in places]
    cross = [(i * 4 + h * 2 + j, j * 4 + (1 - h) * 2 + i) for i, h, j in places]
    far = lax.ppermute(there, ("p", "zh", "c"), cross)
    near = lax.ppermute(here, ("p", "zh", "c"), swap)
    out = near.astype(jnp.float32) + far.astype(jnp.float32)
    out = jnp.where(half == 0, out, out[::-1])
    return out.reshape(ZQ * rows, columns).astype(jnp.bfloat16)


def solution(mesh):
    physical = Mesh(mesh.devices.reshape(Y, ZP, ZQ, X, ZH, C), AXES)
    return jax.shard_map(
        local,
        mesh=physical,
        in_specs=(
            P(DP, TENSOR),
            P(TENSOR, DP),
            P(None, None, TENSOR),
            P(None, None, DP),
            P(),
        ),
        out_specs=P(TENSOR, DP),
        check_vma=False,
    )
```

time: 514 us -> 140 us (0.27)
  waiting for transfers between devices: 479 us -> 49 us
  starting transfers between devices: 0.08 us -> 52.3 us
  matrix products: 15.8 us -> 0 us
  local copies, waits for them, and re-layouts: 2.86 us -> 13.2 us
  Pallas kernels: 0 us -> 9.74 us
    all_gather x1, waiting for transfers between devices: 199 us -> 2.61 us  [local(): gathered = lax.all_gather(joined(first, second), 'y', axis=0, tiled=False)]
    psum x1 -> x0, waiting for transfers between devices: 171 us -> none  [local(): lax.psum(shrink_part.astype(jnp.bfloat16), 'tensor').astype(jnp.float32)]
    reduce_scatter x1 -> x0, waiting for transfers between devices: 109 us -> none  [local(): lax.psum_scatter(partial_value.astype(jnp.bfloat16), 'tensor', scatter_di...]
    ppermute x0 -> x15, starting transfers between devices: none -> 52.3 us  [the longest x3 9.89 us: moved(): lax.ppermute(added(d).astype(jnp.bfloat16), 'x', shift).astype(jnp.float32)]
    ppermute x0 -> x15, waiting for transfers between devices: none -> 46.4 us  [the longest x2 22.4 us: local(): swapped = [lax.ppermute(v, 'p', flip(ZP)) for v in jnp.split(own, 2)]]
    dot_general x3 -> x0, matrix products: 15.8 us -> none  [the longest x1 9.22 us: local(): jnp.dot(gathered, query_key_value_weight, preferred_element_type=jnp.floa...]
    pallas_call x0 -> x3, Pallas kernels: none -> 9.74 us  [the longest x1 6.75 us: partials(): pl.pallas_call(project, out_shape=(out, out), grid_spec=pltpu.PrefetchSca...]
  transfers between devices with their start and end apart: 3 -> 16, of which waited for: 3 -> 11; matrix products, arithmetic and copies ran while one was open for 3% -> 7% of each run, Pallas kernels for 0% -> 2%
where the time goes in v3:
time: 140 us; the launch traced here: 139 us
  starting transfers between devices  52.3 us (37%)
  waiting for transfers between devices  49 us (35%)
  between operations  13.7 us (10%)
  local copies, waits for them, and re-layouts  13.2 us (9%)
  Pallas kernels  9.74 us (7%)
    ppermute x2, waiting for transfers between devices, local(): swapped = [lax.ppermute(v, 'p', flip(ZP)) for v in jnp.split(own, 2)]  22.4 us
    ppermute x3, starting transfers between devices, moved(): lax.ppermute(added(d).astype(jnp.bfloat16), 'x', shift).astype(jnp.float32)  9.89 us
    ppermute x2, starting transfers between devices, local(): swapped = [lax.ppermute(v, 'p', flip(ZP)) for v in jnp.split(own, 2)]  9.67 us
    pallas_call x1, Pallas kernels, partials(): pl.pallas_call(project, out_shape=(out, out), grid_spec=pltpu.PrefetchSca...  6.75 us
    ppermute x1, starting transfers between devices, local(): near = lax.ppermute(here, ('p', 'zh', 'c'), swap)  6.08 us
    ppermute x3, waiting for transfers between devices, moved(): lax.ppermute(added(d).astype(jnp.bfloat16), 'x', shift).astype(jnp.float32)  5.99 us
    ppermute x2, starting transfers between devices, local(): swapped_pair = [lax.ppermute(v, 'x', flip(X)) for v in swapped]  5.61 us
    gather x4, local copies, waits for them, and re-layouts, taken(): return table[adapters(i, j)].reshape(-1, table.shape[2])  5.61 us
  transfers between devices with their start and end apart: 16, of which 11 were waited for; matrix products, arithmetic and copies ran while one was open for 7% of the time, Pallas kernels for 2%

profile of v3, /device:TPU:1, one launch (start us, length us, event | category | flops | bytes accessed | tf_op | source)
XLA Modules:
  0.0 139.2 jit_solution(18429046306375255604)
XLA Ops:
  6.5 1.7 %collective-permute-start = (bf16[128,1024]{1,0:T(8,128)(2,1)}, bf16[128,1024]{1,0:T(8,128)(2,1)S(1)}, u32[]{:S(2)}, u32[]{:S(2)}) collective-permute-start(bf16[128,1024]{1,0:T(8,128)(2,1)} %param.5), channel_id=1, source_target_pairs={{0,0},{4,16},{8,8},{12,24},{16,4},{20,20},{24,12},{28,28},{1,1},{5... | collective-permute-start | bytes 786440 | tf_op jit(solution)/shard_map/ppermute | solution.py:187
  8.3 5.4 %collective-permute-start.1 = (bf16[128,1024]{1,0:T(8,128)(2,1)}, bf16[128,1024]{1,0:T(8,128)(2,1)S(1)}, u32[]{:S(2)}, u32[]{:S(2)}) collective-permute-start(bf16[128,1024]{1,0:T(8,128)(2,1)} %param.5), channel_id=1, source_target_pairs={{0,16},{4,0},{8,24},{12,8},{16,20},{20,4},{24,28},{28,12},{1,17},{... | collective-permute-start | bytes 786440 | tf_op jit(solution)/shard_map/ppermute | solution.py:190
  13.7 4.8 %collective-permute-done.1.second = bf16[128,1024]{1,0:T(8,128)(2,1)S(1)} collective-permute-done((bf16[128,1024]{1,0:T(8,128)(2,1)}, bf16[128,1024]{1,0:T(8,128)(2,1)S(1)}, u32[]{:S(2)}, u32[]{:S(2)}) %collective-permute-start.1) | collective-permute-done | bytes 262176 | tf_op jit(solution)/shard_map/ppermute | solution.py:190
  19.4 2.1 %fusion.11 = (bf16[512,384]{1,0:T(8,128)(2,1)}, bf16[512,384]{1,0:T(8,128)(2,1)}) fusion(bf16[1024,384]{1,0:T(8,128)(2,1)} %refs_0_.1), kind=kLoop, calls=%fused_computation.37 | loop fusion | bytes 1572864 | tf_op jit(solution)/shard_map/split | solution.py:210
  21.6 7.7 %collective-permute-start.2 = (bf16[512,384]{1,0:T(8,128)(2,1)}, bf16[512,384]{1,0:T(8,128)(2,1)S(1)}, u32[]{:S(2)}, u32[]{:S(2)}) collective-permute-start(bf16[512,384]{1,0:T(8,128)(2,1)} %get-tuple-element.16), channel_id=1, source_target_pairs={{0,32},{32,0},{1,33},{33,1},{2,34},{34,2},{3,35},{35,3},{4,36},{36... | collective-permute-start | bytes 1179656 | tf_op jit(solution)/shard_map/ppermute | solution.py:210
  29.3 1.9 %collective-permute-start.3 = (bf16[512,384]{1,0:T(8,128)(2,1)}, bf16[512,384]{1,0:T(8,128)(2,1)}, u32[]{:S(2)}, u32[]{:S(2)}) collective-permute-start(bf16[512,384]{1,0:T(8,128)(2,1)} %get-tuple-element.15), channel_id=1, source_target_pairs={{0,32},{32,0},{1,33},{33,1},{2,34},{34,2},{3,35},{35,3},{4,36},{36... | collective-permute-start | bytes 1179656 | tf_op jit(solution)/shard_map/ppermute | solution.py:210
  31.2 3.0 %collective-permute-start.4 = (bf16[1024,384]{1,0:T(8,128)(2,1)}, bf16[1024,384]{1,0:T(8,128)(2,1)S(1)}, u32[]{:S(2)}, u32[]{:S(2)}) collective-permute-start(bf16[1024,384]{1,0:T(8,128)(2,1)} %refs_0_.1), channel_id=1, source_target_pairs={{0,4},{4,0},{8,12},{12,8},{1,5},{5,1},{9,13},{13,9},{2,6},{6,2},{1... | collective-permute-start | bytes 2359304 | tf_op jit(solution)/shard_map/ppermute | solution.py:209
  37.0 2.2 %collective-permute-start.8 = (bf16[128,1024]{1,0:T(8,128)(2,1)}, bf16[128,1024]{1,0:T(8,128)(2,1)}, u32[]{:S(2)}, u32[]{:S(2)}) collective-permute-start(bf16[128,1024]{1,0:T(8,128)(2,1)} %bitcast.10), channel_id=1, source_target_pairs={{0,4},{4,0},{8,12},{12,8},{1,5},{5,1},{9,13},{13,9},{2,6},{6,2},{1... | collective-permute-start | bytes 786440 | tf_op jit(solution)/shard_map/ppermute | solution.py:204
  39.2 16.8 %collective-permute-done.2.refs_1_ = bf16[512,384]{1,0:T(8,128)(2,1)S(1)} collective-permute-done((bf16[512,384]{1,0:T(8,128)(2,1)}, bf16[512,384]{1,0:T(8,128)(2,1)S(1)}, u32[]{:S(2)}, u32[]{:S(2)}) %collective-permute-start.2) | collective-permute-done | bytes 393248 | tf_op jit(solution)/shard_map/ppermute | solution.py:210
  56.0 2.8 %collective-permute-start.5 = (bf16[512,384]{1,0:T(8,128)(2,1)S(1)}, bf16[512,384]{1,0:T(8,128)(2,1)}, u32[]{:S(2)}, u32[]{:S(2)}) collective-permute-start(bf16[512,384]{1,0:T(8,128)(2,1)S(1)} %collective-permute-done.2.refs_1_), channel_id=1, source_target_pairs={{0,4},{4,0},{8,12},{12,8},{1,5},{5,1},{9,13},{13,9},{2,6},{6,2},{1... | collective-permute-start | bytes 1179656 | tf_op jit(solution)/shard_map/ppermute | solution.py:211
  58.8 5.6 %collective-permute-done.3.refs_2_ = bf16[512,384]{1,0:T(8,128)(2,1)} collective-permute-done((bf16[512,384]{1,0:T(8,128)(2,1)}, bf16[512,384]{1,0:T(8,128)(2,1)}, u32[]{:S(2)}, u32[]{:S(2)}) %collective-permute-start.3) | collective-permute-done | bytes 393248 | tf_op jit(solution)/shard_map/ppermute | solution.py:210
  64.4 2.8 %collective-permute-start.6 = (bf16[512,384]{1,0:T(8,128)(2,1)}, bf16[512,384]{1,0:T(8,128)(2,1)}, u32[]{:S(2)}, u32[]{:S(2)}) collective-permute-start(bf16[512,384]{1,0:T(8,128)(2,1)} %collective-permute-done.3.refs_2_), channel_id=1, source_target_pairs={{0,4},{4,0},{8,12},{12,8},{1,5},{5,1},{9,13},{13,9},{2,6},{6,2},{1... | collective-permute-start | bytes 1179656 | tf_op jit(solution)/shard_map/ppermute | solution.py:211
  67.3 2.2 %gather_fusion.1 = bf16[8,16,384]{2,1,0:T(8,128)(2,1)} fusion(bf16[32,16,384]{2,1,0:T(8,128)(2,1)} %param.8, s32[1024]{0:T(1024)S(1)} %pad_clamp_fusion.1), kind=kCustom, calls=%fused_computation.1 | custom fusion | bytes 196640 | tf_op jit(solution)/shard_map/gather | solution.py:201
  69.5 1.9 %collective-permute-start.7 = (bf16[128,384]{1,0:T(8,128)(2,1)}, bf16[128,384]{1,0:T(8,128)(2,1)S(1)}, u32[]{:S(2)}, u32[]{:S(2)}) collective-permute-start(bf16[128,384]{1,0:T(8,128)(2,1)} %bitcast.7), channel_id=1, source_target_pairs={{0,32},{32,0},{1,33},{33,1},{2,34},{34,2},{3,35},{35,3},{4,36},{36... | collective-permute-start | bytes 294920 | tf_op jit(solution)/shard_map/ppermute | solution.py:206
  72.0 1.6 %gather_fusion = bf16[8,16,384]{2,1,0:T(8,128)(2,1)S(1)} fusion(bf16[32,16,384]{2,1,0:T(8,128)(2,1)} %param.8, s32[1024]{0:T(1024)S(1)} %pad_clamp_fusion.2), kind=kCustom, calls=%fused_computation | custom fusion | bytes 196640 | tf_op jit(solution)/shard_map/gather | solution.py:201
  73.6 2.7 %collective-permute-done.7.refs_7_ = bf16[128,384]{1,0:T(8,128)(2,1)S(1)} collective-permute-done((bf16[128,384]{1,0:T(8,128)(2,1)}, bf16[128,384]{1,0:T(8,128)(2,1)S(1)}, u32[]{:S(2)}, u32[]{:S(2)}) %collective-permute-start.7) | collective-permute-done | bytes 98336 | tf_op jit(solution)/shard_map/ppermute | solution.py:206
  76.8 2.2 %shard_map.56.table = bf16[2688,768]{1,0:T(8,128)(2,1)S(1)} custom-call(s32[2]{0:T(128)S(1)} %pad_add_fusion.slots, bf16[1024,384]{1,0:T(8,128)(2,1)S(1)} %copy-done.3, bf16[512,384]{1,0:T(8,128)(2,1)S(1)} %collective-permute-done.2.refs_1_, bf16[512,384]{1,0:T(8,128)(2,1)} %collective-permute-done.3.refs_2_, ...), custom_call_target="tpu_custom_call" | custom-call | tf_op jit(solution)/shard_map/pallas_call | solution.py:82
  79.0 1.9 %copy-done.1 = bf16[2688,768]{1,0:T(8,128)(2,1)} copy-done((bf16[2688,768]{1,0:T(8,128)(2,1)}, bf16[2688,768]{1,0:T(8,128)(2,1)S(1)}, u32[]{:S(2)}) %copy-start.1) | copy-done | bytes 4128792
  81.0 2.6 %all-gather.3.cloned.1.call-done = bf16[1024,2048]{1,0:T(8,128)(2,1)} async-done(((bf16[128,2048]{1,0:T(8,128)(2,1)}), bf16[1024,2048]{1,0:T(8,128)(2,1)}) %all-gather.3.cloned.1.call-update) | async-done | bytes 4194320 | tf_op jit(solution)/shard_map/all_gather | solution.py:193
  83.6 2.2 %copy-done.2 = bf16[2688,768]{1,0:T(8,128)(2,1)S(1)} copy-done((bf16[2688,768]{1,0:T(8,128)(2,1)S(1)}, bf16[2688,768]{1,0:T(8,128)(2,1)}, u32[]{:S(2)}) %copy-start.2) | copy-done | bytes 4128792
  85.7 6.7 %shard_map.57 = (bf16[4,256,384]{2,1,0:T(8,128)(2,1)S(1)}, bf16[4,256,384]{2,1,0:T(8,128)(2,1)S(1)}) custom-call(s32[1]{0:T(128)} %bitcast.order, bf16[8,128,2048]{2,1,0:T(8,128)(2,1)} %bitcast.55, bf16[2688,768]{1,0:T(8,128)(2,1)S(1)} %copy-done.2), custom_call_target="tpu_custom_call" | custom-call | flops 3221225472 | bytes 9895936 | tf_op jit(solution)/shard_map/pallas_call | solution.py:145
  92.5 2.6 %collective-permute-start.9 = (bf16[4,256,384]{2,1,0:T(8,128)(2,1)S(1)}, bf16[4,256,384]{2,1,0:T(8,128)(2,1)S(1)}, u32[]{:S(2)}, u32[]{:S(2)}) collective-permute-start(bf16[4,256,384]{2,1,0:T(8,128)(2,1)S(1)} %get-tuple-element.8), channel_id=1, source_target_pairs={{0,1},{1,0},{2,3},{3,2},{4,5},{5,4},{6,7},{7,6},{8,9},{9,8},{10,11... | collective-permute-start | bytes 2359304 | tf_op jit(solution)/shard_map/ppermute | solution.py:218
  95.1 1.9 %collective-permute-done.9 = bf16[4,256,384]{2,1,0:T(8,128)(2,1)S(1)} collective-permute-done((bf16[4,256,384]{2,1,0:T(8,128)(2,1)S(1)}, bf16[4,256,384]{2,1,0:T(8,128)(2,1)S(1)}, u32[]{:S(2)}, u32[]{:S(2)}) %collective-permute-start.9) | collective-permute-done | bytes 786464 | tf_op jit(solution)/shard_map/ppermute | solution.py:218
  97.1 4.6 %collective-permute-start.10 = (bf16[256,384]{1,0:T(8,128)(2,1)S(1)}, bf16[256,384]{1,0:T(8,128)(2,1)S(1)}, u32[]{:S(2)}, u32[]{:S(2)}) collective-permute-start(bf16[256,384]{1,0:T(8,128)(2,1)S(1)} %get-tuple-element.12), channel_id=1, source_target_pairs={{0,8},{4,12},{8,0},{12,4},{1,9},{5,13},{9,1},{13,5},{2,10},{6,14},... | collective-permute-start | bytes 589832 | tf_op jit(solution)/shard_map/ppermute | solution.py:225
  101.7 2.8 %collective-permute-start.11 = (bf16[256,384]{1,0:T(8,128)(2,1)S(1)}, bf16[256,384]{1,0:T(8,128)(2,1)S(1)}, u32[]{:S(2)}, u32[]{:S(2)}) collective-permute-start(bf16[256,384]{1,0:T(8,128)(2,1)S(1)} %get-tuple-element.14), channel_id=1, source_target_pairs={{0,12},{4,0},{8,4},{12,8},{1,13},{5,1},{9,5},{13,9},{2,14},{6,2},{... | collective-permute-start | bytes 589832 | tf_op jit(solution)/shard_map/ppermute | solution.py:225
  104.5 2.5 %collective-permute-start.12 = (bf16[256,384]{1,0:T(8,128)(2,1)S(1)}, bf16[256,384]{1,0:T(8,128)(2,1)S(1)}, u32[]{:S(2)}, u32[]{:S(2)}) collective-permute-start(bf16[256,384]{1,0:T(8,128)(2,1)S(1)} %get-tuple-element.13), channel_id=1, source_target_pairs={{0,4},{4,8},{8,12},{12,0},{1,5},{5,9},{9,13},{13,1},{2,6},{6,10},{... | collective-permute-start | bytes 589832 | tf_op jit(solution)/shard_map/ppermute | solution.py:225
  107.1 3.7 %collective-permute-done.11 = bf16[256,384]{1,0:T(8,128)(2,1)S(1)} collective-permute-done((bf16[256,384]{1,0:T(8,128)(2,1)S(1)}, bf16[256,384]{1,0:T(8,128)(2,1)S(1)}, u32[]{:S(2)}, u32[]{:S(2)}) %collective-permute-start.11) | collective-permute-done | bytes 196640 | tf_op jit(solution)/shard_map/ppermute | solution.py:225
  110.9 2.3 %collective-permute-done.12 = bf16[256,384]{1,0:T(8,128)(2,1)S(1)} collective-permute-done((bf16[256,384]{1,0:T(8,128)(2,1)S(1)}, bf16[256,384]{1,0:T(8,128)(2,1)S(1)}, u32[]{:S(2)}, u32[]{:S(2)}) %collective-permute-start.12) | collective-permute-done | bytes 196640 | tf_op jit(solution)/shard_map/ppermute | solution.py:225
  113.3 6.1 %collective-permute-start.13 = (bf16[2,128,384]{2,1,0:T(8,128)(2,1)S(1)}, bf16[2,128,384]{2,1,0:T(8,128)(2,1)S(1)}, u32[]{:S(2)}, u32[]{:S(2)}) collective-permute-start(bf16[2,128,384]{2,1,0:T(8,128)(2,1)S(1)} %fusion.7), channel_id=1, source_target_pairs={{0,0},{1,32},{2,2},{3,34},{32,1},{33,33},{34,3},{35,35},{4,4},{5,3... | collective-permute-start | bytes 589832 | tf_op jit(solution)/shard_map/ppermute | solution.py:238
  119.4 4.1 %collective-permute-start.14 = (bf16[2,128,384]{2,1,0:T(8,128)(2,1)S(1)}, bf16[2,128,384]{2,1,0:T(8,128)(2,1)S(1)}, u32[]{:S(2)}, u32[]{:S(2)}) collective-permute-start(bf16[2,128,384]{2,1,0:T(8,128)(2,1)S(1)} %fusion.2), channel_id=1, source_target_pairs={{0,2},{1,34},{2,0},{3,32},{32,3},{33,35},{34,1},{35,33},{4,6},{5,3... | collective-permute-start | bytes 589832 | tf_op jit(solution)/shard_map/ppermute | solution.py:237
  123.5 4.5 %collective-permute-done.13 = bf16[2,128,384]{2,1,0:T(8,128)(2,1)S(1)} collective-permute-done((bf16[2,128,384]{2,1,0:T(8,128)(2,1)S(1)}, bf16[2,128,384]{2,1,0:T(8,128)(2,1)S(1)}, u32[]{:S(2)}, u32[]{:S(2)}) %collective-permute-start.13) | collective-permute-done | bytes 196640 | tf_op jit(solution)/shard_map/ppermute | solution.py:238
  127.9 3.6 %collective-permute-done.14 = bf16[2,128,384]{2,1,0:T(8,128)(2,1)S(1)} collective-permute-done((bf16[2,128,384]{2,1,0:T(8,128)(2,1)S(1)}, bf16[2,128,384]{2,1,0:T(8,128)(2,1)S(1)}, u32[]{:S(2)}, u32[]{:S(2)}) %collective-permute-start.14) | collective-permute-done | bytes 196640 | tf_op jit(solution)/shard_map/ppermute | solution.py:237
  (32 shorter events, 5.8 us)
Async XLA Ops:
  6.5 29.2 %copy-start = (bf16[32,16,1024]{2,1,0:T(8,128)(2,1)S(1)}, bf16[32,16,1024]{2,1,0:T(8,128)(2,1)}, u32[]{:S(2)}) copy-start(bf16[32,16,1024]{2,1,0:T(8,128)(2,1)} %param.7) | copy-start | bytes 3145732
  6.5 70.3 %copy-start.3 = (bf16[1024,384]{1,0:T(8,128)(2,1)S(1)}, bf16[1024,384]{1,0:T(8,128)(2,1)}, u32[]{:S(2)}) copy-start(bf16[1024,384]{1,0:T(8,128)(2,1)} %refs_0_.1) | copy-start | bytes 2359300
  6.5 77.0 %all-gather.3.cloned.1.call-start = ((), (), s32[]{:S(2)}) async-start(), calls=%async_computation | async-start | bytes 4718592 | tf_op jit(solution)/shard_map/all_gather | solution.py:193
  6.5 7.2 %collective-permute-start = (bf16[128,1024]{1,0:T(8,128)(2,1)}, bf16[128,1024]{1,0:T(8,128)(2,1)S(1)}, u32[]{:S(2)}, u32[]{:S(2)}) collective-permute-start(bf16[128,1024]{1,0:T(8,128)(2,1)} %param.5), channel_id=1, source_target_pairs={{0,0},{4,16},{8,8},{12,24},{16,4},{20,20},{24,12},{28,28},{1,1},{5... | collective-permute-start | bytes 786440 | tf_op jit(solution)/shard_map/ppermute | solution.py:187
  8.3 10.3 %collective-permute-start.1 = (bf16[128,1024]{1,0:T(8,128)(2,1)}, bf16[128,1024]{1,0:T(8,128)(2,1)S(1)}, u32[]{:S(2)}, u32[]{:S(2)}) collective-permute-start(bf16[128,1024]{1,0:T(8,128)(2,1)} %param.5), channel_id=1, source_target_pairs={{0,16},{4,0},{8,24},{12,8},{16,20},{20,4},{24,28},{28,12},{1,17},{... | collective-permute-start | bytes 786440 | tf_op jit(solution)/shard_map/ppermute | solution.py:190
  21.6 34.5 %collective-permute-start.2 = (bf16[512,384]{1,0:T(8,128)(2,1)}, bf16[512,384]{1,0:T(8,128)(2,1)S(1)}, u32[]{:S(2)}, u32[]{:S(2)}) collective-permute-start(bf16[512,384]{1,0:T(8,128)(2,1)} %get-tuple-element.16), channel_id=1, source_target_pairs={{0,32},{32,0},{1,33},{33,1},{2,34},{34,2},{3,35},{35,3},{4,36},{36... | collective-permute-start | bytes 1179656 | tf_op jit(solution)/shard_map/ppermute | solution.py:210
  29.3 35.1 %collective-permute-start.3 = (bf16[512,384]{1,0:T(8,128)(2,1)}, bf16[512,384]{1,0:T(8,128)(2,1)}, u32[]{:S(2)}, u32[]{:S(2)}) collective-permute-start(bf16[512,384]{1,0:T(8,128)(2,1)} %get-tuple-element.15), channel_id=1, source_target_pairs={{0,32},{32,0},{1,33},{33,1},{2,34},{34,2},{3,35},{35,3},{4,36},{36... | collective-permute-start | bytes 1179656 | tf_op jit(solution)/shard_map/ppermute | solution.py:210
  31.2 45.6 %collective-permute-start.4 = (bf16[1024,384]{1,0:T(8,128)(2,1)}, bf16[1024,384]{1,0:T(8,128)(2,1)S(1)}, u32[]{:S(2)}, u32[]{:S(2)}) collective-permute-start(bf16[1024,384]{1,0:T(8,128)(2,1)} %refs_0_.1), channel_id=1, source_target_pairs={{0,4},{4,0},{8,12},{12,8},{1,5},{5,1},{9,13},{13,9},{2,6},{6,2},{1... | collective-permute-start | bytes 2359304 | tf_op jit(solution)/shard_map/ppermute | solution.py:209
  37.0 39.4 %collective-permute-start.8 = (bf16[128,1024]{1,0:T(8,128)(2,1)}, bf16[128,1024]{1,0:T(8,128)(2,1)}, u32[]{:S(2)}, u32[]{:S(2)}) collective-permute-start(bf16[128,1024]{1,0:T(8,128)(2,1)} %bitcast.10), channel_id=1, source_target_pairs={{0,4},{4,0},{8,12},{12,8},{1,5},{5,1},{9,13},{13,9},{2,6},{6,2},{1... | collective-permute-start | bytes 786440 | tf_op jit(solution)/shard_map/ppermute | solution.py:204
  56.0 20.3 %collective-permute-start.5 = (bf16[512,384]{1,0:T(8,128)(2,1)S(1)}, bf16[512,384]{1,0:T(8,128)(2,1)}, u32[]{:S(2)}, u32[]{:S(2)}) collective-permute-start(bf16[512,384]{1,0:T(8,128)(2,1)S(1)} %collective-permute-done.2.refs_1_), channel_id=1, source_target_pairs={{0,4},{4,0},{8,12},{12,8},{1,5},{5,1},{9,13},{13,9},{2,6},{6,2},{1... | collective-permute-start | bytes 1179656 | tf_op jit(solution)/shard_map/ppermute | solution.py:211
  64.4 12.4 %collective-permute-start.6 = (bf16[512,384]{1,0:T(8,128)(2,1)}, bf16[512,384]{1,0:T(8,128)(2,1)}, u32[]{:S(2)}, u32[]{:S(2)}) collective-permute-start(bf16[512,384]{1,0:T(8,128)(2,1)} %collective-permute-done.3.refs_2_), channel_id=1, source_target_pairs={{0,4},{4,0},{8,12},{12,8},{1,5},{5,1},{9,13},{13,9},{2,6},{6,2},{1... | collective-permute-start | bytes 1179656 | tf_op jit(solution)/shard_map/ppermute | solution.py:211
  69.5 6.9 %collective-permute-start.7 = (bf16[128,384]{1,0:T(8,128)(2,1)}, bf16[128,384]{1,0:T(8,128)(2,1)S(1)}, u32[]{:S(2)}, u32[]{:S(2)}) collective-permute-start(bf16[128,384]{1,0:T(8,128)(2,1)} %bitcast.7), channel_id=1, source_target_pairs={{0,32},{32,0},{1,33},{33,1},{2,34},{34,2},{3,35},{35,3},{4,36},{36... | collective-permute-start | bytes 294920 | tf_op jit(solution)/shard_map/ppermute | solution.py:206
  79.0 2.0 %copy-start.1 = (bf16[2688,768]{1,0:T(8,128)(2,1)}, bf16[2688,768]{1,0:T(8,128)(2,1)S(1)}, u32[]{:S(2)}) copy-start(bf16[2688,768]{1,0:T(8,128)(2,1)S(1)} %shard_map.56.table) | copy-start | bytes 12386308
  83.6 2.2 %copy-start.2 = (bf16[2688,768]{1,0:T(8,128)(2,1)S(1)}, bf16[2688,768]{1,0:T(8,128)(2,1)}, u32[]{:S(2)}) copy-start(bf16[2688,768]{1,0:T(8,128)(2,1)} %copy-done.1) | copy-start | bytes 12386308
  92.5 4.5 %collective-permute-start.9 = (bf16[4,256,384]{2,1,0:T(8,128)(2,1)S(1)}, bf16[4,256,384]{2,1,0:T(8,128)(2,1)S(1)}, u32[]{:S(2)}, u32[]{:S(2)}) collective-permute-start(bf16[4,256,384]{2,1,0:T(8,128)(2,1)S(1)} %get-tuple-element.8), channel_id=1, source_target_pairs={{0,1},{1,0},{2,3},{3,2},{4,5},{5,4},{6,7},{7,6},{8,9},{9,8},{10,11... | collective-permute-start | bytes 2359304 | tf_op jit(solution)/shard_map/ppermute | solution.py:218
  97.1 9.9 %collective-permute-start.10 = (bf16[256,384]{1,0:T(8,128)(2,1)S(1)}, bf16[256,384]{1,0:T(8,128)(2,1)S(1)}, u32[]{:S(2)}, u32[]{:S(2)}) collective-permute-start(bf16[256,384]{1,0:T(8,128)(2,1)S(1)} %get-tuple-element.12), channel_id=1, source_target_pairs={{0,8},{4,12},{8,0},{12,4},{1,9},{5,13},{9,1},{13,5},{2,10},{6,14},... | collective-permute-start | bytes 589832 | tf_op jit(solution)/shard_map/ppermute | solution.py:225
  101.7 9.1 %collective-permute-start.11 = (bf16[256,384]{1,0:T(8,128)(2,1)S(1)}, bf16[256,384]{1,0:T(8,128)(2,1)S(1)}, u32[]{:S(2)}, u32[]{:S(2)}) collective-permute-start(bf16[256,384]{1,0:T(8,128)(2,1)S(1)} %get-tuple-element.14), channel_id=1, source_target_pairs={{0,12},{4,0},{8,4},{12,8},{1,13},{5,1},{9,5},{13,9},{2,14},{6,2},{... | collective-permute-start | bytes 589832 | tf_op jit(solution)/shard_map/ppermute | solution.py:225
  104.5 8.6 %collective-permute-start.12 = (bf16[256,384]{1,0:T(8,128)(2,1)S(1)}, bf16[256,384]{1,0:T(8,128)(2,1)S(1)}, u32[]{:S(2)}, u32[]{:S(2)}) collective-permute-start(bf16[256,384]{1,0:T(8,128)(2,1)S(1)} %get-tuple-element.13), channel_id=1, source_target_pairs={{0,4},{4,8},{8,12},{12,0},{1,5},{5,9},{9,13},{13,1},{2,6},{6,10},{... | collective-permute-start | bytes 589832 | tf_op jit(solution)/shard_map/ppermute | solution.py:225
  113.3 14.7 %collective-permute-start.13 = (bf16[2,128,384]{2,1,0:T(8,128)(2,1)S(1)}, bf16[2,128,384]{2,1,0:T(8,128)(2,1)S(1)}, u32[]{:S(2)}, u32[]{:S(2)}) collective-permute-start(bf16[2,128,384]{2,1,0:T(8,128)(2,1)S(1)} %fusion.7), channel_id=1, source_target_pairs={{0,0},{1,32},{2,2},{3,34},{32,1},{33,33},{34,3},{35,35},{4,4},{5,3... | collective-permute-start | bytes 589832 | tf_op jit(solution)/shard_map/ppermute | solution.py:238
  119.4 12.2 %collective-permute-start.14 = (bf16[2,128,384]{2,1,0:T(8,128)(2,1)S(1)}, bf16[2,128,384]{2,1,0:T(8,128)(2,1)S(1)}, u32[]{:S(2)}, u32[]{:S(2)}) collective-permute-start(bf16[2,128,384]{2,1,0:T(8,128)(2,1)S(1)} %fusion.2), channel_id=1, source_target_pairs={{0,2},{1,34},{2,0},{3,32},{32,3},{33,35},{34,1},{35,33},{4,6},{5,3... | collective-permute-start | bytes 589832 | tf_op jit(solution)/shard_map/ppermute | solution.py:237
Sparse Core Ops, SparseCore 0:
  19.5 63.9 all-gather.2

commit v4 on v0

v4 whole, which is shorter than its diff:
```python
import functools

import jax
import jax.numpy as jnp
from jax import lax
from jax.experimental import pallas as pl
from jax.experimental.pallas import tpu as pltpu
from jax.sharding import Mesh, PartitionSpec as P

Y, ZP, ZQ, X, ZH, C = 8, 2, 2, 4, 2, 2
AXES = ("y", "p", "q", "x", "zh", "c")
DP, TENSOR = ("y", "p", "q"), ("x", "zh", "c")
GROUPS = Y // X
VMEM_BYTES = 16_000_000
PLACE_FLOPS = 10_000_000_000
OFFSETS = (0, -1, 1, -2, 2, -3, 3, 4)
VMEM = pl.BlockSpec(memory_space=pltpu.VMEM)
SMEM = pl.BlockSpec(memory_space=pltpu.SMEM)
ANY = pl.BlockSpec(memory_space=pl.ANY)
PARAMS = pltpu.CompilerParams(vmem_limit_bytes=VMEM_BYTES)


def flip(size):
    return [(i, i ^ 1) for i in range(size)]


def copied(moves):
    for move in moves:
        move.start()
    for move in moves:
        move.wait()


def block_of(where, i, p):
    return (i // ZQ) * ZP * ZQ + p * ZQ + (where[2] ^ (i % ZQ))


def join_rows(first, second, out):
    rows = first.shape[0]
    out[:rows] = first[...]
    out[rows:] = second[...]


def joined(first, second):
    rows, features = first.shape
    return pl.pallas_call(
        join_rows,
        out_shape=jax.ShapeDtypeStruct((2 * rows, features), first.dtype),
        in_specs=[VMEM] * 2,
        out_specs=VMEM,
        compiler_params=PARAMS,
    )(first, second)


def pick_up_rows(where, adapter, up, out, sems):
    rank = up.shape[1]
    copied(
        [
            pltpu.make_async_copy(
                up.at[adapter[block_of(where, i, 1 - where[1])]],
                out.at[pl.ds(i * rank, rank)],
                sems.at[i],
            )
            for i in range(Y * ZQ)
        ]
    )


def picked(where, adapter, up):
    rank, columns = up.shape[1:]
    return pl.pallas_call(
        pick_up_rows,
        out_shape=jax.ShapeDtypeStruct((Y * ZQ * rank, columns), up.dtype),
        in_specs=[SMEM, SMEM, ANY],
        out_specs=VMEM,
        scratch_shapes=[pltpu.SemaphoreType.DMA((Y * ZQ,))],
        compiler_params=PARAMS,
    )(where, adapter, up)


def place_table(where, adapter, down, up, first, *refs):
    swapped, (table, downs, sems) = refs[:-3], refs[-3:]
    features, columns = first.shape
    rank = up.shape[1]
    moves = []

    def move(source, target):
        moves.append(pltpu.make_async_copy(source, target, sems.at[len(moves)]))

    def part(row, rows, col):
        cols = pl.ds(pl.multiple_of(col * columns, 128), columns)
        return table.at[pl.ds(row, rows), cols]

    own, other = where[4], 1 - where[4]
    move(first, part(0, features, own))
    row = 0
    for v in swapped:
        move(v, part(row, v.shape[0], other))
        row += v.shape[0]
    for i in range(Y * ZQ):
        index = adapter[block_of(where, i, where[1])]
        move(up.at[index], part(features + i * rank, rank, own))
        move(down.at[index], downs.at[pl.ds(i * rank, rank)])
    copied(moves)


def placed(where, adapter, down, up, first, swapped):
    features, columns = first.shape
    ranks = Y * ZQ * up.shape[1]
    return pl.pallas_call(
        place_table,
        out_shape=(
            jax.ShapeDtypeStruct((features + ranks, 2 * columns), first.dtype),
            jax.ShapeDtypeStruct((ranks, features), first.dtype),
        ),
        in_specs=[SMEM] * 2 + [ANY] * (3 + len(swapped)),
        out_specs=(VMEM, VMEM),
        scratch_shapes=[pltpu.SemaphoreType.DMA((1 + len(swapped) + 2 * Y * ZQ,))],
        compiler_params=PARAMS,
        cost_estimate=pl.CostEstimate(
            flops=PLACE_FLOPS, bytes_accessed=4 * first.size, transcendentals=0
        ),
    )(where, adapter, down, up, first, *swapped)


def project(offsets, where, table, downs, *refs):
    count = len(offsets)
    chunks, (keep, send, held, made, fetches, stores) = refs[:count], refs[-6:]
    rows, features = chunks[0].shape
    ranks = downs.shape[0]
    columns = table.shape[1] // 2
    y, x = where[0], where[3]
    sources = [(y + offset + Y) % Y for offset in offsets]

    def fetch(i):
        at = held.at[i, :, pl.ds(0, features)]
        return pltpu.make_async_copy(chunks[i], at, fetches.at[i])

    def store(i, j, out):
        tile, group = (sources[i] // GROUPS - x + X) % X, sources[i] % GROUPS
        at = out.at[tile, pl.ds(pl.multiple_of(group * rows, rows), rows)]
        at = out if out.shape[0] == rows else at
        return pltpu.make_async_copy(made.at[i, j], at, stores.at[i, j])

    for i in range(count):
        fetch(i).start()
    block_rows = rows // ZQ
    rank = ranks // (Y * ZQ)
    for i in range(count):
        fetch(i).wait()
        shrink = lax.dot_general(
            held[i, :, :features],
            downs[...],
            (((1,), (1,)), ((), ())),
            preferred_element_type=jnp.float32,
        )
        block = lax.broadcasted_iota(jnp.int32, shrink.shape, 0) // block_rows
        adapter = lax.broadcasted_iota(jnp.int32, shrink.shape, 1) // rank
        low = jnp.where(block + sources[i] * ZQ == adapter, 0.5 * shrink, 0.0)
        held[i, :, features:] = low.astype(held.dtype)
        total = jnp.dot(held[i], table[...], preferred_element_type=jnp.float32)
        total = total.astype(made.dtype)
        for j, out in enumerate((keep, send)):
            made[i, j] = total[:, j * columns : (j + 1) * columns]
            store(i, j, out).start()
    for i in range(count):
        for j, out in enumerate((keep, send)):
            store(i, j, out).wait()


def partials(where, table, downs, offsets, chunks, keep=None):
    count, outs = len(chunks), [] if keep is None else [keep]
    rows, features = chunks[0].shape
    width, columns = table.shape[0], table.shape[1] // 2
    out = jax.ShapeDtypeStruct((X, GROUPS * rows, columns), table.dtype)
    last = jax.ShapeDtypeStruct((rows, columns), table.dtype)
    return pl.pallas_call(
        functools.partial(project, offsets),
        out_shape=(out, last if outs else out),
        in_specs=[SMEM, VMEM, VMEM] + [ANY] * (count + len(outs)),
        out_specs=(ANY, ANY),
        scratch_shapes=[
            pltpu.VMEM((count, rows, width), table.dtype),
            pltpu.VMEM((count, 2, rows, columns), table.dtype),
            pltpu.SemaphoreType.DMA((count,)),
            pltpu.SemaphoreType.DMA((count, 2)),
        ],
        input_output_aliases={3 + count: 0} if outs else {},
        compiler_params=PARAMS,
        cost_estimate=pl.CostEstimate(
            flops=4 * count * rows * width * columns,
            bytes_accessed=2 * count * rows * (features + 2 * columns) + 2 * table.size,
            transcendentals=0,
        ),
    )(where, table, downs, *chunks, *outs)


def local(
    tokens, query_key_value_weight, adapter_down_weight, adapter_up_weight, adapter_per_block
):
    y, p, q, x, zh, c = (lax.axis_index(a) for a in AXES)
    rows, features = tokens.shape
    columns = query_key_value_weight.shape[1]
    adapter, down, up = adapter_per_block, adapter_down_weight, adapter_up_weight
    where = jnp.stack([y, p, q, x, (c != p) * 1]).astype(jnp.int32)

    def over(axis, size, step):
        return lambda v: lax.ppermute(v, axis, [(i, (i + step) % size) for i in range(size)])

    def opposite(v):
        pairs = [(i, j) for i in range(Y) for j in range(C)]
        return lax.ppermute(
            v, ("y", "c"), [(i * C + j, (i + 1 - 2 * j) % Y * C + j) for i, j in pairs]
        )

    def step(operands, done=()):
        values = lax.optimization_barrier(tuple(v for _, v in operands) + tuple(done))
        return [f(v) for (f, _), v in zip(operands, values)]

    own = query_key_value_weight
    forward, back, to_p = over("y", Y, 1), over("y", Y, -1), over("p", ZP, 1)
    up_swapped = to_p(picked(where, adapter, up))
    chunk = joined(tokens, over("q", ZQ, 1)(tokens))
    swapped, up_1, down_1 = step([(to_p, own), (forward, chunk), (back, chunk)], [up_swapped])
    up_2, down_2 = step([(forward, up_1), (back, down_1)])
    up_3, down_3 = step([(forward, up_2), (back, down_2)])

    table, downs = placed(where, adapter, down, up, own, [swapped, up_swapped])
    up_3, down_3, table = lax.optimization_barrier((up_3, down_3, table))
    far_y = opposite(jnp.where(c == 0, up_3, down_3))
    chunks = [chunk, up_1, down_1, up_2, down_2, up_3, down_3]
    keep, send = partials(where, table, downs, OFFSETS[:-1], chunks)
    received = over("c", C, 1)(lax.optimization_barrier((send, far_y))[0])
    keep, last = partials(where, table, downs, OFFSETS[-1:], [far_y], keep)
    source = (y + Y // 2) % Y
    start = ((source // GROUPS - x + X) % X, source % GROUPS * ZQ * rows, 0)
    received = lax.dynamic_update_slice(received, over("c", C, 1)(last)[None], start)

    def added(d):
        return keep[d].astype(jnp.float32) + received[d].astype(jnp.float32)

    def moved(d):
        return over("x", X, d)(added(d).astype(jnp.bfloat16)).astype(jnp.float32)

    total = moved(1) + moved(3) + moved(2) + added(0)
    total = total.astype(jnp.bfloat16).reshape(ZH, ZQ * rows, columns)

    here = jnp.where(zh == 0, total[0], total[1])
    there = jnp.where(zh == 0, total[1], total[0])
    places = [(i, h, j) for i in range(ZP) for h in range(ZH) for j in range(C)]
    swap = [(i * 4 + h * 2 + j, j * 4 + h * 2 + i) for i, h, j in places]
    cross = [(i * 4 + h * 2 + j, j * 4 + (1 - h) * 2 + i) for i, h, j in places]
    far = lax.ppermute(there, ("p", "zh", "c"), cross)
    near = lax.ppermute(here, ("p", "zh", "c"), swap)
    out = near.astype(jnp.float32) + far.astype(jnp.float32)
    out = out.reshape(ZQ, rows, columns)
    out = jnp.where(q == 0, out, out[::-1])
    return out.reshape(ZQ * rows, columns).astype(jnp.bfloat16)


def solution(mesh):
    physical = Mesh(mesh.devices.reshape(Y, ZP, ZQ, X, ZH, C), AXES)
    return jax.shard_map(
        local,
        mesh=physical,
        in_specs=(
            P(DP, TENSOR),
            P(TENSOR, DP),
            P(None, None, TENSOR),
            P(None, None, DP),
            P(),
        ),
        out_specs=P(TENSOR, DP),
        check_vma=False,
    )
```

time: 514 us -> 146 us (0.28)
  waiting for transfers between devices: 479 us -> 50.8 us
  starting transfers between devices: 0.08 us -> 65.4 us
  matrix products: 15.8 us -> 0 us
  Pallas kernels: 0 us -> 15.4 us
  between operations: 13.2 us -> 0.36 us
    all_gather x1 -> x0, waiting for transfers between devices: 199 us -> none  [local(): gathered = lax.all_gather(tokens, 'dp', axis=0, tiled=True)]
    psum x1 -> x0, waiting for transfers between devices: 171 us -> none  [local(): lax.psum(shrink_part.astype(jnp.bfloat16), 'tensor').astype(jnp.float32)]
    reduce_scatter x1 -> x0, waiting for transfers between devices: 109 us -> none  [local(): lax.psum_scatter(partial_value.astype(jnp.bfloat16), 'tensor', scatter_di...]
    ppermute x0 -> x17, starting transfers between devices: none -> 65.4 us  [the longest x14 51.3 us: over(): lax.ppermute(v, axis, [(i, (i + step) % size) for i in range(size)])]
    ppermute x0 -> x17, waiting for transfers between devices: none -> 50.8 us  [the longest x14 45.3 us: over(): lax.ppermute(v, axis, [(i, (i + step) % size) for i in range(size)])]
    dot_general x3 -> x0, matrix products: 15.8 us -> none  [the longest x1 9.22 us: local(): jnp.dot(gathered, query_key_value_weight, preferred_element_type=jnp.floa...]
    pallas_call x0 -> x5, Pallas kernels: none -> 15.4 us  [the longest x2 12.4 us: partials(): pl.pallas_call(functools.partial(project, offsets), out_shape=(out, last...]
    unnamed x6 -> x22, local copies, waits for them, and re-layouts: 0.01 us -> 6.57 us
  transfers between devices with their start and end apart: 3 -> 17, of which waited for: 3 -> 13; matrix products, arithmetic and copies ran while one was open for 3% -> 0% of each run, Pallas kernels for 0% -> 11%
where the time goes in v4:
time: 146 us; the launch traced here: 144 us
  starting transfers between devices  65.4 us (45%)
  waiting for transfers between devices  50.8 us (35%)
  Pallas kernels  15.4 us (11%)
  local copies, waits for them, and re-layouts  7.35 us (5%)
  other arithmetic  4.38 us (3%)
    ppermute x14, starting transfers between devices, over(): lax.ppermute(v, axis, [(i, (i + step) % size) for i in range(size)])  51.3 us
    ppermute x14, waiting for transfers between devices, over(): lax.ppermute(v, axis, [(i, (i + step) % size) for i in range(size)])  45.3 us
    pallas_call x2, Pallas kernels, partials(): pl.pallas_call(functools.partial(project, offsets), out_shape=(out, last...  12.4 us
    unnamed x22, local copies, waits for them, and re-layouts  6.57 us
    ppermute x1, starting transfers between devices, local(): far = lax.ppermute(there, ('p', 'zh', 'c'), cross)  5.34 us
    ppermute x1, starting transfers between devices, local(): near = lax.ppermute(here, ('p', 'zh', 'c'), swap)  4.77 us
    ppermute x1, starting transfers between devices, opposite(): lax.ppermute(v, ('y', 'c'), [(i * C + j, (i + 1 - 2 * j) % Y * C + j) for...  3.99 us
    ppermute x1, waiting for transfers between devices, local(): near = lax.ppermute(here, ('p', 'zh', 'c'), swap)  3.25 us
  transfers between devices with their start and end apart: 17, of which 13 were waited for; matrix products, arithmetic and copies ran while one was open for 0% of the time, Pallas kernels for 11%

profile of v4, /device:TPU:1, one launch (start us, length us, event | category | flops | bytes accessed | tf_op | source)
XLA Modules:
  0.0 143.7 jit_solution(875525923621773798)
XLA Ops:
  0.0 5.0 %collective-permute-start = (bf16[128,1024]{1,0:T(8,128)(2,1)}, bf16[128,1024]{1,0:T(8,128)(2,1)S(1)}, u32[]{:S(2)}, u32[]{:S(2)}) collective-permute-start(bf16[128,1024]{1,0:T(8,128)(2,1)} %first.2), channel_id=1, source_target_pairs={{0,16},{16,0},{1,17},{17,1},{2,18},{18,2},{3,19},{19,3},{4,20},{20... | collective-permute-start | bytes 786440 | tf_op jit(solution)/shard_map/ppermute | solution.py:208
  7.7 5.8 %collective-permute-start.1 = (bf16[256,384]{1,0:T(8,128)(2,1)S(1)}, bf16[256,384]{1,0:T(8,128)(2,1)S(1)}, u32[]{:S(2)}, u32[]{:S(2)}) collective-permute-start(bf16[256,384]{1,0:T(8,128)(2,1)S(1)} %shard_map.56), channel_id=1, source_target_pairs={{0,32},{32,0},{1,33},{33,1},{2,34},{34,2},{3,35},{35,3},{4,36},{36... | collective-permute-start | bytes 589832 | tf_op jit(solution)/shard_map/ppermute | solution.py:208
  14.5 7.6 %collective-permute-done.1.refs_1_ = bf16[256,384]{1,0:T(8,128)(2,1)S(1)} collective-permute-done((bf16[256,384]{1,0:T(8,128)(2,1)S(1)}, bf16[256,384]{1,0:T(8,128)(2,1)S(1)}, u32[]{:S(2)}, u32[]{:S(2)}) %collective-permute-start.1) | collective-permute-done | bytes 196640 | tf_op jit(solution)/shard_map/ppermute | solution.py:208
  22.8 3.6 %collective-permute-start.2 = (bf16[256,1024]{1,0:T(8,128)(2,1)S(1)}, bf16[256,1024]{1,0:T(8,128)(2,1)S(1)}, u32[]{:S(2)}, u32[]{:S(2)}) collective-permute-start(bf16[256,1024]{1,0:T(8,128)(2,1)S(1)} %shard_map.55.refs_0_), channel_id=1, source_target_pairs={{0,64},{64,128},{128,192},{192,256},{256,320},{320,384},{384,448},... | collective-permute-start | bytes 1572872 | tf_op jit(solution)/shard_map/ppermute | solution.py:208
  26.5 3.8 %collective-permute-start.3 = (bf16[256,1024]{1,0:T(8,128)(2,1)S(1)}, bf16[256,1024]{1,0:T(8,128)(2,1)S(1)}, u32[]{:S(2)}, u32[]{:S(2)}) collective-permute-start(bf16[256,1024]{1,0:T(8,128)(2,1)S(1)} %shard_map.55.refs_0_), channel_id=1, source_target_pairs={{0,448},{64,0},{128,64},{192,128},{256,192},{320,256},{384,320},{4... | collective-permute-start | bytes 1572872 | tf_op jit(solution)/shard_map/ppermute | solution.py:208
  30.3 1.9 %collective-permute-start.8 = (bf16[1024,384]{1,0:T(8,128)(2,1)}, bf16[1024,384]{1,0:T(8,128)(2,1)S(1)}, u32[]{:S(2)}, u32[]{:S(2)}) collective-permute-start(bf16[1024,384]{1,0:T(8,128)(2,1)} %first.3), channel_id=1, source_target_pairs={{0,32},{32,0},{1,33},{33,1},{2,34},{34,2},{3,35},{35,3},{4,36},{36... | collective-permute-start | bytes 2359304 | tf_op jit(solution)/shard_map/ppermute | solution.py:208
  32.2 7.4 %collective-permute-done.2.refs_1_ = bf16[256,1024]{1,0:T(8,128)(2,1)S(1)} collective-permute-done((bf16[256,1024]{1,0:T(8,128)(2,1)S(1)}, bf16[256,1024]{1,0:T(8,128)(2,1)S(1)}, u32[]{:S(2)}, u32[]{:S(2)}) %collective-permute-start.2) | collective-permute-done | bytes 524320 | tf_op jit(solution)/shard_map/ppermute | solution.py:208
  40.5 3.2 %collective-permute-start.4 = (bf16[256,1024]{1,0:T(8,128)(2,1)S(1)}, bf16[256,1024]{1,0:T(8,128)(2,1)}, u32[]{:S(2)}, u32[]{:S(2)}) collective-permute-start(bf16[256,1024]{1,0:T(8,128)(2,1)S(1)} %collective-permute-done.2.refs_1_), channel_id=1, source_target_pairs={{0,64},{64,128},{128,192},{192,256},{256,320},{320,384},{384,448},... | collective-permute-start | bytes 1572872 | tf_op jit(solution)/shard_map/ppermute | solution.py:208
  43.7 4.0 %collective-permute-start.5 = (bf16[256,1024]{1,0:T(8,128)(2,1)S(1)}, bf16[256,1024]{1,0:T(8,128)(2,1)}, u32[]{:S(2)}, u32[]{:S(2)}) collective-permute-start(bf16[256,1024]{1,0:T(8,128)(2,1)S(1)} %collective-permute-done.3.refs_2_), channel_id=1, source_target_pairs={{0,448},{64,0},{128,64},{192,128},{256,192},{320,256},{384,320},{4... | collective-permute-start | bytes 1572872 | tf_op jit(solution)/shard_map/ppermute | solution.py:208
  47.8 8.5 %collective-permute-done.4.refs_3_ = bf16[256,1024]{1,0:T(8,128)(2,1)} collective-permute-done((bf16[256,1024]{1,0:T(8,128)(2,1)S(1)}, bf16[256,1024]{1,0:T(8,128)(2,1)}, u32[]{:S(2)}, u32[]{:S(2)}) %collective-permute-start.4) | collective-permute-done | bytes 524320 | tf_op jit(solution)/shard_map/ppermute | solution.py:208
  56.2 2.2 %collective-permute-done.5.refs_4_ = bf16[256,1024]{1,0:T(8,128)(2,1)} collective-permute-done((bf16[256,1024]{1,0:T(8,128)(2,1)S(1)}, bf16[256,1024]{1,0:T(8,128)(2,1)}, u32[]{:S(2)}, u32[]{:S(2)}) %collective-permute-start.5) | collective-permute-done | bytes 524320 | tf_op jit(solution)/shard_map/ppermute | solution.py:208
  58.4 4.0 %collective-permute-start.6 = (bf16[256,1024]{1,0:T(8,128)(2,1)}, bf16[256,1024]{1,0:T(8,128)(2,1)S(1)}, u32[]{:S(2)}, u32[]{:S(2)}) collective-permute-start(bf16[256,1024]{1,0:T(8,128)(2,1)} %collective-permute-done.4.refs_3_), channel_id=1, source_target_pairs={{0,64},{64,128},{128,192},{192,256},{256,320},{320,384},{384,448},... | collective-permute-start | bytes 1572872 | tf_op jit(solution)/shard_map/ppermute | solution.py:208
  62.4 2.5 %collective-permute-start.7 = (bf16[256,1024]{1,0:T(8,128)(2,1)}, bf16[256,1024]{1,0:T(8,128)(2,1)S(1)}, u32[]{:S(2)}, u32[]{:S(2)}) collective-permute-start(bf16[256,1024]{1,0:T(8,128)(2,1)} %collective-permute-done.5.refs_4_), channel_id=1, source_target_pairs={{0,448},{64,0},{128,64},{192,128},{256,192},{320,256},{384,320},{4... | collective-permute-start | bytes 1572872 | tf_op jit(solution)/shard_map/ppermute | solution.py:208
  64.9 4.0 %collective-permute-done.8.refs_0_ = bf16[1024,384]{1,0:T(8,128)(2,1)S(1)} collective-permute-done((bf16[1024,384]{1,0:T(8,128)(2,1)}, bf16[1024,384]{1,0:T(8,128)(2,1)S(1)}, u32[]{:S(2)}, u32[]{:S(2)}) %collective-permute-start.8) | collective-permute-done | bytes 786464 | tf_op jit(solution)/shard_map/ppermute | solution.py:208
  72.2 2.0 %shard_map.57 = (bf16[1280,768]{1,0:T(8,128)(2,1)S(1)}, bf16[256,1024]{1,0:T(8,128)(2,1)S(1)}) custom-call(s32[5]{0:T(128)S(1)} %stack.27.where, s32[32]{0:T(128)S(1)} %copy-done.4, bf16[32,16,1024]{2,1,0:T(8,128)(2,1)S(1)} %copy-done.5, bf16[32,16,384]{2,1,0:T(8,128)(2,1)S(1)} %copy-done.1, bf16[1024,384]{1,0:T(8,128)(2,1)S(1)} %copy-done.6, ...), custom_call_target="tpu_custom_call" | custom-call | flops 10000000000 | bytes 1572864 | tf_op jit(solution)/shard_map/pallas_call | solution.py:110
  74.6 4.0 %collective-permute-start.9 = (bf16[256,1024]{1,0:T(8,128)(2,1)S(1)}, bf16[256,1024]{1,0:T(8,128)(2,1)S(1)}, u32[]{:S(2)}, u32[]{:S(2)}) collective-permute-start(bf16[256,1024]{1,0:T(8,128)(2,1)S(1)} %broadcast_select_fusion), channel_id=1, source_target_pairs={{0,64},{1,449},{64,128},{65,1},{128,192},{129,65},{192,256},{193,1... | collective-permute-start | bytes 1572872 | tf_op jit(solution)/shard_map/ppermute | solution.py:212
  78.6 10.4 %shard_map.58 = (bf16[4,512,384]{2,1,0:T(8,128)(2,1)S(1)}, bf16[4,512,384]{2,1,0:T(8,128)(2,1)}) custom-call(s32[5]{0:T(128)S(1)} %stack.27.where, bf16[1280,768]{1,0:T(8,128)(2,1)S(1)} %get-tuple-element.30.table, bf16[256,1024]{1,0:T(8,128)(2,1)S(1)} %get-tuple-element.31.downs, bf16[256,1024]{1,0:T(8,128)(2,1)S(1)} %shard_map.55.refs_0_, ...), custom_call_target="tpu_custom_call" | custom-call | flops 3523215360 | bytes 8388608 | tf_op jit(solution)/shard_map/pallas_call | solution.py:177
  89.0 5.7 %collective-permute-start.10 = (bf16[4,512,384]{2,1,0:T(8,128)(2,1)}, bf16[4,512,384]{2,1,0:T(8,128)(2,1)}, u32[]{:S(2)}, u32[]{:S(2)}) collective-permute-start(bf16[4,512,384]{2,1,0:T(8,128)(2,1)} %get-tuple-element.37), channel_id=1, source_target_pairs={{0,1},{1,0},{2,3},{3,2},{4,5},{5,4},{6,7},{7,6},{8,9},{9,8},{10,11... | collective-permute-start | bytes 4718600 | tf_op jit(solution)/shard_map/ppermute | solution.py:208
  94.6 2.0 %shard_map.59 = (bf16[4,512,384]{2,1,0:T(8,128)(2,1)S(1)}, bf16[256,384]{1,0:T(8,128)(2,1)S(1)}) custom-call(s32[5]{0:T(128)S(1)} %stack.27.where, bf16[1280,768]{1,0:T(8,128)(2,1)S(1)} %get-tuple-element.30.table, bf16[256,1024]{1,0:T(8,128)(2,1)S(1)} %get-tuple-element.31.downs, ...), custom_call_target="tpu_custom_call", output_to_operand_aliasing={{0}: (4, {})} | custom-call | flops 503316480 | bytes 2883584 | tf_op jit(solution)/shard_map/pallas_call | solution.py:177
  96.7 1.9 %collective-permute-start.11 = (bf16[256,384]{1,0:T(8,128)(2,1)S(1)}, bf16[256,384]{1,0:T(8,128)(2,1)S(1)}, u32[]{:S(2)}, u32[]{:S(2)}) collective-permute-start(bf16[256,384]{1,0:T(8,128)(2,1)S(1)} %get-tuple-element.38), channel_id=1, source_target_pairs={{0,1},{1,0},{2,3},{3,2},{4,5},{5,4},{6,7},{7,6},{8,9},{9,8},{10,11... | collective-permute-start | bytes 589832 | tf_op jit(solution)/shard_map/ppermute | solution.py:208
  98.7 1.3 collective-permute-done.11
  100.7 2.3 %fusion.2 = (bf16[512,384]{1,0:T(8,128)(2,1)S(1)}, bf16[512,384]{1,0:T(8,128)(2,1)}, bf16[512,384]{1,0:T(8,128)(2,1)S(1)}) fusion(bf16[4,512,384]{2,1,0:T(8,128)(2,1)} %bitcast_dynamic-update-slice_fusion, bf16[4,512,384]{2,1,0:T(8,128)(2,1)S(1)} %get-tuple-element.35), kind=kLoop, calls=%fused_computation.8 | loop fusion | flops 2359296 | bytes 3538944 | tf_op jit(solution)/shard_map/convert_element_type | solution.py:243
  103.0 4.7 %collective-permute-start.14 = (bf16[512,384]{1,0:T(8,128)(2,1)}, bf16[512,384]{1,0:T(8,128)(2,1)S(1)}, u32[]{:S(2)}, u32[]{:S(2)}) collective-permute-start(bf16[512,384]{1,0:T(8,128)(2,1)} %get-tuple-element.40), channel_id=1, source_target_pairs={{0,8},{4,12},{8,0},{12,4},{1,9},{5,13},{9,1},{13,5},{2,10},{6,14},... | collective-permute-start | bytes 1179656 | tf_op jit(solution)/shard_map/ppermute | solution.py:208
  107.7 2.7 %collective-permute-start.13 = (bf16[512,384]{1,0:T(8,128)(2,1)S(1)}, bf16[512,384]{1,0:T(8,128)(2,1)S(1)}, u32[]{:S(2)}, u32[]{:S(2)}) collective-permute-start(bf16[512,384]{1,0:T(8,128)(2,1)S(1)} %get-tuple-element.41), channel_id=1, source_target_pairs={{0,12},{4,0},{8,4},{12,8},{1,13},{5,1},{9,5},{13,9},{2,14},{6,2},{... | collective-permute-start | bytes 1179656 | tf_op jit(solution)/shard_map/ppermute | solution.py:208
  110.4 2.5 %collective-permute-start.12 = (bf16[512,384]{1,0:T(8,128)(2,1)S(1)}, bf16[512,384]{1,0:T(8,128)(2,1)S(1)}, u32[]{:S(2)}, u32[]{:S(2)}) collective-permute-start(bf16[512,384]{1,0:T(8,128)(2,1)S(1)} %get-tuple-element.39), channel_id=1, source_target_pairs={{0,4},{4,8},{8,12},{12,0},{1,5},{5,9},{9,13},{13,1},{2,6},{6,10},{... | collective-permute-start | bytes 1179656 | tf_op jit(solution)/shard_map/ppermute | solution.py:208
  113.0 4.2 %collective-permute-done.14 = bf16[512,384]{1,0:T(8,128)(2,1)S(1)} collective-permute-done((bf16[512,384]{1,0:T(8,128)(2,1)}, bf16[512,384]{1,0:T(8,128)(2,1)S(1)}, u32[]{:S(2)}, u32[]{:S(2)}) %collective-permute-start.14) | collective-permute-done | bytes 393248 | tf_op jit(solution)/shard_map/ppermute | solution.py:208
  117.1 8.5 %collective-permute-done.13 = bf16[512,384]{1,0:T(8,128)(2,1)S(1)} collective-permute-done((bf16[512,384]{1,0:T(8,128)(2,1)S(1)}, bf16[512,384]{1,0:T(8,128)(2,1)S(1)}, u32[]{:S(2)}, u32[]{:S(2)}) %collective-permute-start.13) | collective-permute-done | bytes 393248 | tf_op jit(solution)/shard_map/ppermute | solution.py:208
  126.0 1.2 fusion
  127.3 5.3 %collective-permute-start.16 = (bf16[256,384]{1,0:T(8,128)(2,1)S(1)}, bf16[256,384]{1,0:T(8,128)(2,1)S(1)}, u32[]{:S(2)}, u32[]{:S(2)}) collective-permute-start(bf16[256,384]{1,0:T(8,128)(2,1)S(1)} %get-tuple-element.43), channel_id=1, source_target_pairs={{0,2},{1,34},{2,0},{3,32},{32,3},{33,35},{34,1},{35,33},{4,6},{5,3... | collective-permute-start | bytes 589832 | tf_op jit(solution)/shard_map/ppermute | solution.py:253
  132.7 4.8 %collective-permute-start.15 = (bf16[256,384]{1,0:T(8,128)(2,1)S(1)}, bf16[256,384]{1,0:T(8,128)(2,1)S(1)}, u32[]{:S(2)}, u32[]{:S(2)}) collective-permute-start(bf16[256,384]{1,0:T(8,128)(2,1)S(1)} %get-tuple-element.42), channel_id=1, source_target_pairs={{0,0},{1,32},{2,2},{3,34},{32,1},{33,33},{34,3},{35,35},{4,4},{5,3... | collective-permute-start | bytes 589832 | tf_op jit(solution)/shard_map/ppermute | solution.py:254
  137.4 2.3 %collective-permute-done.16 = bf16[256,384]{1,0:T(8,128)(2,1)S(1)} collective-permute-done((bf16[256,384]{1,0:T(8,128)(2,1)S(1)}, bf16[256,384]{1,0:T(8,128)(2,1)S(1)}, u32[]{:S(2)}, u32[]{:S(2)}) %collective-permute-start.16) | collective-permute-done | bytes 196640 | tf_op jit(solution)/shard_map/ppermute | solution.py:253
  139.7 3.2 %collective-permute-done.15 = bf16[256,384]{1,0:T(8,128)(2,1)S(1)} collective-permute-done((bf16[256,384]{1,0:T(8,128)(2,1)S(1)}, bf16[256,384]{1,0:T(8,128)(2,1)S(1)}, u32[]{:S(2)}, u32[]{:S(2)}) %collective-permute-start.15) | collective-permute-done | bytes 196640 | tf_op jit(solution)/shard_map/ppermute | solution.py:254
  (37 shorter events, 10.8 us)
Async XLA Ops:
  0.0 68.9 %copy-start.4 = (s32[32]{0:T(128)S(1)}, s32[32]{0:T(128)}, u32[]{:S(2)}) copy-start(s32[32]{0:T(128)} %adapter.3) | copy-start | bytes 388
  0.0 13.5 %collective-permute-start = (bf16[128,1024]{1,0:T(8,128)(2,1)}, bf16[128,1024]{1,0:T(8,128)(2,1)S(1)}, u32[]{:S(2)}, u32[]{:S(2)}) collective-permute-start(bf16[128,1024]{1,0:T(8,128)(2,1)} %first.2), channel_id=1, source_target_pairs={{0,16},{16,0},{1,17},{17,1},{2,18},{18,2},{3,19},{19,3},{4,20},{20... | collective-permute-start | bytes 786440 | tf_op jit(solution)/shard_map/ppermute | solution.py:208
  5.1 1.0 copy-start
  6.1 0.7 copy-start.3
  6.7 62.2 %copy-start.1 = (bf16[32,16,384]{2,1,0:T(8,128)(2,1)S(1)}, bf16[32,16,384]{2,1,0:T(8,128)(2,1)}, u32[]{:S(2)}) copy-start(bf16[32,16,384]{2,1,0:T(8,128)(2,1)} %up.3) | copy-start | bytes 1179652
  7.7 14.4 %collective-permute-start.1 = (bf16[256,384]{1,0:T(8,128)(2,1)S(1)}, bf16[256,384]{1,0:T(8,128)(2,1)S(1)}, u32[]{:S(2)}, u32[]{:S(2)}) collective-permute-start(bf16[256,384]{1,0:T(8,128)(2,1)S(1)} %shard_map.56), channel_id=1, source_target_pairs={{0,32},{32,0},{1,33},{33,1},{2,34},{34,2},{3,35},{35,3},{4,36},{36... | collective-permute-start | bytes 589832 | tf_op jit(solution)/shard_map/ppermute | solution.py:208
  13.6 1.0 copy-start.2
  22.2 0.7 copy-start.9
  22.8 16.8 %collective-permute-start.2 = (bf16[256,1024]{1,0:T(8,128)(2,1)S(1)}, bf16[256,1024]{1,0:T(8,128)(2,1)S(1)}, u32[]{:S(2)}, u32[]{:S(2)}) collective-permute-start(bf16[256,1024]{1,0:T(8,128)(2,1)S(1)} %shard_map.55.refs_0_), channel_id=1, source_target_pairs={{0,64},{64,128},{128,192},{192,256},{256,320},{320,384},{384,448},... | collective-permute-start | bytes 1572872 | tf_op jit(solution)/shard_map/ppermute | solution.py:208
  26.5 14.0 %collective-permute-start.3 = (bf16[256,1024]{1,0:T(8,128)(2,1)S(1)}, bf16[256,1024]{1,0:T(8,128)(2,1)S(1)}, u32[]{:S(2)}, u32[]{:S(2)}) collective-permute-start(bf16[256,1024]{1,0:T(8,128)(2,1)S(1)} %shard_map.55.refs_0_), channel_id=1, source_target_pairs={{0,448},{64,0},{128,64},{192,128},{256,192},{320,256},{384,320},{4... | collective-permute-start | bytes 1572872 | tf_op jit(solution)/shard_map/ppermute | solution.py:208
  30.3 38.6 %collective-permute-start.8 = (bf16[1024,384]{1,0:T(8,128)(2,1)}, bf16[1024,384]{1,0:T(8,128)(2,1)S(1)}, u32[]{:S(2)}, u32[]{:S(2)}) collective-permute-start(bf16[1024,384]{1,0:T(8,128)(2,1)} %first.3), channel_id=1, source_target_pairs={{0,32},{32,0},{1,33},{33,1},{2,34},{34,2},{3,35},{35,3},{4,36},{36... | collective-permute-start | bytes 2359304 | tf_op jit(solution)/shard_map/ppermute | solution.py:208
  40.5 33.6 %copy-start.7 = (bf16[256,1024]{1,0:T(8,128)(2,1)}, bf16[256,1024]{1,0:T(8,128)(2,1)S(1)}, u32[]{:S(2)}) copy-start(bf16[256,1024]{1,0:T(8,128)(2,1)S(1)} %collective-permute-done.3.refs_2_) | copy-start | bytes 1572868
  40.5 15.7 %collective-permute-start.4 = (bf16[256,1024]{1,0:T(8,128)(2,1)S(1)}, bf16[256,1024]{1,0:T(8,128)(2,1)}, u32[]{:S(2)}, u32[]{:S(2)}) collective-permute-start(bf16[256,1024]{1,0:T(8,128)(2,1)S(1)} %collective-permute-done.2.refs_1_), channel_id=1, source_target_pairs={{0,64},{64,128},{128,192},{192,256},{256,320},{320,384},{384,448},... | collective-permute-start | bytes 1572872 | tf_op jit(solution)/shard_map/ppermute | solution.py:208
  43.7 14.7 %collective-permute-start.5 = (bf16[256,1024]{1,0:T(8,128)(2,1)S(1)}, bf16[256,1024]{1,0:T(8,128)(2,1)}, u32[]{:S(2)}, u32[]{:S(2)}) collective-permute-start(bf16[256,1024]{1,0:T(8,128)(2,1)S(1)} %collective-permute-done.3.refs_2_), channel_id=1, source_target_pairs={{0,448},{64,0},{128,64},{192,128},{256,192},{320,256},{384,320},{4... | collective-permute-start | bytes 1572872 | tf_op jit(solution)/shard_map/ppermute | solution.py:208
  58.4 15.8 %collective-permute-start.6 = (bf16[256,1024]{1,0:T(8,128)(2,1)}, bf16[256,1024]{1,0:T(8,128)(2,1)S(1)}, u32[]{:S(2)}, u32[]{:S(2)}) collective-permute-start(bf16[256,1024]{1,0:T(8,128)(2,1)} %collective-permute-done.4.refs_3_), channel_id=1, source_target_pairs={{0,64},{64,128},{128,192},{192,256},{256,320},{320,384},{384,448},... | collective-permute-start | bytes 1572872 | tf_op jit(solution)/shard_map/ppermute | solution.py:208
  62.4 12.1 %collective-permute-start.7 = (bf16[256,1024]{1,0:T(8,128)(2,1)}, bf16[256,1024]{1,0:T(8,128)(2,1)S(1)}, u32[]{:S(2)}, u32[]{:S(2)}) collective-permute-start(bf16[256,1024]{1,0:T(8,128)(2,1)} %collective-permute-done.5.refs_4_), channel_id=1, source_target_pairs={{0,448},{64,0},{128,64},{192,128},{256,192},{320,256},{384,320},{4... | collective-permute-start | bytes 1572872 | tf_op jit(solution)/shard_map/ppermute | solution.py:208
  68.9 1.2 copy-start.5
  70.1 1.1 copy-start.6
  71.2 0.9 copy-start.10
  74.2 4.4 %copy-start.8 = (bf16[256,1024]{1,0:T(8,128)(2,1)S(1)}, bf16[256,1024]{1,0:T(8,128)(2,1)}, u32[]{:S(2)}) copy-start(bf16[256,1024]{1,0:T(8,128)(2,1)} %copy-done.7) | copy-start | bytes 1572868
  74.6 14.4 %collective-permute-start.9 = (bf16[256,1024]{1,0:T(8,128)(2,1)S(1)}, bf16[256,1024]{1,0:T(8,128)(2,1)S(1)}, u32[]{:S(2)}, u32[]{:S(2)}) collective-permute-start(bf16[256,1024]{1,0:T(8,128)(2,1)S(1)} %broadcast_select_fusion), channel_id=1, source_target_pairs={{0,64},{1,449},{64,128},{65,1},{128,192},{129,65},{192,256},{193,1... | collective-permute-start | bytes 1572872 | tf_op jit(solution)/shard_map/ppermute | solution.py:212
  89.0 11.1 %collective-permute-start.10 = (bf16[4,512,384]{2,1,0:T(8,128)(2,1)}, bf16[4,512,384]{2,1,0:T(8,128)(2,1)}, u32[]{:S(2)}, u32[]{:S(2)}) collective-permute-start(bf16[4,512,384]{2,1,0:T(8,128)(2,1)} %get-tuple-element.37), channel_id=1, source_target_pairs={{0,1},{1,0},{2,3},{3,2},{4,5},{5,4},{6,7},{7,6},{8,9},{9,8},{10,11... | collective-permute-start | bytes 4718600 | tf_op jit(solution)/shard_map/ppermute | solution.py:208
  96.7 3.3 %collective-permute-start.11 = (bf16[256,384]{1,0:T(8,128)(2,1)S(1)}, bf16[256,384]{1,0:T(8,128)(2,1)S(1)}, u32[]{:S(2)}, u32[]{:S(2)}) collective-permute-start(bf16[256,384]{1,0:T(8,128)(2,1)S(1)} %get-tuple-element.38), channel_id=1, source_target_pairs={{0,1},{1,0},{2,3},{3,2},{4,5},{5,4},{6,7},{7,6},{8,9},{9,8},{10,11... | collective-permute-start | bytes 589832 | tf_op jit(solution)/shard_map/ppermute | solution.py:208
  103.0 14.2 %collective-permute-start.14 = (bf16[512,384]{1,0:T(8,128)(2,1)}, bf16[512,384]{1,0:T(8,128)(2,1)S(1)}, u32[]{:S(2)}, u32[]{:S(2)}) collective-permute-start(bf16[512,384]{1,0:T(8,128)(2,1)} %get-tuple-element.40), channel_id=1, source_target_pairs={{0,8},{4,12},{8,0},{12,4},{1,9},{5,13},{9,1},{13,5},{2,10},{6,14},... | collective-permute-start | bytes 1179656 | tf_op jit(solution)/shard_map/ppermute | solution.py:208
  107.7 18.0 %collective-permute-start.13 = (bf16[512,384]{1,0:T(8,128)(2,1)S(1)}, bf16[512,384]{1,0:T(8,128)(2,1)S(1)}, u32[]{:S(2)}, u32[]{:S(2)}) collective-permute-start(bf16[512,384]{1,0:T(8,128)(2,1)S(1)} %get-tuple-element.41), channel_id=1, source_target_pairs={{0,12},{4,0},{8,4},{12,8},{1,13},{5,1},{9,5},{13,9},{2,14},{6,2},{... | collective-permute-start | bytes 1179656 | tf_op jit(solution)/shard_map/ppermute | solution.py:208
  110.4 15.6 %collective-permute-start.12 = (bf16[512,384]{1,0:T(8,128)(2,1)S(1)}, bf16[512,384]{1,0:T(8,128)(2,1)S(1)}, u32[]{:S(2)}, u32[]{:S(2)}) collective-permute-start(bf16[512,384]{1,0:T(8,128)(2,1)S(1)} %get-tuple-element.39), channel_id=1, source_target_pairs={{0,4},{4,8},{8,12},{12,0},{1,5},{5,9},{9,13},{13,1},{2,6},{6,10},{... | collective-permute-start | bytes 1179656 | tf_op jit(solution)/shard_map/ppermute | solution.py:208
  127.3 12.4 %collective-permute-start.16 = (bf16[256,384]{1,0:T(8,128)(2,1)S(1)}, bf16[256,384]{1,0:T(8,128)(2,1)S(1)}, u32[]{:S(2)}, u32[]{:S(2)}) collective-permute-start(bf16[256,384]{1,0:T(8,128)(2,1)S(1)} %get-tuple-element.43), channel_id=1, source_target_pairs={{0,2},{1,34},{2,0},{3,32},{32,3},{33,35},{34,1},{35,33},{4,6},{5,3... | collective-permute-start | bytes 589832 | tf_op jit(solution)/shard_map/ppermute | solution.py:253
  132.7 10.3 %collective-permute-start.15 = (bf16[256,384]{1,0:T(8,128)(2,1)S(1)}, bf16[256,384]{1,0:T(8,128)(2,1)S(1)}, u32[]{:S(2)}, u32[]{:S(2)}) collective-permute-start(bf16[256,384]{1,0:T(8,128)(2,1)S(1)} %get-tuple-element.42), channel_id=1, source_target_pairs={{0,0},{1,32},{2,2},{3,34},{32,1},{33,33},{34,3},{35,35},{4,4},{5,3... | collective-permute-start | bytes 589832 | tf_op jit(solution)/shard_map/ppermute | solution.py:254

commit v5 on v3

--- a/solution.py
+++ b/solution.py
@@ -224,19 +224,28 @@
         shift = [(i, (i + d) % X) for i in range(X)]
         return lax.ppermute(added(d).astype(jnp.bfloat16), "x", shift).astype(jnp.float32)
 
-    across = moved(2)
-    beside = moved(3) + moved(1)
-    total = jnp.stack([added(0) + across, beside]).astype(jnp.bfloat16)
-    total = total.reshape(2, ZH, rows, columns)
-
-    here = jnp.where(zh == 0, total[:, 0], total[:, 1])
-    there = jnp.where(zh == 0, total[:, 1], total[:, 0])
     places = [(i, h, j) for i in range(ZP) for h in range(ZH) for j in range(C)]
     swap = [(i * 4 + h * 2 + j, j * 4 + h * 2 + i) for i, h, j in places]
     cross = [(i * 4 + h * 2 + j, j * 4 + (1 - h) * 2 + i) for i, h, j in places]
-    far = lax.ppermute(there, ("p", "zh", "c"), cross)
-    near = lax.ppermute(here, ("p", "zh", "c"), swap)
-    out = near.astype(jnp.float32) + far.astype(jnp.float32)
+
+    def split(total):
+        total = total.astype(jnp.bfloat16).reshape(ZH, rows, columns)
+        here = jnp.where(zh == 0, total[0], total[1])
+        there = jnp.where(zh == 0, total[1], total[0])
+        return here, there
+
+    def sent(value, pairs):
+        return lax.ppermute(value, ("p", "zh", "c"), pairs)
+
+    from_2, from_3, from_1 = moved(2), moved(3), moved(1)
+    here, there = split(added(0) + from_2)
+    far = sent(there, cross)
+    near = sent(here, swap)
+    here, there = split(from_3 + from_1)
+    far_beside = sent(there, cross)
+    near_beside = sent(here, swap)
+    out = jnp.stack([near, near_beside]).astype(jnp.float32)
+    out += jnp.stack([far, far_beside]).astype(jnp.float32)
     out = jnp.where(half == 0, out, out[::-1])
     return out.reshape(ZQ * rows, columns).astype(jnp.bfloat16)
 

time: 140 us -> 138 us (0.986)
  waiting for transfers between devices: 49 us -> 41 us
  starting transfers between devices: 52.3 us -> 58.2 us
    ppermute x3, waiting for transfers between devices: 5.99 us -> 0.01 us  [moved(): lax.ppermute(added(d).astype(jnp.bfloat16), 'x', shift).astype(jnp.float32)]
    ppermute x2 -> x4, starting transfers between devices: 10.2 us -> 16.1 us  [sent(): return lax.ppermute(value, ('p', 'zh', 'c'), pairs)]
    ppermute x2 -> x4, waiting for transfers between devices: 8.1 us -> 6.02 us  [sent(): return lax.ppermute(value, ('p', 'zh', 'c'), pairs)]
  transfers between devices with their start and end apart: 16 -> 18, of which waited for: 11 -> 9; matrix products, arithmetic and copies ran while one was open for 7% -> 7% of each run, Pallas kernels for 2% -> 2%
where the time goes in v5:
time: 138 us; the launch traced here: 137 us
  starting transfers between devices  58.2 us (42%)
  waiting for transfers between devices  41 us (30%)
  between operations  13.8 us (10%)
  local copies, waits for them, and re-layouts  13.2 us (10%)
  Pallas kernels  9.77 us (7%)
    ppermute x2, waiting for transfers between devices, local(): swapped = [lax.ppermute(v, 'p', flip(ZP)) for v in jnp.split(own, 2)]  22.4 us
    ppermute x4, starting transfers between devices, sent(): return lax.ppermute(value, ('p', 'zh', 'c'), pairs)  16.1 us
    ppermute x3, starting transfers between devices, moved(): lax.ppermute(added(d).astype(jnp.bfloat16), 'x', shift).astype(jnp.float32)  9.89 us
    ppermute x2, starting transfers between devices, local(): swapped = [lax.ppermute(v, 'p', flip(ZP)) for v in jnp.split(own, 2)]  9.67 us
    pallas_call x1, Pallas kernels, partials(): pl.pallas_call(project, out_shape=(out, out), grid_spec=pltpu.PrefetchSca...  6.75 us
    ppermute x4, waiting for transfers between devices, sent(): return lax.ppermute(value, ('p', 'zh', 'c'), pairs)  6.02 us
    ppermute x2, starting transfers between devices, local(): swapped_pair = [lax.ppermute(v, 'x', flip(X)) for v in swapped]  5.61 us
    gather x4, local copies, waits for them, and re-layouts, taken(): return table[adapters(i, j)].reshape(-1, table.shape[2])  5.61 us
  transfers between devices with their start and end apart: 18, of which 9 were waited for; matrix products, arithmetic and copies ran while one was open for 7% of the time, Pallas kernels for 2%

profile of v5, /device:TPU:1, one launch (start us, length us, event | category | flops | bytes accessed | tf_op | source)
XLA Modules:
  0.0 137.1 jit_solution(218882384508013939)
XLA Ops:
  6.5 1.7 %collective-permute-start = (bf16[128,1024]{1,0:T(8,128)(2,1)}, bf16[128,1024]{1,0:T(8,128)(2,1)S(1)}, u32[]{:S(2)}, u32[]{:S(2)}) collective-permute-start(bf16[128,1024]{1,0:T(8,128)(2,1)} %param.5), channel_id=1, source_target_pairs={{0,0},{4,16},{8,8},{12,24},{16,4},{20,20},{24,12},{28,28},{1,1},{5... | collective-permute-start | bytes 786440 | tf_op jit(solution)/shard_map/ppermute | solution.py:187
  8.3 5.4 %collective-permute-start.1 = (bf16[128,1024]{1,0:T(8,128)(2,1)}, bf16[128,1024]{1,0:T(8,128)(2,1)S(1)}, u32[]{:S(2)}, u32[]{:S(2)}) collective-permute-start(bf16[128,1024]{1,0:T(8,128)(2,1)} %param.5), channel_id=1, source_target_pairs={{0,16},{4,0},{8,24},{12,8},{16,20},{20,4},{24,28},{28,12},{1,17},{... | collective-permute-start | bytes 786440 | tf_op jit(solution)/shard_map/ppermute | solution.py:190
  13.7 4.8 %collective-permute-done.1.second = bf16[128,1024]{1,0:T(8,128)(2,1)S(1)} collective-permute-done((bf16[128,1024]{1,0:T(8,128)(2,1)}, bf16[128,1024]{1,0:T(8,128)(2,1)S(1)}, u32[]{:S(2)}, u32[]{:S(2)}) %collective-permute-start.1) | collective-permute-done | bytes 262176 | tf_op jit(solution)/shard_map/ppermute | solution.py:190
  19.5 2.1 %fusion.8 = (bf16[512,384]{1,0:T(8,128)(2,1)}, bf16[512,384]{1,0:T(8,128)(2,1)}) fusion(bf16[1024,384]{1,0:T(8,128)(2,1)} %refs_0_.1), kind=kLoop, calls=%fused_computation.33 | loop fusion | bytes 1572864 | tf_op jit(solution)/shard_map/split | solution.py:210
  21.6 7.7 %collective-permute-start.2 = (bf16[512,384]{1,0:T(8,128)(2,1)}, bf16[512,384]{1,0:T(8,128)(2,1)S(1)}, u32[]{:S(2)}, u32[]{:S(2)}) collective-permute-start(bf16[512,384]{1,0:T(8,128)(2,1)} %get-tuple-element.16), channel_id=1, source_target_pairs={{0,32},{32,0},{1,33},{33,1},{2,34},{34,2},{3,35},{35,3},{4,36},{36... | collective-permute-start | bytes 1179656 | tf_op jit(solution)/shard_map/ppermute | solution.py:210
  29.3 1.9 %collective-permute-start.3 = (bf16[512,384]{1,0:T(8,128)(2,1)}, bf16[512,384]{1,0:T(8,128)(2,1)}, u32[]{:S(2)}, u32[]{:S(2)}) collective-permute-start(bf16[512,384]{1,0:T(8,128)(2,1)} %get-tuple-element.15), channel_id=1, source_target_pairs={{0,32},{32,0},{1,33},{33,1},{2,34},{34,2},{3,35},{35,3},{4,36},{36... | collective-permute-start | bytes 1179656 | tf_op jit(solution)/shard_map/ppermute | solution.py:210
  31.2 3.0 %collective-permute-start.4 = (bf16[1024,384]{1,0:T(8,128)(2,1)}, bf16[1024,384]{1,0:T(8,128)(2,1)S(1)}, u32[]{:S(2)}, u32[]{:S(2)}) collective-permute-start(bf16[1024,384]{1,0:T(8,128)(2,1)} %refs_0_.1), channel_id=1, source_target_pairs={{0,4},{4,0},{8,12},{12,8},{1,5},{5,1},{9,13},{13,9},{2,6},{6,2},{1... | collective-permute-start | bytes 2359304 | tf_op jit(solution)/shard_map/ppermute | solution.py:209
  37.0 2.2 %collective-permute-start.8 = (bf16[128,1024]{1,0:T(8,128)(2,1)}, bf16[128,1024]{1,0:T(8,128)(2,1)}, u32[]{:S(2)}, u32[]{:S(2)}) collective-permute-start(bf16[128,1024]{1,0:T(8,128)(2,1)} %bitcast.10), channel_id=1, source_target_pairs={{0,4},{4,0},{8,12},{12,8},{1,5},{5,1},{9,13},{13,9},{2,6},{6,2},{1... | collective-permute-start | bytes 786440 | tf_op jit(solution)/shard_map/ppermute | solution.py:204
  39.2 16.8 %collective-permute-done.2.refs_1_ = bf16[512,384]{1,0:T(8,128)(2,1)S(1)} collective-permute-done((bf16[512,384]{1,0:T(8,128)(2,1)}, bf16[512,384]{1,0:T(8,128)(2,1)S(1)}, u32[]{:S(2)}, u32[]{:S(2)}) %collective-permute-start.2) | collective-permute-done | bytes 393248 | tf_op jit(solution)/shard_map/ppermute | solution.py:210
  56.0 2.8 %collective-permute-start.5 = (bf16[512,384]{1,0:T(8,128)(2,1)S(1)}, bf16[512,384]{1,0:T(8,128)(2,1)}, u32[]{:S(2)}, u32[]{:S(2)}) collective-permute-start(bf16[512,384]{1,0:T(8,128)(2,1)S(1)} %collective-permute-done.2.refs_1_), channel_id=1, source_target_pairs={{0,4},{4,0},{8,12},{12,8},{1,5},{5,1},{9,13},{13,9},{2,6},{6,2},{1... | collective-permute-start | bytes 1179656 | tf_op jit(solution)/shard_map/ppermute | solution.py:211
  58.8 5.6 %collective-permute-done.3.refs_2_ = bf16[512,384]{1,0:T(8,128)(2,1)} collective-permute-done((bf16[512,384]{1,0:T(8,128)(2,1)}, bf16[512,384]{1,0:T(8,128)(2,1)}, u32[]{:S(2)}, u32[]{:S(2)}) %collective-permute-start.3) | collective-permute-done | bytes 393248 | tf_op jit(solution)/shard_map/ppermute | solution.py:210
  64.4 2.8 %collective-permute-start.6 = (bf16[512,384]{1,0:T(8,128)(2,1)}, bf16[512,384]{1,0:T(8,128)(2,1)}, u32[]{:S(2)}, u32[]{:S(2)}) collective-permute-start(bf16[512,384]{1,0:T(8,128)(2,1)} %collective-permute-done.3.refs_2_), channel_id=1, source_target_pairs={{0,4},{4,0},{8,12},{12,8},{1,5},{5,1},{9,13},{13,9},{2,6},{6,2},{1... | collective-permute-start | bytes 1179656 | tf_op jit(solution)/shard_map/ppermute | solution.py:211
  67.3 2.2 %gather_fusion.1 = bf16[8,16,384]{2,1,0:T(8,128)(2,1)} fusion(bf16[32,16,384]{2,1,0:T(8,128)(2,1)} %param.8, s32[1024]{0:T(1024)S(1)} %pad_clamp_fusion.1), kind=kCustom, calls=%fused_computation.1 | custom fusion | bytes 196640 | tf_op jit(solution)/shard_map/gather | solution.py:201
  69.5 1.9 %collective-permute-start.7 = (bf16[128,384]{1,0:T(8,128)(2,1)}, bf16[128,384]{1,0:T(8,128)(2,1)S(1)}, u32[]{:S(2)}, u32[]{:S(2)}) collective-permute-start(bf16[128,384]{1,0:T(8,128)(2,1)} %bitcast.7), channel_id=1, source_target_pairs={{0,32},{32,0},{1,33},{33,1},{2,34},{34,2},{3,35},{35,3},{4,36},{36... | collective-permute-start | bytes 294920 | tf_op jit(solution)/shard_map/ppermute | solution.py:206
  72.0 1.6 %gather_fusion = bf16[8,16,384]{2,1,0:T(8,128)(2,1)S(1)} fusion(bf16[32,16,384]{2,1,0:T(8,128)(2,1)} %param.8, s32[1024]{0:T(1024)S(1)} %pad_clamp_fusion.2), kind=kCustom, calls=%fused_computation | custom fusion | bytes 196640 | tf_op jit(solution)/shard_map/gather | solution.py:201
  73.7 2.7 %collective-permute-done.7.refs_7_ = bf16[128,384]{1,0:T(8,128)(2,1)S(1)} collective-permute-done((bf16[128,384]{1,0:T(8,128)(2,1)}, bf16[128,384]{1,0:T(8,128)(2,1)S(1)}, u32[]{:S(2)}, u32[]{:S(2)}) %collective-permute-start.7) | collective-permute-done | bytes 98336 | tf_op jit(solution)/shard_map/ppermute | solution.py:206
  76.8 2.2 %shard_map.56.table = bf16[2688,768]{1,0:T(8,128)(2,1)S(1)} custom-call(s32[2]{0:T(128)S(1)} %pad_add_fusion.slots, bf16[1024,384]{1,0:T(8,128)(2,1)S(1)} %copy-done.3, bf16[512,384]{1,0:T(8,128)(2,1)S(1)} %collective-permute-done.2.refs_1_, bf16[512,384]{1,0:T(8,128)(2,1)} %collective-permute-done.3.refs_2_, ...), custom_call_target="tpu_custom_call" | custom-call | tf_op jit(solution)/shard_map/pallas_call | solution.py:82
  79.0 2.0 %copy-done.1 = bf16[2688,768]{1,0:T(8,128)(2,1)} copy-done((bf16[2688,768]{1,0:T(8,128)(2,1)}, bf16[2688,768]{1,0:T(8,128)(2,1)S(1)}, u32[]{:S(2)}) %copy-start.1) | copy-done | bytes 4128792
  81.0 2.6 %all-gather.3.cloned.1.call-done = bf16[1024,2048]{1,0:T(8,128)(2,1)} async-done(((bf16[128,2048]{1,0:T(8,128)(2,1)}), bf16[1024,2048]{1,0:T(8,128)(2,1)}) %all-gather.3.cloned.1.call-update) | async-done | bytes 4194320 | tf_op jit(solution)/shard_map/all_gather | solution.py:193
  83.6 2.2 %copy-done.2 = bf16[2688,768]{1,0:T(8,128)(2,1)S(1)} copy-done((bf16[2688,768]{1,0:T(8,128)(2,1)S(1)}, bf16[2688,768]{1,0:T(8,128)(2,1)}, u32[]{:S(2)}) %copy-start.2) | copy-done | bytes 4128792
  85.8 6.7 %shard_map.57 = (bf16[4,256,384]{2,1,0:T(8,128)(2,1)S(1)}, bf16[4,256,384]{2,1,0:T(8,128)(2,1)S(1)}) custom-call(s32[1]{0:T(128)} %bitcast.order, bf16[8,128,2048]{2,1,0:T(8,128)(2,1)} %bitcast.41, bf16[2688,768]{1,0:T(8,128)(2,1)S(1)} %copy-done.2), custom_call_target="tpu_custom_call" | custom-call | flops 3221225472 | bytes 9895936 | tf_op jit(solution)/shard_map/pallas_call | solution.py:145
  92.5 2.6 %collective-permute-start.9 = (bf16[4,256,384]{2,1,0:T(8,128)(2,1)S(1)}, bf16[4,256,384]{2,1,0:T(8,128)(2,1)S(1)}, u32[]{:S(2)}, u32[]{:S(2)}) collective-permute-start(bf16[4,256,384]{2,1,0:T(8,128)(2,1)S(1)} %get-tuple-element.8), channel_id=1, source_target_pairs={{0,1},{1,0},{2,3},{3,2},{4,5},{5,4},{6,7},{7,6},{8,9},{9,8},{10,11... | collective-permute-start | bytes 2359304 | tf_op jit(solution)/shard_map/ppermute | solution.py:218
  95.1 1.9 %collective-permute-done.9 = bf16[4,256,384]{2,1,0:T(8,128)(2,1)S(1)} collective-permute-done((bf16[4,256,384]{2,1,0:T(8,128)(2,1)S(1)}, bf16[4,256,384]{2,1,0:T(8,128)(2,1)S(1)}, u32[]{:S(2)}, u32[]{:S(2)}) %collective-permute-start.9) | collective-permute-done | bytes 786464 | tf_op jit(solution)/shard_map/ppermute | solution.py:218
  97.1 4.6 %collective-permute-start.10 = (bf16[256,384]{1,0:T(8,128)(2,1)S(1)}, bf16[256,384]{1,0:T(8,128)(2,1)S(1)}, u32[]{:S(2)}, u32[]{:S(2)}) collective-permute-start(bf16[256,384]{1,0:T(8,128)(2,1)S(1)} %get-tuple-element.12), channel_id=1, source_target_pairs={{0,8},{4,12},{8,0},{12,4},{1,9},{5,13},{9,1},{13,5},{2,10},{6,14},... | collective-permute-start | bytes 589832 | tf_op jit(solution)/shard_map/ppermute | solution.py:225
  101.8 2.8 %collective-permute-start.12 = (bf16[256,384]{1,0:T(8,128)(2,1)S(1)}, bf16[256,384]{1,0:T(8,128)(2,1)S(1)}, u32[]{:S(2)}, u32[]{:S(2)}) collective-permute-start(bf16[256,384]{1,0:T(8,128)(2,1)S(1)} %get-tuple-element.14), channel_id=1, source_target_pairs={{0,12},{4,0},{8,4},{12,8},{1,13},{5,1},{9,5},{13,9},{2,14},{6,2},{... | collective-permute-start | bytes 589832 | tf_op jit(solution)/shard_map/ppermute | solution.py:225
  104.6 2.5 %collective-permute-start.13 = (bf16[256,384]{1,0:T(8,128)(2,1)S(1)}, bf16[256,384]{1,0:T(8,128)(2,1)S(1)}, u32[]{:S(2)}, u32[]{:S(2)}) collective-permute-start(bf16[256,384]{1,0:T(8,128)(2,1)S(1)} %get-tuple-element.13), channel_id=1, source_target_pairs={{0,4},{4,8},{8,12},{12,0},{1,5},{5,9},{9,13},{13,1},{2,6},{6,10},{... | collective-permute-start | bytes 589832 | tf_op jit(solution)/shard_map/ppermute | solution.py:225
  107.2 5.5 %collective-permute-start.11 = (bf16[128,384]{1,0:T(8,128)(2,1)S(1)}, bf16[128,384]{1,0:T(8,128)(2,1)S(1)}, u32[]{:S(2)}, u32[]{:S(2)}) collective-permute-start(bf16[128,384]{1,0:T(8,128)(2,1)S(1)} %get-tuple-element.18), channel_id=1, source_target_pairs={{0,0},{1,32},{2,2},{3,34},{32,1},{33,33},{34,3},{35,35},{4,4},{5,3... | collective-permute-start | bytes 294920 | tf_op jit(solution)/shard_map/ppermute | solution.py:238
  112.6 4.7 %collective-permute-start.15 = (bf16[128,384]{1,0:T(8,128)(2,1)S(1)}, bf16[128,384]{1,0:T(8,128)(2,1)S(1)}, u32[]{:S(2)}, u32[]{:S(2)}) collective-permute-start(bf16[128,384]{1,0:T(8,128)(2,1)S(1)} %get-tuple-element.17), channel_id=1, source_target_pairs={{0,2},{1,34},{2,0},{3,32},{32,3},{33,35},{34,1},{35,33},{4,6},{5,3... | collective-permute-start | bytes 294920 | tf_op jit(solution)/shard_map/ppermute | solution.py:238
  117.5 3.7 %collective-permute-start.14 = (bf16[128,384]{1,0:T(8,128)(2,1)S(1)}, bf16[128,384]{1,0:T(8,128)(2,1)S(1)}, u32[]{:S(2)}, u32[]{:S(2)}) collective-permute-start(bf16[128,384]{1,0:T(8,128)(2,1)S(1)} %get-tuple-element.20), channel_id=1, source_target_pairs={{0,0},{1,32},{2,2},{3,34},{32,1},{33,33},{34,3},{35,35},{4,4},{5,3... | collective-permute-start | bytes 294920 | tf_op jit(solution)/shard_map/ppermute | solution.py:238
  121.2 2.2 %collective-permute-start.16 = (bf16[128,384]{1,0:T(8,128)(2,1)S(1)}, bf16[128,384]{1,0:T(8,128)(2,1)S(1)}, u32[]{:S(2)}, u32[]{:S(2)}) collective-permute-start(bf16[128,384]{1,0:T(8,128)(2,1)S(1)} %get-tuple-element.19), channel_id=1, source_target_pairs={{0,2},{1,34},{2,0},{3,32},{32,3},{33,35},{34,1},{35,33},{4,6},{5,3... | collective-permute-start | bytes 294920 | tf_op jit(solution)/shard_map/ppermute | solution.py:238
  123.5 3.1 %collective-permute-done.14 = bf16[128,384]{1,0:T(8,128)(2,1)S(1)} collective-permute-done((bf16[128,384]{1,0:T(8,128)(2,1)S(1)}, bf16[128,384]{1,0:T(8,128)(2,1)S(1)}, u32[]{:S(2)}, u32[]{:S(2)}) %collective-permute-start.14) | collective-permute-done | bytes 98336 | tf_op jit(solution)/shard_map/ppermute | solution.py:238
  126.6 2.9 %collective-permute-done.16 = bf16[128,384]{1,0:T(8,128)(2,1)S(1)} collective-permute-done((bf16[128,384]{1,0:T(8,128)(2,1)S(1)}, bf16[128,384]{1,0:T(8,128)(2,1)S(1)}, u32[]{:S(2)}, u32[]{:S(2)}) %collective-permute-start.16) | collective-permute-done | bytes 98336 | tf_op jit(solution)/shard_map/ppermute | solution.py:238
  (36 shorter events, 5.8 us)
Async XLA Ops:
  6.5 29.2 %copy-start = (bf16[32,16,1024]{2,1,0:T(8,128)(2,1)S(1)}, bf16[32,16,1024]{2,1,0:T(8,128)(2,1)}, u32[]{:S(2)}) copy-start(bf16[32,16,1024]{2,1,0:T(8,128)(2,1)} %param.7) | copy-start | bytes 3145732
  6.5 70.3 %copy-start.3 = (bf16[1024,384]{1,0:T(8,128)(2,1)S(1)}, bf16[1024,384]{1,0:T(8,128)(2,1)}, u32[]{:S(2)}) copy-start(bf16[1024,384]{1,0:T(8,128)(2,1)} %refs_0_.1) | copy-start | bytes 2359300
  6.5 77.0 %all-gather.3.cloned.1.call-start = ((), (), s32[]{:S(2)}) async-start(), calls=%async_computation | async-start | bytes 4718592 | tf_op jit(solution)/shard_map/all_gather | solution.py:193
  6.5 7.2 %collective-permute-start = (bf16[128,1024]{1,0:T(8,128)(2,1)}, bf16[128,1024]{1,0:T(8,128)(2,1)S(1)}, u32[]{:S(2)}, u32[]{:S(2)}) collective-permute-start(bf16[128,1024]{1,0:T(8,128)(2,1)} %param.5), channel_id=1, source_target_pairs={{0,0},{4,16},{8,8},{12,24},{16,4},{20,20},{24,12},{28,28},{1,1},{5... | collective-permute-start | bytes 786440 | tf_op jit(solution)/shard_map/ppermute | solution.py:187
  8.3 10.3 %collective-permute-start.1 = (bf16[128,1024]{1,0:T(8,128)(2,1)}, bf16[128,1024]{1,0:T(8,128)(2,1)S(1)}, u32[]{:S(2)}, u32[]{:S(2)}) collective-permute-start(bf16[128,1024]{1,0:T(8,128)(2,1)} %param.5), channel_id=1, source_target_pairs={{0,16},{4,0},{8,24},{12,8},{16,20},{20,4},{24,28},{28,12},{1,17},{... | collective-permute-start | bytes 786440 | tf_op jit(solution)/shard_map/ppermute | solution.py:190
  21.6 34.5 %collective-permute-start.2 = (bf16[512,384]{1,0:T(8,128)(2,1)}, bf16[512,384]{1,0:T(8,128)(2,1)S(1)}, u32[]{:S(2)}, u32[]{:S(2)}) collective-permute-start(bf16[512,384]{1,0:T(8,128)(2,1)} %get-tuple-element.16), channel_id=1, source_target_pairs={{0,32},{32,0},{1,33},{33,1},{2,34},{34,2},{3,35},{35,3},{4,36},{36... | collective-permute-start | bytes 1179656 | tf_op jit(solution)/shard_map/ppermute | solution.py:210
  29.3 35.1 %collective-permute-start.3 = (bf16[512,384]{1,0:T(8,128)(2,1)}, bf16[512,384]{1,0:T(8,128)(2,1)}, u32[]{:S(2)}, u32[]{:S(2)}) collective-permute-start(bf16[512,384]{1,0:T(8,128)(2,1)} %get-tuple-element.15), channel_id=1, source_target_pairs={{0,32},{32,0},{1,33},{33,1},{2,34},{34,2},{3,35},{35,3},{4,36},{36... | collective-permute-start | bytes 1179656 | tf_op jit(solution)/shard_map/ppermute | solution.py:210
  31.2 45.6 %collective-permute-start.4 = (bf16[1024,384]{1,0:T(8,128)(2,1)}, bf16[1024,384]{1,0:T(8,128)(2,1)S(1)}, u32[]{:S(2)}, u32[]{:S(2)}) collective-permute-start(bf16[1024,384]{1,0:T(8,128)(2,1)} %refs_0_.1), channel_id=1, source_target_pairs={{0,4},{4,0},{8,12},{12,8},{1,5},{5,1},{9,13},{13,9},{2,6},{6,2},{1... | collective-permute-start | bytes 2359304 | tf_op jit(solution)/shard_map/ppermute | solution.py:209
  37.0 39.4 %collective-permute-start.8 = (bf16[128,1024]{1,0:T(8,128)(2,1)}, bf16[128,1024]{1,0:T(8,128)(2,1)}, u32[]{:S(2)}, u32[]{:S(2)}) collective-permute-start(bf16[128,1024]{1,0:T(8,128)(2,1)} %bitcast.10), channel_id=1, source_target_pairs={{0,4},{4,0},{8,12},{12,8},{1,5},{5,1},{9,13},{13,9},{2,6},{6,2},{1... | collective-permute-start | bytes 786440 | tf_op jit(solution)/shard_map/ppermute | solution.py:204
  56.0 20.3 %collective-permute-start.5 = (bf16[512,384]{1,0:T(8,128)(2,1)S(1)}, bf16[512,384]{1,0:T(8,128)(2,1)}, u32[]{:S(2)}, u32[]{:S(2)}) collective-permute-start(bf16[512,384]{1,0:T(8,128)(2,1)S(1)} %collective-permute-done.2.refs_1_), channel_id=1, source_target_pairs={{0,4},{4,0},{8,12},{12,8},{1,5},{5,1},{9,13},{13,9},{2,6},{6,2},{1... | collective-permute-start | bytes 1179656 | tf_op jit(solution)/shard_map/ppermute | solution.py:211
  64.4 12.4 %collective-permute-start.6 = (bf16[512,384]{1,0:T(8,128)(2,1)}, bf16[512,384]{1,0:T(8,128)(2,1)}, u32[]{:S(2)}, u32[]{:S(2)}) collective-permute-start(bf16[512,384]{1,0:T(8,128)(2,1)} %collective-permute-done.3.refs_2_), channel_id=1, source_target_pairs={{0,4},{4,0},{8,12},{12,8},{1,5},{5,1},{9,13},{13,9},{2,6},{6,2},{1... | collective-permute-start | bytes 1179656 | tf_op jit(solution)/shard_map/ppermute | solution.py:211
  69.5 6.9 %collective-permute-start.7 = (bf16[128,384]{1,0:T(8,128)(2,1)}, bf16[128,384]{1,0:T(8,128)(2,1)S(1)}, u32[]{:S(2)}, u32[]{:S(2)}) collective-permute-start(bf16[128,384]{1,0:T(8,128)(2,1)} %bitcast.7), channel_id=1, source_target_pairs={{0,32},{32,0},{1,33},{33,1},{2,34},{34,2},{3,35},{35,3},{4,36},{36... | collective-permute-start | bytes 294920 | tf_op jit(solution)/shard_map/ppermute | solution.py:206
  79.0 2.0 %copy-start.1 = (bf16[2688,768]{1,0:T(8,128)(2,1)}, bf16[2688,768]{1,0:T(8,128)(2,1)S(1)}, u32[]{:S(2)}) copy-start(bf16[2688,768]{1,0:T(8,128)(2,1)S(1)} %shard_map.56.table) | copy-start | bytes 12386308
  83.6 2.2 %copy-start.2 = (bf16[2688,768]{1,0:T(8,128)(2,1)S(1)}, bf16[2688,768]{1,0:T(8,128)(2,1)}, u32[]{:S(2)}) copy-start(bf16[2688,768]{1,0:T(8,128)(2,1)} %copy-done.1) | copy-start | bytes 12386308
  92.5 4.5 %collective-permute-start.9 = (bf16[4,256,384]{2,1,0:T(8,128)(2,1)S(1)}, bf16[4,256,384]{2,1,0:T(8,128)(2,1)S(1)}, u32[]{:S(2)}, u32[]{:S(2)}) collective-permute-start(bf16[4,256,384]{2,1,0:T(8,128)(2,1)S(1)} %get-tuple-element.8), channel_id=1, source_target_pairs={{0,1},{1,0},{2,3},{3,2},{4,5},{5,4},{6,7},{7,6},{8,9},{9,8},{10,11... | collective-permute-start | bytes 2359304 | tf_op jit(solution)/shard_map/ppermute | solution.py:218
  97.1 9.9 %collective-permute-start.10 = (bf16[256,384]{1,0:T(8,128)(2,1)S(1)}, bf16[256,384]{1,0:T(8,128)(2,1)S(1)}, u32[]{:S(2)}, u32[]{:S(2)}) collective-permute-start(bf16[256,384]{1,0:T(8,128)(2,1)S(1)} %get-tuple-element.12), channel_id=1, source_target_pairs={{0,8},{4,12},{8,0},{12,4},{1,9},{5,13},{9,1},{13,5},{2,10},{6,14},... | collective-permute-start | bytes 589832 | tf_op jit(solution)/shard_map/ppermute | solution.py:225
  101.8 15.7 %collective-permute-start.12 = (bf16[256,384]{1,0:T(8,128)(2,1)S(1)}, bf16[256,384]{1,0:T(8,128)(2,1)S(1)}, u32[]{:S(2)}, u32[]{:S(2)}) collective-permute-start(bf16[256,384]{1,0:T(8,128)(2,1)S(1)} %get-tuple-element.14), channel_id=1, source_target_pairs={{0,12},{4,0},{8,4},{12,8},{1,13},{5,1},{9,5},{13,9},{2,14},{6,2},{... | collective-permute-start | bytes 589832 | tf_op jit(solution)/shard_map/ppermute | solution.py:225
  104.6 12.9 %collective-permute-start.13 = (bf16[256,384]{1,0:T(8,128)(2,1)S(1)}, bf16[256,384]{1,0:T(8,128)(2,1)S(1)}, u32[]{:S(2)}, u32[]{:S(2)}) collective-permute-start(bf16[256,384]{1,0:T(8,128)(2,1)S(1)} %get-tuple-element.13), channel_id=1, source_target_pairs={{0,4},{4,8},{8,12},{12,0},{1,5},{5,9},{9,13},{13,1},{2,6},{6,10},{... | collective-permute-start | bytes 589832 | tf_op jit(solution)/shard_map/ppermute | solution.py:225
  107.2 16.3 %collective-permute-start.11 = (bf16[128,384]{1,0:T(8,128)(2,1)S(1)}, bf16[128,384]{1,0:T(8,128)(2,1)S(1)}, u32[]{:S(2)}, u32[]{:S(2)}) collective-permute-start(bf16[128,384]{1,0:T(8,128)(2,1)S(1)} %get-tuple-element.18), channel_id=1, source_target_pairs={{0,0},{1,32},{2,2},{3,34},{32,1},{33,33},{34,3},{35,35},{4,4},{5,3... | collective-permute-start | bytes 294920 | tf_op jit(solution)/shard_map/ppermute | solution.py:238
  112.6 10.8 %collective-permute-start.15 = (bf16[128,384]{1,0:T(8,128)(2,1)S(1)}, bf16[128,384]{1,0:T(8,128)(2,1)S(1)}, u32[]{:S(2)}, u32[]{:S(2)}) collective-permute-start(bf16[128,384]{1,0:T(8,128)(2,1)S(1)} %get-tuple-element.17), channel_id=1, source_target_pairs={{0,2},{1,34},{2,0},{3,32},{32,3},{33,35},{34,1},{35,33},{4,6},{5,3... | collective-permute-start | bytes 294920 | tf_op jit(solution)/shard_map/ppermute | solution.py:238
  117.5 9.0 %collective-permute-start.14 = (bf16[128,384]{1,0:T(8,128)(2,1)S(1)}, bf16[128,384]{1,0:T(8,128)(2,1)S(1)}, u32[]{:S(2)}, u32[]{:S(2)}) collective-permute-start(bf16[128,384]{1,0:T(8,128)(2,1)S(1)} %get-tuple-element.20), channel_id=1, source_target_pairs={{0,0},{1,32},{2,2},{3,34},{32,1},{33,33},{34,3},{35,35},{4,4},{5,3... | collective-permute-start | bytes 294920 | tf_op jit(solution)/shard_map/ppermute | solution.py:238
  121.2 8.3 %collective-permute-start.16 = (bf16[128,384]{1,0:T(8,128)(2,1)S(1)}, bf16[128,384]{1,0:T(8,128)(2,1)S(1)}, u32[]{:S(2)}, u32[]{:S(2)}) collective-permute-start(bf16[128,384]{1,0:T(8,128)(2,1)S(1)} %get-tuple-element.19), channel_id=1, source_target_pairs={{0,2},{1,34},{2,0},{3,32},{32,3},{33,35},{34,1},{35,33},{4,6},{5,3... | collective-permute-start | bytes 294920 | tf_op jit(solution)/shard_map/ppermute | solution.py:238
Sparse Core Ops, SparseCore 0:
  19.6 63.9 all-gather.2

commit v6 on v5

--- a/solution.py
+++ b/solution.py
@@ -244,8 +244,8 @@
     here, there = split(from_3 + from_1)
     far_beside = sent(there, cross)
     near_beside = sent(here, swap)
-    out = jnp.stack([near, near_beside]).astype(jnp.float32)
-    out += jnp.stack([far, far_beside]).astype(jnp.float32)
+    out = jnp.stack([far, far_beside]).astype(jnp.float32)
+    out += jnp.stack([near, near_beside]).astype(jnp.float32)
     out = jnp.where(half == 0, out, out[::-1])
     return out.reshape(ZQ * rows, columns).astype(jnp.bfloat16)
 

time: 138 us -> 137 us (level)
  transfers between devices with their start and end apart: 18 -> 18, of which waited for: 9 -> 10; matrix products, arithmetic and copies ran while one was open for 7% -> 7% of each run, Pallas kernels for 2% -> 2%
where the time goes in v6:
time: 137 us
  starting transfers between devices  58.2 us (42%)
  waiting for transfers between devices  40.6 us (30%)
  between operations  13.8 us (10%)
  local copies, waits for them, and re-layouts  13.2 us (10%)
  Pallas kernels  9.77 us (7%)
    ppermute x2, waiting for transfers between devices, local(): swapped = [lax.ppermute(v, 'p', flip(ZP)) for v in jnp.split(own, 2)]  22.4 us
    ppermute x4, starting transfers between devices, sent(): return lax.ppermute(value, ('p', 'zh', 'c'), pairs)  16.1 us
    ppermute x3, starting transfers between devices, moved(): lax.ppermute(added(d).astype(jnp.bfloat16), 'x', shift).astype(jnp.float32)  9.89 us
    ppermute x2, starting transfers between devices, local(): swapped = [lax.ppermute(v, 'p', flip(ZP)) for v in jnp.split(own, 2)]  9.67 us
    pallas_call x1, Pallas kernels, partials(): pl.pallas_call(project, out_shape=(out, out), grid_spec=pltpu.PrefetchSca...  6.75 us
    ppermute x4, waiting for transfers between devices, sent(): return lax.ppermute(value, ('p', 'zh', 'c'), pairs)  5.71 us
    ppermute x2, starting transfers between devices, local(): swapped_pair = [lax.ppermute(v, 'x', flip(X)) for v in swapped]  5.61 us
    gather x4, local copies, waits for them, and re-layouts, taken(): return table[adapters(i, j)].reshape(-1, table.shape[2])  5.61 us
  transfers between devices with their start and end apart: 18, of which 10 were waited for; matrix products, arithmetic and copies ran while one was open for 7% of the time, Pallas kernels for 2%

profile of v6, /device:TPU:1, one launch (start us, length us, event | category | flops | bytes accessed | tf_op | source)
XLA Modules:
  0.0 136.8 jit_solution(11823730411133626866)
XLA Ops:
  6.5 1.7 %collective-permute-start = (bf16[128,1024]{1,0:T(8,128)(2,1)}, bf16[128,1024]{1,0:T(8,128)(2,1)S(1)}, u32[]{:S(2)}, u32[]{:S(2)}) collective-permute-start(bf16[128,1024]{1,0:T(8,128)(2,1)} %param.5), channel_id=1, source_target_pairs={{0,0},{4,16},{8,8},{12,24},{16,4},{20,20},{24,12},{28,28},{1,1},{5... | collective-permute-start | bytes 786440 | tf_op jit(solution)/shard_map/ppermute | solution.py:187
  8.3 5.4 %collective-permute-start.1 = (bf16[128,1024]{1,0:T(8,128)(2,1)}, bf16[128,1024]{1,0:T(8,128)(2,1)S(1)}, u32[]{:S(2)}, u32[]{:S(2)}) collective-permute-start(bf16[128,1024]{1,0:T(8,128)(2,1)} %param.5), channel_id=1, source_target_pairs={{0,16},{4,0},{8,24},{12,8},{16,20},{20,4},{24,28},{28,12},{1,17},{... | collective-permute-start | bytes 786440 | tf_op jit(solution)/shard_map/ppermute | solution.py:190
  13.7 4.8 %collective-permute-done.1.second = bf16[128,1024]{1,0:T(8,128)(2,1)S(1)} collective-permute-done((bf16[128,1024]{1,0:T(8,128)(2,1)}, bf16[128,1024]{1,0:T(8,128)(2,1)S(1)}, u32[]{:S(2)}, u32[]{:S(2)}) %collective-permute-start.1) | collective-permute-done | bytes 262176 | tf_op jit(solution)/shard_map/ppermute | solution.py:190
  19.5 2.1 %fusion.8 = (bf16[512,384]{1,0:T(8,128)(2,1)}, bf16[512,384]{1,0:T(8,128)(2,1)}) fusion(bf16[1024,384]{1,0:T(8,128)(2,1)} %refs_0_.1), kind=kLoop, calls=%fused_computation.33 | loop fusion | bytes 1572864 | tf_op jit(solution)/shard_map/split | solution.py:210
  21.6 7.7 %collective-permute-start.2 = (bf16[512,384]{1,0:T(8,128)(2,1)}, bf16[512,384]{1,0:T(8,128)(2,1)S(1)}, u32[]{:S(2)}, u32[]{:S(2)}) collective-permute-start(bf16[512,384]{1,0:T(8,128)(2,1)} %get-tuple-element.16), channel_id=1, source_target_pairs={{0,32},{32,0},{1,33},{33,1},{2,34},{34,2},{3,35},{35,3},{4,36},{36... | collective-permute-start | bytes 1179656 | tf_op jit(solution)/shard_map/ppermute | solution.py:210
  29.3 1.9 %collective-permute-start.3 = (bf16[512,384]{1,0:T(8,128)(2,1)}, bf16[512,384]{1,0:T(8,128)(2,1)}, u32[]{:S(2)}, u32[]{:S(2)}) collective-permute-start(bf16[512,384]{1,0:T(8,128)(2,1)} %get-tuple-element.15), channel_id=1, source_target_pairs={{0,32},{32,0},{1,33},{33,1},{2,34},{34,2},{3,35},{35,3},{4,36},{36... | collective-permute-start | bytes 1179656 | tf_op jit(solution)/shard_map/ppermute | solution.py:210
  31.2 3.0 %collective-permute-start.4 = (bf16[1024,384]{1,0:T(8,128)(2,1)}, bf16[1024,384]{1,0:T(8,128)(2,1)S(1)}, u32[]{:S(2)}, u32[]{:S(2)}) collective-permute-start(bf16[1024,384]{1,0:T(8,128)(2,1)} %refs_0_.1), channel_id=1, source_target_pairs={{0,4},{4,0},{8,12},{12,8},{1,5},{5,1},{9,13},{13,9},{2,6},{6,2},{1... | collective-permute-start | bytes 2359304 | tf_op jit(solution)/shard_map/ppermute | solution.py:209
  37.0 2.2 %collective-permute-start.8 = (bf16[128,1024]{1,0:T(8,128)(2,1)}, bf16[128,1024]{1,0:T(8,128)(2,1)}, u32[]{:S(2)}, u32[]{:S(2)}) collective-permute-start(bf16[128,1024]{1,0:T(8,128)(2,1)} %bitcast.10), channel_id=1, source_target_pairs={{0,4},{4,0},{8,12},{12,8},{1,5},{5,1},{9,13},{13,9},{2,6},{6,2},{1... | collective-permute-start | bytes 786440 | tf_op jit(solution)/shard_map/ppermute | solution.py:204
  39.2 16.8 %collective-permute-done.2.refs_1_ = bf16[512,384]{1,0:T(8,128)(2,1)S(1)} collective-permute-done((bf16[512,384]{1,0:T(8,128)(2,1)}, bf16[512,384]{1,0:T(8,128)(2,1)S(1)}, u32[]{:S(2)}, u32[]{:S(2)}) %collective-permute-start.2) | collective-permute-done | bytes 393248 | tf_op jit(solution)/shard_map/ppermute | solution.py:210
  56.0 2.8 %collective-permute-start.5 = (bf16[512,384]{1,0:T(8,128)(2,1)S(1)}, bf16[512,384]{1,0:T(8,128)(2,1)}, u32[]{:S(2)}, u32[]{:S(2)}) collective-permute-start(bf16[512,384]{1,0:T(8,128)(2,1)S(1)} %collective-permute-done.2.refs_1_), channel_id=1, source_target_pairs={{0,4},{4,0},{8,12},{12,8},{1,5},{5,1},{9,13},{13,9},{2,6},{6,2},{1... | collective-permute-start | bytes 1179656 | tf_op jit(solution)/shard_map/ppermute | solution.py:211
  58.8 5.6 %collective-permute-done.3.refs_2_ = bf16[512,384]{1,0:T(8,128)(2,1)} collective-permute-done((bf16[512,384]{1,0:T(8,128)(2,1)}, bf16[512,384]{1,0:T(8,128)(2,1)}, u32[]{:S(2)}, u32[]{:S(2)}) %collective-permute-start.3) | collective-permute-done | bytes 393248 | tf_op jit(solution)/shard_map/ppermute | solution.py:210
  64.4 2.8 %collective-permute-start.6 = (bf16[512,384]{1,0:T(8,128)(2,1)}, bf16[512,384]{1,0:T(8,128)(2,1)}, u32[]{:S(2)}, u32[]{:S(2)}) collective-permute-start(bf16[512,384]{1,0:T(8,128)(2,1)} %collective-permute-done.3.refs_2_), channel_id=1, source_target_pairs={{0,4},{4,0},{8,12},{12,8},{1,5},{5,1},{9,13},{13,9},{2,6},{6,2},{1... | collective-permute-start | bytes 1179656 | tf_op jit(solution)/shard_map/ppermute | solution.py:211
  67.3 2.2 %gather_fusion.1 = bf16[8,16,384]{2,1,0:T(8,128)(2,1)} fusion(bf16[32,16,384]{2,1,0:T(8,128)(2,1)} %param.8, s32[1024]{0:T(1024)S(1)} %pad_clamp_fusion.1), kind=kCustom, calls=%fused_computation.1 | custom fusion | bytes 196640 | tf_op jit(solution)/shard_map/gather | solution.py:201
  69.5 1.9 %collective-permute-start.7 = (bf16[128,384]{1,0:T(8,128)(2,1)}, bf16[128,384]{1,0:T(8,128)(2,1)S(1)}, u32[]{:S(2)}, u32[]{:S(2)}) collective-permute-start(bf16[128,384]{1,0:T(8,128)(2,1)} %bitcast.7), channel_id=1, source_target_pairs={{0,32},{32,0},{1,33},{33,1},{2,34},{34,2},{3,35},{35,3},{4,36},{36... | collective-permute-start | bytes 294920 | tf_op jit(solution)/shard_map/ppermute | solution.py:206
  72.0 1.6 %gather_fusion = bf16[8,16,384]{2,1,0:T(8,128)(2,1)S(1)} fusion(bf16[32,16,384]{2,1,0:T(8,128)(2,1)} %param.8, s32[1024]{0:T(1024)S(1)} %pad_clamp_fusion.2), kind=kCustom, calls=%fused_computation | custom fusion | bytes 196640 | tf_op jit(solution)/shard_map/gather | solution.py:201
  73.7 2.7 %collective-permute-done.7.refs_7_ = bf16[128,384]{1,0:T(8,128)(2,1)S(1)} collective-permute-done((bf16[128,384]{1,0:T(8,128)(2,1)}, bf16[128,384]{1,0:T(8,128)(2,1)S(1)}, u32[]{:S(2)}, u32[]{:S(2)}) %collective-permute-start.7) | collective-permute-done | bytes 98336 | tf_op jit(solution)/shard_map/ppermute | solution.py:206
  76.8 2.2 %shard_map.56.table = bf16[2688,768]{1,0:T(8,128)(2,1)S(1)} custom-call(s32[2]{0:T(128)S(1)} %pad_add_fusion.slots, bf16[1024,384]{1,0:T(8,128)(2,1)S(1)} %copy-done.3, bf16[512,384]{1,0:T(8,128)(2,1)S(1)} %collective-permute-done.2.refs_1_, bf16[512,384]{1,0:T(8,128)(2,1)} %collective-permute-done.3.refs_2_, ...), custom_call_target="tpu_custom_call" | custom-call | tf_op jit(solution)/shard_map/pallas_call | solution.py:82
  79.0 2.0 %copy-done.1 = bf16[2688,768]{1,0:T(8,128)(2,1)} copy-done((bf16[2688,768]{1,0:T(8,128)(2,1)}, bf16[2688,768]{1,0:T(8,128)(2,1)S(1)}, u32[]{:S(2)}) %copy-start.1) | copy-done | bytes 4128792
  81.0 2.6 %all-gather.3.cloned.1.call-done = bf16[1024,2048]{1,0:T(8,128)(2,1)} async-done(((bf16[128,2048]{1,0:T(8,128)(2,1)}), bf16[1024,2048]{1,0:T(8,128)(2,1)}) %all-gather.3.cloned.1.call-update) | async-done | bytes 4194320 | tf_op jit(solution)/shard_map/all_gather | solution.py:193
  83.6 2.2 %copy-done.2 = bf16[2688,768]{1,0:T(8,128)(2,1)S(1)} copy-done((bf16[2688,768]{1,0:T(8,128)(2,1)S(1)}, bf16[2688,768]{1,0:T(8,128)(2,1)}, u32[]{:S(2)}) %copy-start.2) | copy-done | bytes 4128792
  85.8 6.7 %shard_map.57 = (bf16[4,256,384]{2,1,0:T(8,128)(2,1)S(1)}, bf16[4,256,384]{2,1,0:T(8,128)(2,1)S(1)}) custom-call(s32[1]{0:T(128)} %bitcast.order, bf16[8,128,2048]{2,1,0:T(8,128)(2,1)} %bitcast.41, bf16[2688,768]{1,0:T(8,128)(2,1)S(1)} %copy-done.2), custom_call_target="tpu_custom_call" | custom-call | flops 3221225472 | bytes 9895936 | tf_op jit(solution)/shard_map/pallas_call | solution.py:145
  92.5 2.6 %collective-permute-start.9 = (bf16[4,256,384]{2,1,0:T(8,128)(2,1)S(1)}, bf16[4,256,384]{2,1,0:T(8,128)(2,1)S(1)}, u32[]{:S(2)}, u32[]{:S(2)}) collective-permute-start(bf16[4,256,384]{2,1,0:T(8,128)(2,1)S(1)} %get-tuple-element.8), channel_id=1, source_target_pairs={{0,1},{1,0},{2,3},{3,2},{4,5},{5,4},{6,7},{7,6},{8,9},{9,8},{10,11... | collective-permute-start | bytes 2359304 | tf_op jit(solution)/shard_map/ppermute | solution.py:218
  95.1 1.9 %collective-permute-done.9 = bf16[4,256,384]{2,1,0:T(8,128)(2,1)S(1)} collective-permute-done((bf16[4,256,384]{2,1,0:T(8,128)(2,1)S(1)}, bf16[4,256,384]{2,1,0:T(8,128)(2,1)S(1)}, u32[]{:S(2)}, u32[]{:S(2)}) %collective-permute-start.9) | collective-permute-done | bytes 786464 | tf_op jit(solution)/shard_map/ppermute | solution.py:218
  97.1 4.6 %collective-permute-start.10 = (bf16[256,384]{1,0:T(8,128)(2,1)S(1)}, bf16[256,384]{1,0:T(8,128)(2,1)S(1)}, u32[]{:S(2)}, u32[]{:S(2)}) collective-permute-start(bf16[256,384]{1,0:T(8,128)(2,1)S(1)} %get-tuple-element.12), channel_id=1, source_target_pairs={{0,8},{4,12},{8,0},{12,4},{1,9},{5,13},{9,1},{13,5},{2,10},{6,14},... | collective-permute-start | bytes 589832 | tf_op jit(solution)/shard_map/ppermute | solution.py:225
  101.8 2.8 %collective-permute-start.12 = (bf16[256,384]{1,0:T(8,128)(2,1)S(1)}, bf16[256,384]{1,0:T(8,128)(2,1)S(1)}, u32[]{:S(2)}, u32[]{:S(2)}) collective-permute-start(bf16[256,384]{1,0:T(8,128)(2,1)S(1)} %get-tuple-element.14), channel_id=1, source_target_pairs={{0,12},{4,0},{8,4},{12,8},{1,13},{5,1},{9,5},{13,9},{2,14},{6,2},{... | collective-permute-start | bytes 589832 | tf_op jit(solution)/shard_map/ppermute | solution.py:225
  104.6 2.5 %collective-permute-start.13 = (bf16[256,384]{1,0:T(8,128)(2,1)S(1)}, bf16[256,384]{1,0:T(8,128)(2,1)S(1)}, u32[]{:S(2)}, u32[]{:S(2)}) collective-permute-start(bf16[256,384]{1,0:T(8,128)(2,1)S(1)} %get-tuple-element.13), channel_id=1, source_target_pairs={{0,4},{4,8},{8,12},{12,0},{1,5},{5,9},{9,13},{13,1},{2,6},{6,10},{... | collective-permute-start | bytes 589832 | tf_op jit(solution)/shard_map/ppermute | solution.py:225
  107.2 7.4 %collective-permute-start.11 = (bf16[128,384]{1,0:T(8,128)(2,1)S(1)}, bf16[128,384]{1,0:T(8,128)(2,1)S(1)}, u32[]{:S(2)}, u32[]{:S(2)}) collective-permute-start(bf16[128,384]{1,0:T(8,128)(2,1)S(1)} %get-tuple-element.18), channel_id=1, source_target_pairs={{0,2},{1,34},{2,0},{3,32},{32,3},{33,35},{34,1},{35,33},{4,6},{5,3... | collective-permute-start | bytes 294920 | tf_op jit(solution)/shard_map/ppermute | solution.py:238
  114.6 2.8 %collective-permute-start.15 = (bf16[128,384]{1,0:T(8,128)(2,1)S(1)}, bf16[128,384]{1,0:T(8,128)(2,1)S(1)}, u32[]{:S(2)}, u32[]{:S(2)}) collective-permute-start(bf16[128,384]{1,0:T(8,128)(2,1)S(1)} %get-tuple-element.17), channel_id=1, source_target_pairs={{0,0},{1,32},{2,2},{3,34},{32,1},{33,33},{34,3},{35,35},{4,4},{5,3... | collective-permute-start | bytes 294920 | tf_op jit(solution)/shard_map/ppermute | solution.py:238
  117.5 3.7 %collective-permute-start.14 = (bf16[128,384]{1,0:T(8,128)(2,1)S(1)}, bf16[128,384]{1,0:T(8,128)(2,1)S(1)}, u32[]{:S(2)}, u32[]{:S(2)}) collective-permute-start(bf16[128,384]{1,0:T(8,128)(2,1)S(1)} %get-tuple-element.20), channel_id=1, source_target_pairs={{0,2},{1,34},{2,0},{3,32},{32,3},{33,35},{34,1},{35,33},{4,6},{5,3... | collective-permute-start | bytes 294920 | tf_op jit(solution)/shard_map/ppermute | solution.py:238
  121.3 2.2 %collective-permute-start.16 = (bf16[128,384]{1,0:T(8,128)(2,1)S(1)}, bf16[128,384]{1,0:T(8,128)(2,1)S(1)}, u32[]{:S(2)}, u32[]{:S(2)}) collective-permute-start(bf16[128,384]{1,0:T(8,128)(2,1)S(1)} %get-tuple-element.19), channel_id=1, source_target_pairs={{0,0},{1,32},{2,2},{3,34},{32,1},{33,33},{34,3},{35,35},{4,4},{5,3... | collective-permute-start | bytes 294920 | tf_op jit(solution)/shard_map/ppermute | solution.py:238
  124.1 1.9 %collective-permute-done.14 = bf16[128,384]{1,0:T(8,128)(2,1)S(1)} collective-permute-done((bf16[128,384]{1,0:T(8,128)(2,1)S(1)}, bf16[128,384]{1,0:T(8,128)(2,1)S(1)}, u32[]{:S(2)}, u32[]{:S(2)}) %collective-permute-start.14) | collective-permute-done | bytes 98336 | tf_op jit(solution)/shard_map/ppermute | solution.py:238
  126.0 3.2 %collective-permute-done.16 = bf16[128,384]{1,0:T(8,128)(2,1)S(1)} collective-permute-done((bf16[128,384]{1,0:T(8,128)(2,1)S(1)}, bf16[128,384]{1,0:T(8,128)(2,1)S(1)}, u32[]{:S(2)}, u32[]{:S(2)}) %collective-permute-start.16) | collective-permute-done | bytes 98336 | tf_op jit(solution)/shard_map/ppermute | solution.py:238
  (36 shorter events, 6.4 us)
Async XLA Ops:
  6.5 29.2 %copy-start = (bf16[32,16,1024]{2,1,0:T(8,128)(2,1)S(1)}, bf16[32,16,1024]{2,1,0:T(8,128)(2,1)}, u32[]{:S(2)}) copy-start(bf16[32,16,1024]{2,1,0:T(8,128)(2,1)} %param.7) | copy-start | bytes 3145732
  6.5 70.3 %copy-start.3 = (bf16[1024,384]{1,0:T(8,128)(2,1)S(1)}, bf16[1024,384]{1,0:T(8,128)(2,1)}, u32[]{:S(2)}) copy-start(bf16[1024,384]{1,0:T(8,128)(2,1)} %refs_0_.1) | copy-start | bytes 2359300
  6.5 77.0 %all-gather.3.cloned.1.call-start = ((), (), s32[]{:S(2)}) async-start(), calls=%async_computation | async-start | bytes 4718592 | tf_op jit(solution)/shard_map/all_gather | solution.py:193
  6.5 7.2 %collective-permute-start = (bf16[128,1024]{1,0:T(8,128)(2,1)}, bf16[128,1024]{1,0:T(8,128)(2,1)S(1)}, u32[]{:S(2)}, u32[]{:S(2)}) collective-permute-start(bf16[128,1024]{1,0:T(8,128)(2,1)} %param.5), channel_id=1, source_target_pairs={{0,0},{4,16},{8,8},{12,24},{16,4},{20,20},{24,12},{28,28},{1,1},{5... | collective-permute-start | bytes 786440 | tf_op jit(solution)/shard_map/ppermute | solution.py:187
  8.3 10.3 %collective-permute-start.1 = (bf16[128,1024]{1,0:T(8,128)(2,1)}, bf16[128,1024]{1,0:T(8,128)(2,1)S(1)}, u32[]{:S(2)}, u32[]{:S(2)}) collective-permute-start(bf16[128,1024]{1,0:T(8,128)(2,1)} %param.5), channel_id=1, source_target_pairs={{0,16},{4,0},{8,24},{12,8},{16,20},{20,4},{24,28},{28,12},{1,17},{... | collective-permute-start | bytes 786440 | tf_op jit(solution)/shard_map/ppermute | solution.py:190
  21.6 34.5 %collective-permute-start.2 = (bf16[512,384]{1,0:T(8,128)(2,1)}, bf16[512,384]{1,0:T(8,128)(2,1)S(1)}, u32[]{:S(2)}, u32[]{:S(2)}) collective-permute-start(bf16[512,384]{1,0:T(8,128)(2,1)} %get-tuple-element.16), channel_id=1, source_target_pairs={{0,32},{32,0},{1,33},{33,1},{2,34},{34,2},{3,35},{35,3},{4,36},{36... | collective-permute-start | bytes 1179656 | tf_op jit(solution)/shard_map/ppermute | solution.py:210
  29.3 35.1 %collective-permute-start.3 = (bf16[512,384]{1,0:T(8,128)(2,1)}, bf16[512,384]{1,0:T(8,128)(2,1)}, u32[]{:S(2)}, u32[]{:S(2)}) collective-permute-start(bf16[512,384]{1,0:T(8,128)(2,1)} %get-tuple-element.15), channel_id=1, source_target_pairs={{0,32},{32,0},{1,33},{33,1},{2,34},{34,2},{3,35},{35,3},{4,36},{36... | collective-permute-start | bytes 1179656 | tf_op jit(solution)/shard_map/ppermute | solution.py:210
  31.2 45.6 %collective-permute-start.4 = (bf16[1024,384]{1,0:T(8,128)(2,1)}, bf16[1024,384]{1,0:T(8,128)(2,1)S(1)}, u32[]{:S(2)}, u32[]{:S(2)}) collective-permute-start(bf16[1024,384]{1,0:T(8,128)(2,1)} %refs_0_.1), channel_id=1, source_target_pairs={{0,4},{4,0},{8,12},{12,8},{1,5},{5,1},{9,13},{13,9},{2,6},{6,2},{1... | collective-permute-start | bytes 2359304 | tf_op jit(solution)/shard_map/ppermute | solution.py:209
  37.0 39.4 %collective-permute-start.8 = (bf16[128,1024]{1,0:T(8,128)(2,1)}, bf16[128,1024]{1,0:T(8,128)(2,1)}, u32[]{:S(2)}, u32[]{:S(2)}) collective-permute-start(bf16[128,1024]{1,0:T(8,128)(2,1)} %bitcast.10), channel_id=1, source_target_pairs={{0,4},{4,0},{8,12},{12,8},{1,5},{5,1},{9,13},{13,9},{2,6},{6,2},{1... | collective-permute-start | bytes 786440 | tf_op jit(solution)/shard_map/ppermute | solution.py:204
  56.0 20.3 %collective-permute-start.5 = (bf16[512,384]{1,0:T(8,128)(2,1)S(1)}, bf16[512,384]{1,0:T(8,128)(2,1)}, u32[]{:S(2)}, u32[]{:S(2)}) collective-permute-start(bf16[512,384]{1,0:T(8,128)(2,1)S(1)} %collective-permute-done.2.refs_1_), channel_id=1, source_target_pairs={{0,4},{4,0},{8,12},{12,8},{1,5},{5,1},{9,13},{13,9},{2,6},{6,2},{1... | collective-permute-start | bytes 1179656 | tf_op jit(solution)/shard_map/ppermute | solution.py:211
  64.4 12.4 %collective-permute-start.6 = (bf16[512,384]{1,0:T(8,128)(2,1)}, bf16[512,384]{1,0:T(8,128)(2,1)}, u32[]{:S(2)}, u32[]{:S(2)}) collective-permute-start(bf16[512,384]{1,0:T(8,128)(2,1)} %collective-permute-done.3.refs_2_), channel_id=1, source_target_pairs={{0,4},{4,0},{8,12},{12,8},{1,5},{5,1},{9,13},{13,9},{2,6},{6,2},{1... | collective-permute-start | bytes 1179656 | tf_op jit(solution)/shard_map/ppermute | solution.py:211
  69.5 6.9 %collective-permute-start.7 = (bf16[128,384]{1,0:T(8,128)(2,1)}, bf16[128,384]{1,0:T(8,128)(2,1)S(1)}, u32[]{:S(2)}, u32[]{:S(2)}) collective-permute-start(bf16[128,384]{1,0:T(8,128)(2,1)} %bitcast.7), channel_id=1, source_target_pairs={{0,32},{32,0},{1,33},{33,1},{2,34},{34,2},{3,35},{35,3},{4,36},{36... | collective-permute-start | bytes 294920 | tf_op jit(solution)/shard_map/ppermute | solution.py:206
  79.0 2.0 %copy-start.1 = (bf16[2688,768]{1,0:T(8,128)(2,1)}, bf16[2688,768]{1,0:T(8,128)(2,1)S(1)}, u32[]{:S(2)}) copy-start(bf16[2688,768]{1,0:T(8,128)(2,1)S(1)} %shard_map.56.table) | copy-start | bytes 12386308
  83.6 2.2 %copy-start.2 = (bf16[2688,768]{1,0:T(8,128)(2,1)S(1)}, bf16[2688,768]{1,0:T(8,128)(2,1)}, u32[]{:S(2)}) copy-start(bf16[2688,768]{1,0:T(8,128)(2,1)} %copy-done.1) | copy-start | bytes 12386308
  92.5 4.5 %collective-permute-start.9 = (bf16[4,256,384]{2,1,0:T(8,128)(2,1)S(1)}, bf16[4,256,384]{2,1,0:T(8,128)(2,1)S(1)}, u32[]{:S(2)}, u32[]{:S(2)}) collective-permute-start(bf16[4,256,384]{2,1,0:T(8,128)(2,1)S(1)} %get-tuple-element.8), channel_id=1, source_target_pairs={{0,1},{1,0},{2,3},{3,2},{4,5},{5,4},{6,7},{7,6},{8,9},{9,8},{10,11... | collective-permute-start | bytes 2359304 | tf_op jit(solution)/shard_map/ppermute | solution.py:218
  97.1 9.9 %collective-permute-start.10 = (bf16[256,384]{1,0:T(8,128)(2,1)S(1)}, bf16[256,384]{1,0:T(8,128)(2,1)S(1)}, u32[]{:S(2)}, u32[]{:S(2)}) collective-permute-start(bf16[256,384]{1,0:T(8,128)(2,1)S(1)} %get-tuple-element.12), channel_id=1, source_target_pairs={{0,8},{4,12},{8,0},{12,4},{1,9},{5,13},{9,1},{13,5},{2,10},{6,14},... | collective-permute-start | bytes 589832 | tf_op jit(solution)/shard_map/ppermute | solution.py:225
  101.8 15.7 %collective-permute-start.12 = (bf16[256,384]{1,0:T(8,128)(2,1)S(1)}, bf16[256,384]{1,0:T(8,128)(2,1)S(1)}, u32[]{:S(2)}, u32[]{:S(2)}) collective-permute-start(bf16[256,384]{1,0:T(8,128)(2,1)S(1)} %get-tuple-element.14), channel_id=1, source_target_pairs={{0,12},{4,0},{8,4},{12,8},{1,13},{5,1},{9,5},{13,9},{2,14},{6,2},{... | collective-permute-start | bytes 589832 | tf_op jit(solution)/shard_map/ppermute | solution.py:225
  104.6 12.9 %collective-permute-start.13 = (bf16[256,384]{1,0:T(8,128)(2,1)S(1)}, bf16[256,384]{1,0:T(8,128)(2,1)S(1)}, u32[]{:S(2)}, u32[]{:S(2)}) collective-permute-start(bf16[256,384]{1,0:T(8,128)(2,1)S(1)} %get-tuple-element.13), channel_id=1, source_target_pairs={{0,4},{4,8},{8,12},{12,0},{1,5},{5,9},{9,13},{13,1},{2,6},{6,10},{... | collective-permute-start | bytes 589832 | tf_op jit(solution)/shard_map/ppermute | solution.py:225
  107.2 16.3 %collective-permute-start.11 = (bf16[128,384]{1,0:T(8,128)(2,1)S(1)}, bf16[128,384]{1,0:T(8,128)(2,1)S(1)}, u32[]{:S(2)}, u32[]{:S(2)}) collective-permute-start(bf16[128,384]{1,0:T(8,128)(2,1)S(1)} %get-tuple-element.18), channel_id=1, source_target_pairs={{0,2},{1,34},{2,0},{3,32},{32,3},{33,35},{34,1},{35,33},{4,6},{5,3... | collective-permute-start | bytes 294920 | tf_op jit(solution)/shard_map/ppermute | solution.py:238
  114.6 9.5 %collective-permute-start.15 = (bf16[128,384]{1,0:T(8,128)(2,1)S(1)}, bf16[128,384]{1,0:T(8,128)(2,1)S(1)}, u32[]{:S(2)}, u32[]{:S(2)}) collective-permute-start(bf16[128,384]{1,0:T(8,128)(2,1)S(1)} %get-tuple-element.17), channel_id=1, source_target_pairs={{0,0},{1,32},{2,2},{3,34},{32,1},{33,33},{34,3},{35,35},{4,4},{5,3... | collective-permute-start | bytes 294920 | tf_op jit(solution)/shard_map/ppermute | solution.py:238
  117.5 8.4 %collective-permute-start.14 = (bf16[128,384]{1,0:T(8,128)(2,1)S(1)}, bf16[128,384]{1,0:T(8,128)(2,1)S(1)}, u32[]{:S(2)}, u32[]{:S(2)}) collective-permute-start(bf16[128,384]{1,0:T(8,128)(2,1)S(1)} %get-tuple-element.20), channel_id=1, source_target_pairs={{0,2},{1,34},{2,0},{3,32},{32,3},{33,35},{34,1},{35,33},{4,6},{5,3... | collective-permute-start | bytes 294920 | tf_op jit(solution)/shard_map/ppermute | solution.py:238
  121.3 7.9 %collective-permute-start.16 = (bf16[128,384]{1,0:T(8,128)(2,1)S(1)}, bf16[128,384]{1,0:T(8,128)(2,1)S(1)}, u32[]{:S(2)}, u32[]{:S(2)}) collective-permute-start(bf16[128,384]{1,0:T(8,128)(2,1)S(1)} %get-tuple-element.19), channel_id=1, source_target_pairs={{0,0},{1,32},{2,2},{3,34},{32,1},{33,33},{34,3},{35,35},{4,4},{5,3... | collective-permute-start | bytes 294920 | tf_op jit(solution)/shard_map/ppermute | solution.py:238
Sparse Core Ops, SparseCore 0:
  19.6 63.9 all-gather.2

commit v7 on v6

--- a/solution.py
+++ b/solution.py
@@ -1,3 +1,5 @@
+import functools
+
 import jax
 import jax.numpy as jnp
 from jax import lax
@@ -90,8 +92,7 @@
     )(slots, *parts)
 
 
-def project(order, tokens, table, keep, send, held, sems):
-    step = pl.program_id(0)
+def project(base, order, tokens, table, keep, send, held, sems):
     rows, features = tokens.shape[1:]
     ranks = held.shape[3] - features
     rank = ranks // Y
@@ -99,17 +100,14 @@
     groups = tile_rows // rows
 
     def fetch(t):
-        at = pl.ds((t + order[0]) % X * groups, groups)
+        at = pl.ds((base + t + order[0]) % X * groups, groups)
         return pltpu.make_async_copy(
             tokens.at[at], held.at[t, :, :, pl.ds(0, features)], sems.at[t]
         )
 
-    @pl.when(step == 0)
-    def _():
-        for t in range(X):
-            fetch(t).start()
-
-    here = [step * tiles + i for i in range(tiles)]
+    here = range(tiles)
+    for t in here:
+        fetch(t).start()
     for t in here:
         fetch(t).wait()
     for t in here:
@@ -124,7 +122,7 @@
                 preferred_element_type=jnp.float32,
             )
         block = lax.broadcasted_iota(jnp.int32, shrink.shape, 0) // rows
-        block += (t + order[0]) % X * groups
+        block += (base + t + order[0]) % X * groups
         adapter = lax.broadcasted_iota(jnp.int32, shrink.shape, 1) // rank
         low = jnp.where(block == adapter, 0.5 * shrink, 0.0).astype(held.dtype)
         held[t, :, :, features:] = low.reshape(groups, rows, ranks)
@@ -136,18 +134,18 @@
         send[i] = total[:, columns:]
 
 
-def partials(x, gathered, table, ranks):
+def partials(x, gathered, table, ranks, base):
     rows, features = gathered.shape[1:]
     columns = table.shape[1] // 2
     groups = Y // X
     tiles = 2
-    out = jax.ShapeDtypeStruct((X, groups * rows, columns), jnp.bfloat16)
+    out = jax.ShapeDtypeStruct((tiles, groups * rows, columns), jnp.bfloat16)
     return pl.pallas_call(
-        project,
+        functools.partial(project, base),
         out_shape=(out, out),
         grid_spec=pltpu.PrefetchScalarGridSpec(
             num_scalar_prefetch=1,
-            grid=(X // tiles,),
+            grid=(1,),
             in_specs=[
                 pl.BlockSpec(memory_space=pltpu.HBM),
                 pl.BlockSpec(memory_space=pltpu.VMEM),
@@ -157,14 +155,14 @@
             ]
             * 2,
             scratch_shapes=[
-                pltpu.VMEM((X, groups, rows, features + ranks), jnp.bfloat16),
-                pltpu.SemaphoreType.DMA((X,)),
+                pltpu.VMEM((tiles, groups, rows, features + ranks), jnp.bfloat16),
+                pltpu.SemaphoreType.DMA((tiles,)),
             ],
         ),
         compiler_params=pltpu.CompilerParams(vmem_limit_bytes=VMEM_BYTES),
         cost_estimate=pl.CostEstimate(
-            flops=4 * gathered.size * columns,
-            bytes_accessed=2 * (gathered.size + table.size + 2 * out.size),
+            flops=2 * gathered.size * columns,
+            bytes_accessed=2 * (gathered.size // 2 + table.size + 2 * out.size),
             transcendentals=0,
         ),
     )(x.reshape(1), gathered, table)
@@ -214,8 +212,12 @@
         slots, [own, *swapped, pair, *swapped_pair, up, up_swapped, down, down_pair]
     )
 
-    keep, send = partials(x, gathered, table, down.shape[0])
-    received = lax.ppermute(send, "c", flip(C))
+    keep, received = {}, {}
+    for base in (2, 0):
+        kept, send = partials(x, gathered, table, down.shape[0], base)
+        got = lax.ppermute(send, "c", flip(C))
+        for i in range(2):
+            keep[base + i], received[base + i] = kept[i], got[i]
 
     def added(d):
         return keep[d].astype(jnp.float32) + received[d].astype(jnp.float32)

time: 137 us -> 139 us (1.015)
  starting transfers between devices: 58.2 us -> 60 us
  waiting for transfers between devices: 40.6 us -> 39 us
  Pallas kernels: 9.77 us -> 11.3 us
    ppermute x1 -> x2, starting transfers between devices: 2.58 us -> 4.51 us  [local(): got = lax.ppermute(send, 'c', flip(C))]
    ppermute x1 -> x2, waiting for transfers between devices: 1.89 us -> 0.01 us  [local(): got = lax.ppermute(send, 'c', flip(C))]
    pallas_call x1 -> x2, Pallas kernels: 6.75 us -> 8.25 us  [partials(): pl.pallas_call(functools.partial(project, base), out_shape=(out, out), gr...]
  transfers between devices with their start and end apart: 18 -> 19, of which waited for: 10 -> 9; matrix products, arithmetic and copies ran while one was open for 7% -> 7% of each run, Pallas kernels for 2% -> 5%
where the time goes in v7:
time: 139 us; the launch traced here: 138 us
  starting transfers between devices  60 us (43%)
  waiting for transfers between devices  39 us (28%)
  between operations  13.8 us (10%)
  local copies, waits for them, and re-layouts  13.2 us (9%)
  Pallas kernels  11.3 us (8%)
    ppermute x2, waiting for transfers between devices, local(): swapped = [lax.ppermute(v, 'p', flip(ZP)) for v in jnp.split(own, 2)]  22.4 us
    ppermute x4, starting transfers between devices, sent(): return lax.ppermute(value, ('p', 'zh', 'c'), pairs)  16 us
    ppermute x3, starting transfers between devices, moved(): lax.ppermute(added(d).astype(jnp.bfloat16), 'x', shift).astype(jnp.float32)  9.88 us
    ppermute x2, starting transfers between devices, local(): swapped = [lax.ppermute(v, 'p', flip(ZP)) for v in jnp.split(own, 2)]  9.67 us
    pallas_call x2, Pallas kernels, partials(): pl.pallas_call(functools.partial(project, base), out_shape=(out, out), gr...  8.25 us
    ppermute x4, waiting for transfers between devices, sent(): return lax.ppermute(value, ('p', 'zh', 'c'), pairs)  5.96 us
    gather x4, local copies, waits for them, and re-layouts, taken(): return table[adapters(i, j)].reshape(-1, table.shape[2])  5.62 us
    ppermute x2, starting transfers between devices, local(): swapped_pair = [lax.ppermute(v, 'x', flip(X)) for v in swapped]  5.61 us
  transfers between devices with their start and end apart: 19, of which 9 were waited for; matrix products, arithmetic and copies ran while one was open for 7% of the time, Pallas kernels for 5%

profile of v7, /device:TPU:1, one launch (start us, length us, event | category | flops | bytes accessed | tf_op | source)
XLA Modules:
  0.0 138.5 jit_solution(10237906983340867606)
XLA Ops:
  6.5 1.7 %collective-permute-start = (bf16[128,1024]{1,0:T(8,128)(2,1)}, bf16[128,1024]{1,0:T(8,128)(2,1)S(1)}, u32[]{:S(2)}, u32[]{:S(2)}) collective-permute-start(bf16[128,1024]{1,0:T(8,128)(2,1)} %param.5), channel_id=1, source_target_pairs={{0,0},{4,16},{8,8},{12,24},{16,4},{20,20},{24,12},{28,28},{1,1},{5... | collective-permute-start | bytes 786440 | tf_op jit(solution)/shard_map/ppermute | solution.py:185
  8.3 5.4 %collective-permute-start.1 = (bf16[128,1024]{1,0:T(8,128)(2,1)}, bf16[128,1024]{1,0:T(8,128)(2,1)S(1)}, u32[]{:S(2)}, u32[]{:S(2)}) collective-permute-start(bf16[128,1024]{1,0:T(8,128)(2,1)} %param.5), channel_id=1, source_target_pairs={{0,16},{4,0},{8,24},{12,8},{16,20},{20,4},{24,28},{28,12},{1,17},{... | collective-permute-start | bytes 786440 | tf_op jit(solution)/shard_map/ppermute | solution.py:188
  13.7 4.8 %collective-permute-done.1.second = bf16[128,1024]{1,0:T(8,128)(2,1)S(1)} collective-permute-done((bf16[128,1024]{1,0:T(8,128)(2,1)}, bf16[128,1024]{1,0:T(8,128)(2,1)S(1)}, u32[]{:S(2)}, u32[]{:S(2)}) %collective-permute-start.1) | collective-permute-done | bytes 262176 | tf_op jit(solution)/shard_map/ppermute | solution.py:188
  19.5 2.1 %fusion.8 = (bf16[512,384]{1,0:T(8,128)(2,1)}, bf16[512,384]{1,0:T(8,128)(2,1)}) fusion(bf16[1024,384]{1,0:T(8,128)(2,1)} %refs_0_.1), kind=kLoop, calls=%fused_computation.33 | loop fusion | bytes 1572864 | tf_op jit(solution)/shard_map/split | solution.py:208
  21.6 7.7 %collective-permute-start.2 = (bf16[512,384]{1,0:T(8,128)(2,1)}, bf16[512,384]{1,0:T(8,128)(2,1)S(1)}, u32[]{:S(2)}, u32[]{:S(2)}) collective-permute-start(bf16[512,384]{1,0:T(8,128)(2,1)} %get-tuple-element.19), channel_id=1, source_target_pairs={{0,32},{32,0},{1,33},{33,1},{2,34},{34,2},{3,35},{35,3},{4,36},{36... | collective-permute-start | bytes 1179656 | tf_op jit(solution)/shard_map/ppermute | solution.py:208
  29.3 1.9 %collective-permute-start.3 = (bf16[512,384]{1,0:T(8,128)(2,1)}, bf16[512,384]{1,0:T(8,128)(2,1)}, u32[]{:S(2)}, u32[]{:S(2)}) collective-permute-start(bf16[512,384]{1,0:T(8,128)(2,1)} %get-tuple-element.18), channel_id=1, source_target_pairs={{0,32},{32,0},{1,33},{33,1},{2,34},{34,2},{3,35},{35,3},{4,36},{36... | collective-permute-start | bytes 1179656 | tf_op jit(solution)/shard_map/ppermute | solution.py:208
  31.2 3.0 %collective-permute-start.4 = (bf16[1024,384]{1,0:T(8,128)(2,1)}, bf16[1024,384]{1,0:T(8,128)(2,1)S(1)}, u32[]{:S(2)}, u32[]{:S(2)}) collective-permute-start(bf16[1024,384]{1,0:T(8,128)(2,1)} %refs_0_.1), channel_id=1, source_target_pairs={{0,4},{4,0},{8,12},{12,8},{1,5},{5,1},{9,13},{13,9},{2,6},{6,2},{1... | collective-permute-start | bytes 2359304 | tf_op jit(solution)/shard_map/ppermute | solution.py:207
  37.0 2.2 %collective-permute-start.8 = (bf16[128,1024]{1,0:T(8,128)(2,1)}, bf16[128,1024]{1,0:T(8,128)(2,1)}, u32[]{:S(2)}, u32[]{:S(2)}) collective-permute-start(bf16[128,1024]{1,0:T(8,128)(2,1)} %bitcast.10), channel_id=1, source_target_pairs={{0,4},{4,0},{8,12},{12,8},{1,5},{5,1},{9,13},{13,9},{2,6},{6,2},{1... | collective-permute-start | bytes 786440 | tf_op jit(solution)/shard_map/ppermute | solution.py:202
  39.2 16.8 %collective-permute-done.2.refs_1_ = bf16[512,384]{1,0:T(8,128)(2,1)S(1)} collective-permute-done((bf16[512,384]{1,0:T(8,128)(2,1)}, bf16[512,384]{1,0:T(8,128)(2,1)S(1)}, u32[]{:S(2)}, u32[]{:S(2)}) %collective-permute-start.2) | collective-permute-done | bytes 393248 | tf_op jit(solution)/shard_map/ppermute | solution.py:208
  56.0 2.8 %collective-permute-start.5 = (bf16[512,384]{1,0:T(8,128)(2,1)S(1)}, bf16[512,384]{1,0:T(8,128)(2,1)}, u32[]{:S(2)}, u32[]{:S(2)}) collective-permute-start(bf16[512,384]{1,0:T(8,128)(2,1)S(1)} %collective-permute-done.2.refs_1_), channel_id=1, source_target_pairs={{0,4},{4,0},{8,12},{12,8},{1,5},{5,1},{9,13},{13,9},{2,6},{6,2},{1... | collective-permute-start | bytes 1179656 | tf_op jit(solution)/shard_map/ppermute | solution.py:209
  58.8 5.6 %collective-permute-done.3.refs_2_ = bf16[512,384]{1,0:T(8,128)(2,1)} collective-permute-done((bf16[512,384]{1,0:T(8,128)(2,1)}, bf16[512,384]{1,0:T(8,128)(2,1)}, u32[]{:S(2)}, u32[]{:S(2)}) %collective-permute-start.3) | collective-permute-done | bytes 393248 | tf_op jit(solution)/shard_map/ppermute | solution.py:208
  64.4 2.8 %collective-permute-start.6 = (bf16[512,384]{1,0:T(8,128)(2,1)}, bf16[512,384]{1,0:T(8,128)(2,1)}, u32[]{:S(2)}, u32[]{:S(2)}) collective-permute-start(bf16[512,384]{1,0:T(8,128)(2,1)} %collective-permute-done.3.refs_2_), channel_id=1, source_target_pairs={{0,4},{4,0},{8,12},{12,8},{1,5},{5,1},{9,13},{13,9},{2,6},{6,2},{1... | collective-permute-start | bytes 1179656 | tf_op jit(solution)/shard_map/ppermute | solution.py:209
  67.3 2.2 %gather_fusion.1 = bf16[8,16,384]{2,1,0:T(8,128)(2,1)} fusion(bf16[32,16,384]{2,1,0:T(8,128)(2,1)} %param.8, s32[1024]{0:T(1024)S(1)} %pad_clamp_fusion.1), kind=kCustom, calls=%fused_computation.1 | custom fusion | bytes 196640 | tf_op jit(solution)/shard_map/gather | solution.py:199
  69.5 1.9 %collective-permute-start.7 = (bf16[128,384]{1,0:T(8,128)(2,1)}, bf16[128,384]{1,0:T(8,128)(2,1)S(1)}, u32[]{:S(2)}, u32[]{:S(2)}) collective-permute-start(bf16[128,384]{1,0:T(8,128)(2,1)} %bitcast.7), channel_id=1, source_target_pairs={{0,32},{32,0},{1,33},{33,1},{2,34},{34,2},{3,35},{35,3},{4,36},{36... | collective-permute-start | bytes 294920 | tf_op jit(solution)/shard_map/ppermute | solution.py:204
  73.7 2.7 %collective-permute-done.7.refs_7_ = bf16[128,384]{1,0:T(8,128)(2,1)S(1)} collective-permute-done((bf16[128,384]{1,0:T(8,128)(2,1)}, bf16[128,384]{1,0:T(8,128)(2,1)S(1)}, u32[]{:S(2)}, u32[]{:S(2)}) %collective-permute-start.7) | collective-permute-done | bytes 98336 | tf_op jit(solution)/shard_map/ppermute | solution.py:204
  76.8 2.2 %shard_map.56.table = bf16[2688,768]{1,0:T(8,128)(2,1)S(1)} custom-call(s32[2]{0:T(128)S(1)} %pad_add_fusion.slots, bf16[1024,384]{1,0:T(8,128)(2,1)S(1)} %copy-done.3, bf16[512,384]{1,0:T(8,128)(2,1)S(1)} %collective-permute-done.2.refs_1_, bf16[512,384]{1,0:T(8,128)(2,1)} %collective-permute-done.3.refs_2_, ...), custom_call_target="tpu_custom_call" | custom-call | tf_op jit(solution)/shard_map/pallas_call | solution.py:84
  79.0 2.0 %copy-done.1 = bf16[2688,768]{1,0:T(8,128)(2,1)} copy-done((bf16[2688,768]{1,0:T(8,128)(2,1)}, bf16[2688,768]{1,0:T(8,128)(2,1)S(1)}, u32[]{:S(2)}) %copy-start.1) | copy-done | bytes 4128792
  81.0 2.6 %all-gather.3.cloned.1.call-done = bf16[1024,2048]{1,0:T(8,128)(2,1)} async-done(((bf16[128,2048]{1,0:T(8,128)(2,1)}), bf16[1024,2048]{1,0:T(8,128)(2,1)}) %all-gather.3.cloned.1.call-update) | async-done | bytes 4194320 | tf_op jit(solution)/shard_map/all_gather | solution.py:191
  83.6 2.2 %copy-done.2 = bf16[2688,768]{1,0:T(8,128)(2,1)S(1)} copy-done((bf16[2688,768]{1,0:T(8,128)(2,1)S(1)}, bf16[2688,768]{1,0:T(8,128)(2,1)}, u32[]{:S(2)}) %copy-start.2) | copy-done | bytes 4128792
  85.8 4.1 %shard_map.58 = (bf16[2,256,384]{2,1,0:T(8,128)(2,1)S(1)}, bf16[2,256,384]{2,1,0:T(8,128)(2,1)S(1)}) custom-call(s32[1]{0:T(128)} %bitcast.order, bf16[8,128,2048]{2,1,0:T(8,128)(2,1)} %bitcast.37, bf16[2688,768]{1,0:T(8,128)(2,1)S(1)} %copy-done.2), custom_call_target="tpu_custom_call" | custom-call | flops 1610612736 | bytes 7012352 | tf_op jit(solution)/shard_map/pallas_call | solution.py:143
  89.9 2.6 %collective-permute-start.10 = (bf16[2,256,384]{2,1,0:T(8,128)(2,1)S(1)}, bf16[2,256,384]{2,1,0:T(8,128)(2,1)S(1)}, u32[]{:S(2)}, u32[]{:S(2)}) collective-permute-start(bf16[2,256,384]{2,1,0:T(8,128)(2,1)S(1)} %get-tuple-element.12), channel_id=1, source_target_pairs={{0,1},{1,0},{2,3},{3,2},{4,5},{5,4},{6,7},{7,6},{8,9},{9,8},{10,11... | collective-permute-start | bytes 1179656 | tf_op jit(solution)/shard_map/ppermute | solution.py:218
  92.5 4.1 %shard_map.57 = (bf16[2,256,384]{2,1,0:T(8,128)(2,1)S(1)}, bf16[2,256,384]{2,1,0:T(8,128)(2,1)S(1)}) custom-call(s32[1]{0:T(128)} %bitcast.order, bf16[8,128,2048]{2,1,0:T(8,128)(2,1)} %bitcast.38, bf16[2688,768]{1,0:T(8,128)(2,1)S(1)} %copy-done.2), custom_call_target="tpu_custom_call" | custom-call | flops 1610612736 | bytes 7012352 | tf_op jit(solution)/shard_map/pallas_call | solution.py:143
  96.6 1.9 %collective-permute-start.9 = (bf16[2,256,384]{2,1,0:T(8,128)(2,1)S(1)}, bf16[2,256,384]{2,1,0:T(8,128)(2,1)S(1)}, u32[]{:S(2)}, u32[]{:S(2)}) collective-permute-start(bf16[2,256,384]{2,1,0:T(8,128)(2,1)S(1)} %get-tuple-element.10), channel_id=1, source_target_pairs={{0,1},{1,0},{2,3},{3,2},{4,5},{5,4},{6,7},{7,6},{8,9},{9,8},{10,11... | collective-permute-start | bytes 1179656 | tf_op jit(solution)/shard_map/ppermute | solution.py:218
  98.7 4.6 %collective-permute-start.11 = (bf16[256,384]{1,0:T(8,128)(2,1)S(1)}, bf16[256,384]{1,0:T(8,128)(2,1)S(1)}, u32[]{:S(2)}, u32[]{:S(2)}) collective-permute-start(bf16[256,384]{1,0:T(8,128)(2,1)S(1)} %get-tuple-element.16), channel_id=1, source_target_pairs={{0,8},{4,12},{8,0},{12,4},{1,9},{5,13},{9,1},{13,5},{2,10},{6,14},... | collective-permute-start | bytes 589832 | tf_op jit(solution)/shard_map/ppermute | solution.py:227
  103.3 2.8 %collective-permute-start.13 = (bf16[256,384]{1,0:T(8,128)(2,1)S(1)}, bf16[256,384]{1,0:T(8,128)(2,1)S(1)}, u32[]{:S(2)}, u32[]{:S(2)}) collective-permute-start(bf16[256,384]{1,0:T(8,128)(2,1)S(1)} %get-tuple-element.17), channel_id=1, source_target_pairs={{0,12},{4,0},{8,4},{12,8},{1,13},{5,1},{9,5},{13,9},{2,14},{6,2},{... | collective-permute-start | bytes 589832 | tf_op jit(solution)/shard_map/ppermute | solution.py:227
  106.2 2.5 %collective-permute-start.14 = (bf16[256,384]{1,0:T(8,128)(2,1)S(1)}, bf16[256,384]{1,0:T(8,128)(2,1)S(1)}, u32[]{:S(2)}, u32[]{:S(2)}) collective-permute-start(bf16[256,384]{1,0:T(8,128)(2,1)S(1)} %fusion.4), channel_id=1, source_target_pairs={{0,4},{4,8},{8,12},{12,0},{1,5},{5,9},{9,13},{13,1},{2,6},{6,10},{... | collective-permute-start | bytes 589832 | tf_op jit(solution)/shard_map/ppermute | solution.py:227
  108.8 7.5 %collective-permute-start.12 = (bf16[128,384]{1,0:T(8,128)(2,1)S(1)}, bf16[128,384]{1,0:T(8,128)(2,1)S(1)}, u32[]{:S(2)}, u32[]{:S(2)}) collective-permute-start(bf16[128,384]{1,0:T(8,128)(2,1)S(1)} %get-tuple-element.21), channel_id=1, source_target_pairs={{0,2},{1,34},{2,0},{3,32},{32,3},{33,35},{34,1},{35,33},{4,6},{5,3... | collective-permute-start | bytes 294920 | tf_op jit(solution)/shard_map/ppermute | solution.py:240
  116.3 2.7 %collective-permute-start.16 = (bf16[128,384]{1,0:T(8,128)(2,1)S(1)}, bf16[128,384]{1,0:T(8,128)(2,1)S(1)}, u32[]{:S(2)}, u32[]{:S(2)}) collective-permute-start(bf16[128,384]{1,0:T(8,128)(2,1)S(1)} %get-tuple-element.20), channel_id=1, source_target_pairs={{0,0},{1,32},{2,2},{3,34},{32,1},{33,33},{34,3},{35,35},{4,4},{5,3... | collective-permute-start | bytes 294920 | tf_op jit(solution)/shard_map/ppermute | solution.py:240
  119.1 3.7 %collective-permute-start.15 = (bf16[128,384]{1,0:T(8,128)(2,1)S(1)}, bf16[128,384]{1,0:T(8,128)(2,1)S(1)}, u32[]{:S(2)}, u32[]{:S(2)}) collective-permute-start(bf16[128,384]{1,0:T(8,128)(2,1)S(1)} %get-tuple-element.23), channel_id=1, source_target_pairs={{0,2},{1,34},{2,0},{3,32},{32,3},{33,35},{34,1},{35,33},{4,6},{5,3... | collective-permute-start | bytes 294920 | tf_op jit(solution)/shard_map/ppermute | solution.py:240
  122.9 2.0 %collective-permute-start.17 = (bf16[128,384]{1,0:T(8,128)(2,1)S(1)}, bf16[128,384]{1,0:T(8,128)(2,1)S(1)}, u32[]{:S(2)}, u32[]{:S(2)}) collective-permute-start(bf16[128,384]{1,0:T(8,128)(2,1)S(1)} %get-tuple-element.22), channel_id=1, source_target_pairs={{0,0},{1,32},{2,2},{3,34},{32,1},{33,33},{34,3},{35,35},{4,4},{5,3... | collective-permute-start | bytes 294920 | tf_op jit(solution)/shard_map/ppermute | solution.py:240
  125.9 1.7 %collective-permute-done.15 = bf16[128,384]{1,0:T(8,128)(2,1)S(1)} collective-permute-done((bf16[128,384]{1,0:T(8,128)(2,1)S(1)}, bf16[128,384]{1,0:T(8,128)(2,1)S(1)}, u32[]{:S(2)}, u32[]{:S(2)}) %collective-permute-start.15) | collective-permute-done | bytes 98336 | tf_op jit(solution)/shard_map/ppermute | solution.py:240
  127.6 3.3 %collective-permute-done.17 = bf16[128,384]{1,0:T(8,128)(2,1)S(1)} collective-permute-done((bf16[128,384]{1,0:T(8,128)(2,1)S(1)}, bf16[128,384]{1,0:T(8,128)(2,1)S(1)}, u32[]{:S(2)}, u32[]{:S(2)}) %collective-permute-start.17) | collective-permute-done | bytes 98336 | tf_op jit(solution)/shard_map/ppermute | solution.py:240
  (40 shorter events, 8.3 us)
Async XLA Ops:
  6.5 29.2 %copy-start = (bf16[32,16,1024]{2,1,0:T(8,128)(2,1)S(1)}, bf16[32,16,1024]{2,1,0:T(8,128)(2,1)}, u32[]{:S(2)}) copy-start(bf16[32,16,1024]{2,1,0:T(8,128)(2,1)} %param.7) | copy-start | bytes 3145732
  6.5 70.3 %copy-start.3 = (bf16[1024,384]{1,0:T(8,128)(2,1)S(1)}, bf16[1024,384]{1,0:T(8,128)(2,1)}, u32[]{:S(2)}) copy-start(bf16[1024,384]{1,0:T(8,128)(2,1)} %refs_0_.1) | copy-start | bytes 2359300
  6.5 77.1 %all-gather.3.cloned.1.call-start = ((), (), s32[]{:S(2)}) async-start(), calls=%async_computation | async-start | bytes 4718592 | tf_op jit(solution)/shard_map/all_gather | solution.py:191
  6.5 7.2 %collective-permute-start = (bf16[128,1024]{1,0:T(8,128)(2,1)}, bf16[128,1024]{1,0:T(8,128)(2,1)S(1)}, u32[]{:S(2)}, u32[]{:S(2)}) collective-permute-start(bf16[128,1024]{1,0:T(8,128)(2,1)} %param.5), channel_id=1, source_target_pairs={{0,0},{4,16},{8,8},{12,24},{16,4},{20,20},{24,12},{28,28},{1,1},{5... | collective-permute-start | bytes 786440 | tf_op jit(solution)/shard_map/ppermute | solution.py:185
  8.3 10.3 %collective-permute-start.1 = (bf16[128,1024]{1,0:T(8,128)(2,1)}, bf16[128,1024]{1,0:T(8,128)(2,1)S(1)}, u32[]{:S(2)}, u32[]{:S(2)}) collective-permute-start(bf16[128,1024]{1,0:T(8,128)(2,1)} %param.5), channel_id=1, source_target_pairs={{0,16},{4,0},{8,24},{12,8},{16,20},{20,4},{24,28},{28,12},{1,17},{... | collective-permute-start | bytes 786440 | tf_op jit(solution)/shard_map/ppermute | solution.py:188
  21.6 34.5 %collective-permute-start.2 = (bf16[512,384]{1,0:T(8,128)(2,1)}, bf16[512,384]{1,0:T(8,128)(2,1)S(1)}, u32[]{:S(2)}, u32[]{:S(2)}) collective-permute-start(bf16[512,384]{1,0:T(8,128)(2,1)} %get-tuple-element.19), channel_id=1, source_target_pairs={{0,32},{32,0},{1,33},{33,1},{2,34},{34,2},{3,35},{35,3},{4,36},{36... | collective-permute-start | bytes 1179656 | tf_op jit(solution)/shard_map/ppermute | solution.py:208
  29.3 35.1 %collective-permute-start.3 = (bf16[512,384]{1,0:T(8,128)(2,1)}, bf16[512,384]{1,0:T(8,128)(2,1)}, u32[]{:S(2)}, u32[]{:S(2)}) collective-permute-start(bf16[512,384]{1,0:T(8,128)(2,1)} %get-tuple-element.18), channel_id=1, source_target_pairs={{0,32},{32,0},{1,33},{33,1},{2,34},{34,2},{3,35},{35,3},{4,36},{36... | collective-permute-start | bytes 1179656 | tf_op jit(solution)/shard_map/ppermute | solution.py:208
  31.2 45.6 %collective-permute-start.4 = (bf16[1024,384]{1,0:T(8,128)(2,1)}, bf16[1024,384]{1,0:T(8,128)(2,1)S(1)}, u32[]{:S(2)}, u32[]{:S(2)}) collective-permute-start(bf16[1024,384]{1,0:T(8,128)(2,1)} %refs_0_.1), channel_id=1, source_target_pairs={{0,4},{4,0},{8,12},{12,8},{1,5},{5,1},{9,13},{13,9},{2,6},{6,2},{1... | collective-permute-start | bytes 2359304 | tf_op jit(solution)/shard_map/ppermute | solution.py:207
  37.0 39.3 %collective-permute-start.8 = (bf16[128,1024]{1,0:T(8,128)(2,1)}, bf16[128,1024]{1,0:T(8,128)(2,1)}, u32[]{:S(2)}, u32[]{:S(2)}) collective-permute-start(bf16[128,1024]{1,0:T(8,128)(2,1)} %bitcast.10), channel_id=1, source_target_pairs={{0,4},{4,0},{8,12},{12,8},{1,5},{5,1},{9,13},{13,9},{2,6},{6,2},{1... | collective-permute-start | bytes 786440 | tf_op jit(solution)/shard_map/ppermute | solution.py:202
  56.0 20.3 %collective-permute-start.5 = (bf16[512,384]{1,0:T(8,128)(2,1)S(1)}, bf16[512,384]{1,0:T(8,128)(2,1)}, u32[]{:S(2)}, u32[]{:S(2)}) collective-permute-start(bf16[512,384]{1,0:T(8,128)(2,1)S(1)} %collective-permute-done.2.refs_1_), channel_id=1, source_target_pairs={{0,4},{4,0},{8,12},{12,8},{1,5},{5,1},{9,13},{13,9},{2,6},{6,2},{1... | collective-permute-start | bytes 1179656 | tf_op jit(solution)/shard_map/ppermute | solution.py:209
  64.4 12.4 %collective-permute-start.6 = (bf16[512,384]{1,0:T(8,128)(2,1)}, bf16[512,384]{1,0:T(8,128)(2,1)}, u32[]{:S(2)}, u32[]{:S(2)}) collective-permute-start(bf16[512,384]{1,0:T(8,128)(2,1)} %collective-permute-done.3.refs_2_), channel_id=1, source_target_pairs={{0,4},{4,0},{8,12},{12,8},{1,5},{5,1},{9,13},{13,9},{2,6},{6,2},{1... | collective-permute-start | bytes 1179656 | tf_op jit(solution)/shard_map/ppermute | solution.py:209
  69.5 6.9 %collective-permute-start.7 = (bf16[128,384]{1,0:T(8,128)(2,1)}, bf16[128,384]{1,0:T(8,128)(2,1)S(1)}, u32[]{:S(2)}, u32[]{:S(2)}) collective-permute-start(bf16[128,384]{1,0:T(8,128)(2,1)} %bitcast.7), channel_id=1, source_target_pairs={{0,32},{32,0},{1,33},{33,1},{2,34},{34,2},{3,35},{35,3},{4,36},{36... | collective-permute-start | bytes 294920 | tf_op jit(solution)/shard_map/ppermute | solution.py:204
  79.0 2.0 %copy-start.1 = (bf16[2688,768]{1,0:T(8,128)(2,1)}, bf16[2688,768]{1,0:T(8,128)(2,1)S(1)}, u32[]{:S(2)}) copy-start(bf16[2688,768]{1,0:T(8,128)(2,1)S(1)} %shard_map.56.table) | copy-start | bytes 12386308
  83.6 2.2 %copy-start.2 = (bf16[2688,768]{1,0:T(8,128)(2,1)S(1)}, bf16[2688,768]{1,0:T(8,128)(2,1)}, u32[]{:S(2)}) copy-start(bf16[2688,768]{1,0:T(8,128)(2,1)} %copy-done.1) | copy-start | bytes 12386308
  89.9 8.7 %collective-permute-start.10 = (bf16[2,256,384]{2,1,0:T(8,128)(2,1)S(1)}, bf16[2,256,384]{2,1,0:T(8,128)(2,1)S(1)}, u32[]{:S(2)}, u32[]{:S(2)}) collective-permute-start(bf16[2,256,384]{2,1,0:T(8,128)(2,1)S(1)} %get-tuple-element.12), channel_id=1, source_target_pairs={{0,1},{1,0},{2,3},{3,2},{4,5},{5,4},{6,7},{7,6},{8,9},{9,8},{10,11... | collective-permute-start | bytes 1179656 | tf_op jit(solution)/shard_map/ppermute | solution.py:218
  96.6 9.5 %collective-permute-start.9 = (bf16[2,256,384]{2,1,0:T(8,128)(2,1)S(1)}, bf16[2,256,384]{2,1,0:T(8,128)(2,1)S(1)}, u32[]{:S(2)}, u32[]{:S(2)}) collective-permute-start(bf16[2,256,384]{2,1,0:T(8,128)(2,1)S(1)} %get-tuple-element.10), channel_id=1, source_target_pairs={{0,1},{1,0},{2,3},{3,2},{4,5},{5,4},{6,7},{7,6},{8,9},{9,8},{10,11... | collective-permute-start | bytes 1179656 | tf_op jit(solution)/shard_map/ppermute | solution.py:218
  98.7 10.0 %collective-permute-start.11 = (bf16[256,384]{1,0:T(8,128)(2,1)S(1)}, bf16[256,384]{1,0:T(8,128)(2,1)S(1)}, u32[]{:S(2)}, u32[]{:S(2)}) collective-permute-start(bf16[256,384]{1,0:T(8,128)(2,1)S(1)} %get-tuple-element.16), channel_id=1, source_target_pairs={{0,8},{4,12},{8,0},{12,4},{1,9},{5,13},{9,1},{13,5},{2,10},{6,14},... | collective-permute-start | bytes 589832 | tf_op jit(solution)/shard_map/ppermute | solution.py:227
  103.3 15.7 %collective-permute-start.13 = (bf16[256,384]{1,0:T(8,128)(2,1)S(1)}, bf16[256,384]{1,0:T(8,128)(2,1)S(1)}, u32[]{:S(2)}, u32[]{:S(2)}) collective-permute-start(bf16[256,384]{1,0:T(8,128)(2,1)S(1)} %get-tuple-element.17), channel_id=1, source_target_pairs={{0,12},{4,0},{8,4},{12,8},{1,13},{5,1},{9,5},{13,9},{2,14},{6,2},{... | collective-permute-start | bytes 589832 | tf_op jit(solution)/shard_map/ppermute | solution.py:227
  106.2 12.9 %collective-permute-start.14 = (bf16[256,384]{1,0:T(8,128)(2,1)S(1)}, bf16[256,384]{1,0:T(8,128)(2,1)S(1)}, u32[]{:S(2)}, u32[]{:S(2)}) collective-permute-start(bf16[256,384]{1,0:T(8,128)(2,1)S(1)} %fusion.4), channel_id=1, source_target_pairs={{0,4},{4,8},{8,12},{12,0},{1,5},{5,9},{9,13},{13,1},{2,6},{6,10},{... | collective-permute-start | bytes 589832 | tf_op jit(solution)/shard_map/ppermute | solution.py:227
  108.8 16.1 %collective-permute-start.12 = (bf16[128,384]{1,0:T(8,128)(2,1)S(1)}, bf16[128,384]{1,0:T(8,128)(2,1)S(1)}, u32[]{:S(2)}, u32[]{:S(2)}) collective-permute-start(bf16[128,384]{1,0:T(8,128)(2,1)S(1)} %get-tuple-element.21), channel_id=1, source_target_pairs={{0,2},{1,34},{2,0},{3,32},{32,3},{33,35},{34,1},{35,33},{4,6},{5,3... | collective-permute-start | bytes 294920 | tf_op jit(solution)/shard_map/ppermute | solution.py:240
  116.3 9.6 %collective-permute-start.16 = (bf16[128,384]{1,0:T(8,128)(2,1)S(1)}, bf16[128,384]{1,0:T(8,128)(2,1)S(1)}, u32[]{:S(2)}, u32[]{:S(2)}) collective-permute-start(bf16[128,384]{1,0:T(8,128)(2,1)S(1)} %get-tuple-element.20), channel_id=1, source_target_pairs={{0,0},{1,32},{2,2},{3,34},{32,1},{33,33},{34,3},{35,35},{4,4},{5,3... | collective-permute-start | bytes 294920 | tf_op jit(solution)/shard_map/ppermute | solution.py:240
  119.1 8.4 %collective-permute-start.15 = (bf16[128,384]{1,0:T(8,128)(2,1)S(1)}, bf16[128,384]{1,0:T(8,128)(2,1)S(1)}, u32[]{:S(2)}, u32[]{:S(2)}) collective-permute-start(bf16[128,384]{1,0:T(8,128)(2,1)S(1)} %get-tuple-element.23), channel_id=1, source_target_pairs={{0,2},{1,34},{2,0},{3,32},{32,3},{33,35},{34,1},{35,33},{4,6},{5,3... | collective-permute-start | bytes 294920 | tf_op jit(solution)/shard_map/ppermute | solution.py:240
  122.9 8.0 %collective-permute-start.17 = (bf16[128,384]{1,0:T(8,128)(2,1)S(1)}, bf16[128,384]{1,0:T(8,128)(2,1)S(1)}, u32[]{:S(2)}, u32[]{:S(2)}) collective-permute-start(bf16[128,384]{1,0:T(8,128)(2,1)S(1)} %get-tuple-element.22), channel_id=1, source_target_pairs={{0,0},{1,32},{2,2},{3,34},{32,1},{33,33},{34,3},{35,35},{4,4},{5,3... | collective-permute-start | bytes 294920 | tf_op jit(solution)/shard_map/ppermute | solution.py:240
Sparse Core Ops, SparseCore 0:
  19.6 63.9 all-gather.2

commit v8 on v6

--- a/solution.py
+++ b/solution.py
@@ -10,7 +10,7 @@
 DP, TENSOR = ("y", "p", "q"), ("x", "zh", "c")
 VMEM_BYTES = 48_000_000
 SMALL_VMEM_BYTES = 16_000_000
-DOWN_COLUMNS = 512
+DOWN_COLUMNS = 768
 
 
 def flip(size):
@@ -69,16 +69,16 @@
     move(up_swapped, 2 * features, other)
     ranks = down_own.shape[0]
     for k, v in ((slots[0], down_own), (1 - slots[0], down_pair)):
-        for i in range(features // DOWN_COLUMNS):
-            row = 2 * features + ranks * (1 + k * (features // DOWN_COLUMNS) + i)
-            move(v.at[:, pl.ds(i * DOWN_COLUMNS, DOWN_COLUMNS)], row, 0)
+        rest = features - DOWN_COLUMNS
+        move(v.at[:, pl.ds(0, DOWN_COLUMNS)], 2 * features + ranks * (1 + k), 0)
+        move(v.at[:, pl.ds(DOWN_COLUMNS, rest)], 2 * features + ranks * 3, k * rest)
     copied(moves)
 
 
 def placed(slots, parts):
     features, columns = parts[0].shape
     ranks = parts[-1].shape[0]
-    down_rows = 2 * features // DOWN_COLUMNS * ranks
+    down_rows = 3 * ranks
     return pl.pallas_call(
         place_weights,
         out_shape=pltpu.VMEM((2 * features + ranks + down_rows, 2 * columns), parts[0].dtype),
@@ -114,15 +114,20 @@
         fetch(t).wait()
     for t in here:
         shrink = 0.0
-        for i in range(features // DOWN_COLUMNS):
-            at = slice(i * DOWN_COLUMNS, (i + 1) * DOWN_COLUMNS)
-            start = features + (1 + i) * ranks
-            shrink += lax.dot_general(
-                held[t, :, :, at].reshape(tile_rows, DOWN_COLUMNS),
-                table[start : start + ranks, :DOWN_COLUMNS],
-                (((1,), (1,)), ((), ())),
-                preferred_element_type=jnp.float32,
-            )
+        part = features // 2
+        rest = part - DOWN_COLUMNS
+        for k in range(2):
+            for row, col, begin, count in (
+                (1 + k, 0, k * part, DOWN_COLUMNS),
+                (3, k * rest, k * part + DOWN_COLUMNS, rest),
+            ):
+                start = features + row * ranks
+                shrink += lax.dot_general(
+                    held[t, :, :, begin : begin + count].reshape(tile_rows, count),
+                    table[start : start + ranks, col : col + count],
+                    (((1,), (1,)), ((), ())),
+                    preferred_element_type=jnp.float32,
+                )
         block = lax.broadcasted_iota(jnp.int32, shrink.shape, 0) // rows
         block += (t + order[0]) % X * groups
         adapter = lax.broadcasted_iota(jnp.int32, shrink.shape, 1) // rank

time: 137 us -> 137 us (level)
  no operation moved by 1% of the time
where the time goes in v8:
time: 137 us
  starting transfers between devices  58.2 us (42%)
  waiting for transfers between devices  40.7 us (30%)
  between operations  13.8 us (10%)
  local copies, waits for them, and re-layouts  13.1 us (10%)
  Pallas kernels  9.73 us (7%)
    ppermute x2, waiting for transfers between devices, local(): swapped = [lax.ppermute(v, 'p', flip(ZP)) for v in jnp.split(own, 2)]  22.4 us
    ppermute x4, starting transfers between devices, sent(): return lax.ppermute(value, ('p', 'zh', 'c'), pairs)  16.1 us
    ppermute x3, starting transfers between devices, moved(): lax.ppermute(added(d).astype(jnp.bfloat16), 'x', shift).astype(jnp.float32)  9.9 us
    ppermute x2, starting transfers between devices, local(): swapped = [lax.ppermute(v, 'p', flip(ZP)) for v in jnp.split(own, 2)]  9.67 us
    pallas_call x1, Pallas kernels, partials(): pl.pallas_call(project, out_shape=(out, out), grid_spec=pltpu.PrefetchSca...  6.74 us
    ppermute x4, waiting for transfers between devices, sent(): return lax.ppermute(value, ('p', 'zh', 'c'), pairs)  5.72 us
    ppermute x2, starting transfers between devices, local(): swapped_pair = [lax.ppermute(v, 'x', flip(X)) for v in swapped]  5.61 us
    gather x4, local copies, waits for them, and re-layouts, taken(): return table[adapters(i, j)].reshape(-1, table.shape[2])  5.61 us
  transfers between devices with their start and end apart: 18, of which 10 were waited for; matrix products, arithmetic and copies ran while one was open for 7% of the time, Pallas kernels for 2%

profile of v8, /device:TPU:1, one launch (start us, length us, event | category | flops | bytes accessed | tf_op | source)
XLA Modules:
  0.0 136.7 jit_solution(6153841640885868129)
XLA Ops:
  6.5 1.7 %collective-permute-start = (bf16[128,1024]{1,0:T(8,128)(2,1)}, bf16[128,1024]{1,0:T(8,128)(2,1)S(1)}, u32[]{:S(2)}, u32[]{:S(2)}) collective-permute-start(bf16[128,1024]{1,0:T(8,128)(2,1)} %param.5), channel_id=1, source_target_pairs={{0,0},{4,16},{8,8},{12,24},{16,4},{20,20},{24,12},{28,28},{1,1},{5... | collective-permute-start | bytes 786440 | tf_op jit(solution)/shard_map/ppermute | solution.py:192
  8.3 5.4 %collective-permute-start.1 = (bf16[128,1024]{1,0:T(8,128)(2,1)}, bf16[128,1024]{1,0:T(8,128)(2,1)S(1)}, u32[]{:S(2)}, u32[]{:S(2)}) collective-permute-start(bf16[128,1024]{1,0:T(8,128)(2,1)} %param.5), channel_id=1, source_target_pairs={{0,16},{4,0},{8,24},{12,8},{16,20},{20,4},{24,28},{28,12},{1,17},{... | collective-permute-start | bytes 786440 | tf_op jit(solution)/shard_map/ppermute | solution.py:195
  13.7 4.8 %collective-permute-done.1.second = bf16[128,1024]{1,0:T(8,128)(2,1)S(1)} collective-permute-done((bf16[128,1024]{1,0:T(8,128)(2,1)}, bf16[128,1024]{1,0:T(8,128)(2,1)S(1)}, u32[]{:S(2)}, u32[]{:S(2)}) %collective-permute-start.1) | collective-permute-done | bytes 262176 | tf_op jit(solution)/shard_map/ppermute | solution.py:195
  19.4 2.1 %fusion.8 = (bf16[512,384]{1,0:T(8,128)(2,1)}, bf16[512,384]{1,0:T(8,128)(2,1)}) fusion(bf16[1024,384]{1,0:T(8,128)(2,1)} %refs_0_.1), kind=kLoop, calls=%fused_computation.33 | loop fusion | bytes 1572864 | tf_op jit(solution)/shard_map/split | solution.py:215
  21.5 7.7 %collective-permute-start.2 = (bf16[512,384]{1,0:T(8,128)(2,1)}, bf16[512,384]{1,0:T(8,128)(2,1)S(1)}, u32[]{:S(2)}, u32[]{:S(2)}) collective-permute-start(bf16[512,384]{1,0:T(8,128)(2,1)} %get-tuple-element.16), channel_id=1, source_target_pairs={{0,32},{32,0},{1,33},{33,1},{2,34},{34,2},{3,35},{35,3},{4,36},{36... | collective-permute-start | bytes 1179656 | tf_op jit(solution)/shard_map/ppermute | solution.py:215
  29.3 1.9 %collective-permute-start.3 = (bf16[512,384]{1,0:T(8,128)(2,1)}, bf16[512,384]{1,0:T(8,128)(2,1)}, u32[]{:S(2)}, u32[]{:S(2)}) collective-permute-start(bf16[512,384]{1,0:T(8,128)(2,1)} %get-tuple-element.15), channel_id=1, source_target_pairs={{0,32},{32,0},{1,33},{33,1},{2,34},{34,2},{3,35},{35,3},{4,36},{36... | collective-permute-start | bytes 1179656 | tf_op jit(solution)/shard_map/ppermute | solution.py:215
  31.2 3.0 %collective-permute-start.4 = (bf16[1024,384]{1,0:T(8,128)(2,1)}, bf16[1024,384]{1,0:T(8,128)(2,1)S(1)}, u32[]{:S(2)}, u32[]{:S(2)}) collective-permute-start(bf16[1024,384]{1,0:T(8,128)(2,1)} %refs_0_.1), channel_id=1, source_target_pairs={{0,4},{4,0},{8,12},{12,8},{1,5},{5,1},{9,13},{13,9},{2,6},{6,2},{1... | collective-permute-start | bytes 2359304 | tf_op jit(solution)/shard_map/ppermute | solution.py:214
  37.0 2.2 %collective-permute-start.8 = (bf16[128,1024]{1,0:T(8,128)(2,1)}, bf16[128,1024]{1,0:T(8,128)(2,1)}, u32[]{:S(2)}, u32[]{:S(2)}) collective-permute-start(bf16[128,1024]{1,0:T(8,128)(2,1)} %bitcast.10), channel_id=1, source_target_pairs={{0,4},{4,0},{8,12},{12,8},{1,5},{5,1},{9,13},{13,9},{2,6},{6,2},{1... | collective-permute-start | bytes 786440 | tf_op jit(solution)/shard_map/ppermute | solution.py:209
  39.2 16.8 %collective-permute-done.2.refs_1_ = bf16[512,384]{1,0:T(8,128)(2,1)S(1)} collective-permute-done((bf16[512,384]{1,0:T(8,128)(2,1)}, bf16[512,384]{1,0:T(8,128)(2,1)S(1)}, u32[]{:S(2)}, u32[]{:S(2)}) %collective-permute-start.2) | collective-permute-done | bytes 393248 | tf_op jit(solution)/shard_map/ppermute | solution.py:215
  56.0 2.8 %collective-permute-start.5 = (bf16[512,384]{1,0:T(8,128)(2,1)S(1)}, bf16[512,384]{1,0:T(8,128)(2,1)}, u32[]{:S(2)}, u32[]{:S(2)}) collective-permute-start(bf16[512,384]{1,0:T(8,128)(2,1)S(1)} %collective-permute-done.2.refs_1_), channel_id=1, source_target_pairs={{0,4},{4,0},{8,12},{12,8},{1,5},{5,1},{9,13},{13,9},{2,6},{6,2},{1... | collective-permute-start | bytes 1179656 | tf_op jit(solution)/shard_map/ppermute | solution.py:216
  58.8 5.6 %collective-permute-done.3.refs_2_ = bf16[512,384]{1,0:T(8,128)(2,1)} collective-permute-done((bf16[512,384]{1,0:T(8,128)(2,1)}, bf16[512,384]{1,0:T(8,128)(2,1)}, u32[]{:S(2)}, u32[]{:S(2)}) %collective-permute-start.3) | collective-permute-done | bytes 393248 | tf_op jit(solution)/shard_map/ppermute | solution.py:215
  64.4 2.8 %collective-permute-start.6 = (bf16[512,384]{1,0:T(8,128)(2,1)}, bf16[512,384]{1,0:T(8,128)(2,1)}, u32[]{:S(2)}, u32[]{:S(2)}) collective-permute-start(bf16[512,384]{1,0:T(8,128)(2,1)} %collective-permute-done.3.refs_2_), channel_id=1, source_target_pairs={{0,4},{4,0},{8,12},{12,8},{1,5},{5,1},{9,13},{13,9},{2,6},{6,2},{1... | collective-permute-start | bytes 1179656 | tf_op jit(solution)/shard_map/ppermute | solution.py:216
  67.3 2.2 %gather_fusion.1 = bf16[8,16,384]{2,1,0:T(8,128)(2,1)} fusion(bf16[32,16,384]{2,1,0:T(8,128)(2,1)} %param.8, s32[1024]{0:T(1024)S(1)} %pad_clamp_fusion.1), kind=kCustom, calls=%fused_computation.1 | custom fusion | bytes 196640 | tf_op jit(solution)/shard_map/gather | solution.py:206
  69.5 1.9 %collective-permute-start.7 = (bf16[128,384]{1,0:T(8,128)(2,1)}, bf16[128,384]{1,0:T(8,128)(2,1)S(1)}, u32[]{:S(2)}, u32[]{:S(2)}) collective-permute-start(bf16[128,384]{1,0:T(8,128)(2,1)} %bitcast.7), channel_id=1, source_target_pairs={{0,32},{32,0},{1,33},{33,1},{2,34},{34,2},{3,35},{35,3},{4,36},{36... | collective-permute-start | bytes 294920 | tf_op jit(solution)/shard_map/ppermute | solution.py:211
  72.0 1.6 %gather_fusion = bf16[8,16,384]{2,1,0:T(8,128)(2,1)S(1)} fusion(bf16[32,16,384]{2,1,0:T(8,128)(2,1)} %param.8, s32[1024]{0:T(1024)S(1)} %pad_clamp_fusion.2), kind=kCustom, calls=%fused_computation | custom fusion | bytes 196640 | tf_op jit(solution)/shard_map/gather | solution.py:206
  73.6 2.7 %collective-permute-done.7.refs_7_ = bf16[128,384]{1,0:T(8,128)(2,1)S(1)} collective-permute-done((bf16[128,384]{1,0:T(8,128)(2,1)}, bf16[128,384]{1,0:T(8,128)(2,1)S(1)}, u32[]{:S(2)}, u32[]{:S(2)}) %collective-permute-start.7) | collective-permute-done | bytes 98336 | tf_op jit(solution)/shard_map/ppermute | solution.py:211
  76.8 2.1 %shard_map.56.table = bf16[2560,768]{1,0:T(8,128)(2,1)S(1)} custom-call(s32[2]{0:T(128)S(1)} %pad_add_fusion.slots, bf16[1024,384]{1,0:T(8,128)(2,1)S(1)} %copy-done.3, bf16[512,384]{1,0:T(8,128)(2,1)S(1)} %collective-permute-done.2.refs_1_, bf16[512,384]{1,0:T(8,128)(2,1)} %collective-permute-done.3.refs_2_, ...), custom_call_target="tpu_custom_call" | custom-call | tf_op jit(solution)/shard_map/pallas_call | solution.py:82
  79.0 1.9 %copy-done.1 = bf16[2560,768]{1,0:T(8,128)(2,1)} copy-done((bf16[2560,768]{1,0:T(8,128)(2,1)}, bf16[2560,768]{1,0:T(8,128)(2,1)S(1)}, u32[]{:S(2)}) %copy-start.1) | copy-done | bytes 3932184
  80.9 2.7 %all-gather.3.cloned.1.call-done = bf16[1024,2048]{1,0:T(8,128)(2,1)} async-done(((bf16[128,2048]{1,0:T(8,128)(2,1)}), bf16[1024,2048]{1,0:T(8,128)(2,1)}) %all-gather.3.cloned.1.call-update) | async-done | bytes 4194320 | tf_op jit(solution)/shard_map/all_gather | solution.py:198
  83.6 2.1 %copy-done.2 = bf16[2560,768]{1,0:T(8,128)(2,1)S(1)} copy-done((bf16[2560,768]{1,0:T(8,128)(2,1)S(1)}, bf16[2560,768]{1,0:T(8,128)(2,1)}, u32[]{:S(2)}) %copy-start.2) | copy-done | bytes 3932184
  85.7 6.7 %shard_map.57 = (bf16[4,256,384]{2,1,0:T(8,128)(2,1)S(1)}, bf16[4,256,384]{2,1,0:T(8,128)(2,1)S(1)}) custom-call(s32[1]{0:T(128)} %bitcast.order, bf16[8,128,2048]{2,1,0:T(8,128)(2,1)} %bitcast.41, bf16[2560,768]{1,0:T(8,128)(2,1)S(1)} %copy-done.2), custom_call_target="tpu_custom_call" | custom-call | flops 3221225472 | bytes 9699328 | tf_op jit(solution)/shard_map/pallas_call | solution.py:150
  92.4 2.6 %collective-permute-start.9 = (bf16[4,256,384]{2,1,0:T(8,128)(2,1)S(1)}, bf16[4,256,384]{2,1,0:T(8,128)(2,1)S(1)}, u32[]{:S(2)}, u32[]{:S(2)}) collective-permute-start(bf16[4,256,384]{2,1,0:T(8,128)(2,1)S(1)} %get-tuple-element.8), channel_id=1, source_target_pairs={{0,1},{1,0},{2,3},{3,2},{4,5},{5,4},{6,7},{7,6},{8,9},{9,8},{10,11... | collective-permute-start | bytes 2359304 | tf_op jit(solution)/shard_map/ppermute | solution.py:223
  95.0 1.9 %collective-permute-done.9 = bf16[4,256,384]{2,1,0:T(8,128)(2,1)S(1)} collective-permute-done((bf16[4,256,384]{2,1,0:T(8,128)(2,1)S(1)}, bf16[4,256,384]{2,1,0:T(8,128)(2,1)S(1)}, u32[]{:S(2)}, u32[]{:S(2)}) %collective-permute-start.9) | collective-permute-done | bytes 786464 | tf_op jit(solution)/shard_map/ppermute | solution.py:223
  97.1 4.6 %collective-permute-start.10 = (bf16[256,384]{1,0:T(8,128)(2,1)S(1)}, bf16[256,384]{1,0:T(8,128)(2,1)S(1)}, u32[]{:S(2)}, u32[]{:S(2)}) collective-permute-start(bf16[256,384]{1,0:T(8,128)(2,1)S(1)} %get-tuple-element.12), channel_id=1, source_target_pairs={{0,8},{4,12},{8,0},{12,4},{1,9},{5,13},{9,1},{13,5},{2,10},{6,14},... | collective-permute-start | bytes 589832 | tf_op jit(solution)/shard_map/ppermute | solution.py:230
  101.7 2.8 %collective-permute-start.12 = (bf16[256,384]{1,0:T(8,128)(2,1)S(1)}, bf16[256,384]{1,0:T(8,128)(2,1)S(1)}, u32[]{:S(2)}, u32[]{:S(2)}) collective-permute-start(bf16[256,384]{1,0:T(8,128)(2,1)S(1)} %get-tuple-element.14), channel_id=1, source_target_pairs={{0,12},{4,0},{8,4},{12,8},{1,13},{5,1},{9,5},{13,9},{2,14},{6,2},{... | collective-permute-start | bytes 589832 | tf_op jit(solution)/shard_map/ppermute | solution.py:230
  104.5 2.5 %collective-permute-start.13 = (bf16[256,384]{1,0:T(8,128)(2,1)S(1)}, bf16[256,384]{1,0:T(8,128)(2,1)S(1)}, u32[]{:S(2)}, u32[]{:S(2)}) collective-permute-start(bf16[256,384]{1,0:T(8,128)(2,1)S(1)} %get-tuple-element.13), channel_id=1, source_target_pairs={{0,4},{4,8},{8,12},{12,0},{1,5},{5,9},{9,13},{13,1},{2,6},{6,10},{... | collective-permute-start | bytes 589832 | tf_op jit(solution)/shard_map/ppermute | solution.py:230
  107.1 7.4 %collective-permute-start.11 = (bf16[128,384]{1,0:T(8,128)(2,1)S(1)}, bf16[128,384]{1,0:T(8,128)(2,1)S(1)}, u32[]{:S(2)}, u32[]{:S(2)}) collective-permute-start(bf16[128,384]{1,0:T(8,128)(2,1)S(1)} %get-tuple-element.18), channel_id=1, source_target_pairs={{0,2},{1,34},{2,0},{3,32},{32,3},{33,35},{34,1},{35,33},{4,6},{5,3... | collective-permute-start | bytes 294920 | tf_op jit(solution)/shard_map/ppermute | solution.py:243
  114.5 2.8 %collective-permute-start.15 = (bf16[128,384]{1,0:T(8,128)(2,1)S(1)}, bf16[128,384]{1,0:T(8,128)(2,1)S(1)}, u32[]{:S(2)}, u32[]{:S(2)}) collective-permute-start(bf16[128,384]{1,0:T(8,128)(2,1)S(1)} %get-tuple-element.17), channel_id=1, source_target_pairs={{0,0},{1,32},{2,2},{3,34},{32,1},{33,33},{34,3},{35,35},{4,4},{5,3... | collective-permute-start | bytes 294920 | tf_op jit(solution)/shard_map/ppermute | solution.py:243
  117.4 3.7 %collective-permute-start.14 = (bf16[128,384]{1,0:T(8,128)(2,1)S(1)}, bf16[128,384]{1,0:T(8,128)(2,1)S(1)}, u32[]{:S(2)}, u32[]{:S(2)}) collective-permute-start(bf16[128,384]{1,0:T(8,128)(2,1)S(1)} %get-tuple-element.20), channel_id=1, source_target_pairs={{0,2},{1,34},{2,0},{3,32},{32,3},{33,35},{34,1},{35,33},{4,6},{5,3... | collective-permute-start | bytes 294920 | tf_op jit(solution)/shard_map/ppermute | solution.py:243
  121.2 2.2 %collective-permute-start.16 = (bf16[128,384]{1,0:T(8,128)(2,1)S(1)}, bf16[128,384]{1,0:T(8,128)(2,1)S(1)}, u32[]{:S(2)}, u32[]{:S(2)}) collective-permute-start(bf16[128,384]{1,0:T(8,128)(2,1)S(1)} %get-tuple-element.19), channel_id=1, source_target_pairs={{0,0},{1,32},{2,2},{3,34},{32,1},{33,33},{34,3},{35,35},{4,4},{5,3... | collective-permute-start | bytes 294920 | tf_op jit(solution)/shard_map/ppermute | solution.py:243
  124.0 1.9 %collective-permute-done.14 = bf16[128,384]{1,0:T(8,128)(2,1)S(1)} collective-permute-done((bf16[128,384]{1,0:T(8,128)(2,1)S(1)}, bf16[128,384]{1,0:T(8,128)(2,1)S(1)}, u32[]{:S(2)}, u32[]{:S(2)}) %collective-permute-start.14) | collective-permute-done | bytes 98336 | tf_op jit(solution)/shard_map/ppermute | solution.py:243
  125.9 3.2 %collective-permute-done.16 = bf16[128,384]{1,0:T(8,128)(2,1)S(1)} collective-permute-done((bf16[128,384]{1,0:T(8,128)(2,1)S(1)}, bf16[128,384]{1,0:T(8,128)(2,1)S(1)}, u32[]{:S(2)}, u32[]{:S(2)}) %collective-permute-start.16) | collective-permute-done | bytes 98336 | tf_op jit(solution)/shard_map/ppermute | solution.py:243
  (36 shorter events, 6.4 us)
Async XLA Ops:
  6.5 29.2 %copy-start = (bf16[32,16,1024]{2,1,0:T(8,128)(2,1)S(1)}, bf16[32,16,1024]{2,1,0:T(8,128)(2,1)}, u32[]{:S(2)}) copy-start(bf16[32,16,1024]{2,1,0:T(8,128)(2,1)} %param.7) | copy-start | bytes 3145732
  6.5 70.3 %copy-start.3 = (bf16[1024,384]{1,0:T(8,128)(2,1)S(1)}, bf16[1024,384]{1,0:T(8,128)(2,1)}, u32[]{:S(2)}) copy-start(bf16[1024,384]{1,0:T(8,128)(2,1)} %refs_0_.1) | copy-start | bytes 2359300
  6.5 77.0 %all-gather.3.cloned.1.call-start = ((), (), s32[]{:S(2)}) async-start(), calls=%async_computation | async-start | bytes 4718592 | tf_op jit(solution)/shard_map/all_gather | solution.py:198
  6.5 7.2 %collective-permute-start = (bf16[128,1024]{1,0:T(8,128)(2,1)}, bf16[128,1024]{1,0:T(8,128)(2,1)S(1)}, u32[]{:S(2)}, u32[]{:S(2)}) collective-permute-start(bf16[128,1024]{1,0:T(8,128)(2,1)} %param.5), channel_id=1, source_target_pairs={{0,0},{4,16},{8,8},{12,24},{16,4},{20,20},{24,12},{28,28},{1,1},{5... | collective-permute-start | bytes 786440 | tf_op jit(solution)/shard_map/ppermute | solution.py:192
  8.3 10.3 %collective-permute-start.1 = (bf16[128,1024]{1,0:T(8,128)(2,1)}, bf16[128,1024]{1,0:T(8,128)(2,1)S(1)}, u32[]{:S(2)}, u32[]{:S(2)}) collective-permute-start(bf16[128,1024]{1,0:T(8,128)(2,1)} %param.5), channel_id=1, source_target_pairs={{0,16},{4,0},{8,24},{12,8},{16,20},{20,4},{24,28},{28,12},{1,17},{... | collective-permute-start | bytes 786440 | tf_op jit(solution)/shard_map/ppermute | solution.py:195
  21.5 34.5 %collective-permute-start.2 = (bf16[512,384]{1,0:T(8,128)(2,1)}, bf16[512,384]{1,0:T(8,128)(2,1)S(1)}, u32[]{:S(2)}, u32[]{:S(2)}) collective-permute-start(bf16[512,384]{1,0:T(8,128)(2,1)} %get-tuple-element.16), channel_id=1, source_target_pairs={{0,32},{32,0},{1,33},{33,1},{2,34},{34,2},{3,35},{35,3},{4,36},{36... | collective-permute-start | bytes 1179656 | tf_op jit(solution)/shard_map/ppermute | solution.py:215
  29.3 35.1 %collective-permute-start.3 = (bf16[512,384]{1,0:T(8,128)(2,1)}, bf16[512,384]{1,0:T(8,128)(2,1)}, u32[]{:S(2)}, u32[]{:S(2)}) collective-permute-start(bf16[512,384]{1,0:T(8,128)(2,1)} %get-tuple-element.15), channel_id=1, source_target_pairs={{0,32},{32,0},{1,33},{33,1},{2,34},{34,2},{3,35},{35,3},{4,36},{36... | collective-permute-start | bytes 1179656 | tf_op jit(solution)/shard_map/ppermute | solution.py:215
  31.2 45.6 %collective-permute-start.4 = (bf16[1024,384]{1,0:T(8,128)(2,1)}, bf16[1024,384]{1,0:T(8,128)(2,1)S(1)}, u32[]{:S(2)}, u32[]{:S(2)}) collective-permute-start(bf16[1024,384]{1,0:T(8,128)(2,1)} %refs_0_.1), channel_id=1, source_target_pairs={{0,4},{4,0},{8,12},{12,8},{1,5},{5,1},{9,13},{13,9},{2,6},{6,2},{1... | collective-permute-start | bytes 2359304 | tf_op jit(solution)/shard_map/ppermute | solution.py:214
  37.0 39.4 %collective-permute-start.8 = (bf16[128,1024]{1,0:T(8,128)(2,1)}, bf16[128,1024]{1,0:T(8,128)(2,1)}, u32[]{:S(2)}, u32[]{:S(2)}) collective-permute-start(bf16[128,1024]{1,0:T(8,128)(2,1)} %bitcast.10), channel_id=1, source_target_pairs={{0,4},{4,0},{8,12},{12,8},{1,5},{5,1},{9,13},{13,9},{2,6},{6,2},{1... | collective-permute-start | bytes 786440 | tf_op jit(solution)/shard_map/ppermute | solution.py:209
  56.0 20.3 %collective-permute-start.5 = (bf16[512,384]{1,0:T(8,128)(2,1)S(1)}, bf16[512,384]{1,0:T(8,128)(2,1)}, u32[]{:S(2)}, u32[]{:S(2)}) collective-permute-start(bf16[512,384]{1,0:T(8,128)(2,1)S(1)} %collective-permute-done.2.refs_1_), channel_id=1, source_target_pairs={{0,4},{4,0},{8,12},{12,8},{1,5},{5,1},{9,13},{13,9},{2,6},{6,2},{1... | collective-permute-start | bytes 1179656 | tf_op jit(solution)/shard_map/ppermute | solution.py:216
  64.4 12.4 %collective-permute-start.6 = (bf16[512,384]{1,0:T(8,128)(2,1)}, bf16[512,384]{1,0:T(8,128)(2,1)}, u32[]{:S(2)}, u32[]{:S(2)}) collective-permute-start(bf16[512,384]{1,0:T(8,128)(2,1)} %collective-permute-done.3.refs_2_), channel_id=1, source_target_pairs={{0,4},{4,0},{8,12},{12,8},{1,5},{5,1},{9,13},{13,9},{2,6},{6,2},{1... | collective-permute-start | bytes 1179656 | tf_op jit(solution)/shard_map/ppermute | solution.py:216
  69.5 6.9 %collective-permute-start.7 = (bf16[128,384]{1,0:T(8,128)(2,1)}, bf16[128,384]{1,0:T(8,128)(2,1)S(1)}, u32[]{:S(2)}, u32[]{:S(2)}) collective-permute-start(bf16[128,384]{1,0:T(8,128)(2,1)} %bitcast.7), channel_id=1, source_target_pairs={{0,32},{32,0},{1,33},{33,1},{2,34},{34,2},{3,35},{35,3},{4,36},{36... | collective-permute-start | bytes 294920 | tf_op jit(solution)/shard_map/ppermute | solution.py:211
  79.0 1.9 %copy-start.1 = (bf16[2560,768]{1,0:T(8,128)(2,1)}, bf16[2560,768]{1,0:T(8,128)(2,1)S(1)}, u32[]{:S(2)}) copy-start(bf16[2560,768]{1,0:T(8,128)(2,1)S(1)} %shard_map.56.table) | copy-start | bytes 11796484
  83.6 2.1 %copy-start.2 = (bf16[2560,768]{1,0:T(8,128)(2,1)S(1)}, bf16[2560,768]{1,0:T(8,128)(2,1)}, u32[]{:S(2)}) copy-start(bf16[2560,768]{1,0:T(8,128)(2,1)} %copy-done.1) | copy-start | bytes 11796484
  92.4 4.5 %collective-permute-start.9 = (bf16[4,256,384]{2,1,0:T(8,128)(2,1)S(1)}, bf16[4,256,384]{2,1,0:T(8,128)(2,1)S(1)}, u32[]{:S(2)}, u32[]{:S(2)}) collective-permute-start(bf16[4,256,384]{2,1,0:T(8,128)(2,1)S(1)} %get-tuple-element.8), channel_id=1, source_target_pairs={{0,1},{1,0},{2,3},{3,2},{4,5},{5,4},{6,7},{7,6},{8,9},{9,8},{10,11... | collective-permute-start | bytes 2359304 | tf_op jit(solution)/shard_map/ppermute | solution.py:223
  97.1 9.9 %collective-permute-start.10 = (bf16[256,384]{1,0:T(8,128)(2,1)S(1)}, bf16[256,384]{1,0:T(8,128)(2,1)S(1)}, u32[]{:S(2)}, u32[]{:S(2)}) collective-permute-start(bf16[256,384]{1,0:T(8,128)(2,1)S(1)} %get-tuple-element.12), channel_id=1, source_target_pairs={{0,8},{4,12},{8,0},{12,4},{1,9},{5,13},{9,1},{13,5},{2,10},{6,14},... | collective-permute-start | bytes 589832 | tf_op jit(solution)/shard_map/ppermute | solution.py:230
  101.7 15.6 %collective-permute-start.12 = (bf16[256,384]{1,0:T(8,128)(2,1)S(1)}, bf16[256,384]{1,0:T(8,128)(2,1)S(1)}, u32[]{:S(2)}, u32[]{:S(2)}) collective-permute-start(bf16[256,384]{1,0:T(8,128)(2,1)S(1)} %get-tuple-element.14), channel_id=1, source_target_pairs={{0,12},{4,0},{8,4},{12,8},{1,13},{5,1},{9,5},{13,9},{2,14},{6,2},{... | collective-permute-start | bytes 589832 | tf_op jit(solution)/shard_map/ppermute | solution.py:230
  104.5 12.9 %collective-permute-start.13 = (bf16[256,384]{1,0:T(8,128)(2,1)S(1)}, bf16[256,384]{1,0:T(8,128)(2,1)S(1)}, u32[]{:S(2)}, u32[]{:S(2)}) collective-permute-start(bf16[256,384]{1,0:T(8,128)(2,1)S(1)} %get-tuple-element.13), channel_id=1, source_target_pairs={{0,4},{4,8},{8,12},{12,0},{1,5},{5,9},{9,13},{13,1},{2,6},{6,10},{... | collective-permute-start | bytes 589832 | tf_op jit(solution)/shard_map/ppermute | solution.py:230
  107.1 16.3 %collective-permute-start.11 = (bf16[128,384]{1,0:T(8,128)(2,1)S(1)}, bf16[128,384]{1,0:T(8,128)(2,1)S(1)}, u32[]{:S(2)}, u32[]{:S(2)}) collective-permute-start(bf16[128,384]{1,0:T(8,128)(2,1)S(1)} %get-tuple-element.18), channel_id=1, source_target_pairs={{0,2},{1,34},{2,0},{3,32},{32,3},{33,35},{34,1},{35,33},{4,6},{5,3... | collective-permute-start | bytes 294920 | tf_op jit(solution)/shard_map/ppermute | solution.py:243
  114.5 9.5 %collective-permute-start.15 = (bf16[128,384]{1,0:T(8,128)(2,1)S(1)}, bf16[128,384]{1,0:T(8,128)(2,1)S(1)}, u32[]{:S(2)}, u32[]{:S(2)}) collective-permute-start(bf16[128,384]{1,0:T(8,128)(2,1)S(1)} %get-tuple-element.17), channel_id=1, source_target_pairs={{0,0},{1,32},{2,2},{3,34},{32,1},{33,33},{34,3},{35,35},{4,4},{5,3... | collective-permute-start | bytes 294920 | tf_op jit(solution)/shard_map/ppermute | solution.py:243
  117.4 8.4 %collective-permute-start.14 = (bf16[128,384]{1,0:T(8,128)(2,1)S(1)}, bf16[128,384]{1,0:T(8,128)(2,1)S(1)}, u32[]{:S(2)}, u32[]{:S(2)}) collective-permute-start(bf16[128,384]{1,0:T(8,128)(2,1)S(1)} %get-tuple-element.20), channel_id=1, source_target_pairs={{0,2},{1,34},{2,0},{3,32},{32,3},{33,35},{34,1},{35,33},{4,6},{5,3... | collective-permute-start | bytes 294920 | tf_op jit(solution)/shard_map/ppermute | solution.py:243
  121.2 7.9 %collective-permute-start.16 = (bf16[128,384]{1,0:T(8,128)(2,1)S(1)}, bf16[128,384]{1,0:T(8,128)(2,1)S(1)}, u32[]{:S(2)}, u32[]{:S(2)}) collective-permute-start(bf16[128,384]{1,0:T(8,128)(2,1)S(1)} %get-tuple-element.19), channel_id=1, source_target_pairs={{0,0},{1,32},{2,2},{3,34},{32,1},{33,33},{34,3},{35,35},{4,4},{5,3... | collective-permute-start | bytes 294920 | tf_op jit(solution)/shard_map/ppermute | solution.py:243
Sparse Core Ops, SparseCore 0:
  19.6 63.9 all-gather.2
